TPU v7x, 256 devices: a whole 4x4x8 slice. The times are simulated.
256 devices in a mesh: dp: 8 (over y, core), ctx: 32 (over z, x).
Axes of the slice: x: 4, y: 4, z: 8, core: 2. Of those that a mesh axis runs over, the one named last changes fastest.
Arguments:
- doc_lengths: int32 [8, 8], P('dp'), may hold values from 1 to 2048, 4096 in all within a row
- values: bfloat16 [8, 4096, 4096], P('dp', 'ctx'), may hold values from -6 to 6
- gate_short: bfloat16 [8, 4096, 4096], P('dp', 'ctx'), may hold values from -6 to 6
- gate_long: bfloat16 [8, 4096, 4096], P('dp', 'ctx'), may hold values from -6 to 6
- short_taps: float32 [7, 4096], replicated, may hold values from -2 to 2
- long_taps: float32 [128, 4096], replicated
- cotangent: bfloat16 [8, 4096, 4096], P('dp', 'ctx'), may hold values from -6 to 6
Outputs:
- output: bfloat16 [8, 4096, 4096], P('dp', 'ctx')
- grad_gate_short: bfloat16 [8, 4096, 4096], P('dp', 'ctx')
- grad_values: bfloat16 [8, 4096, 4096], P('dp', 'ctx')
- grad_gate_long: bfloat16 [8, 4096, 4096], P('dp', 'ctx')
- grad_short_taps: float32 [7, 4096], replicated
- grad_long_taps: float32 [128, 4096], replicated
Inputs may be any that keep to these rules, and one draw needn't show every extreme that they name: `doc_lengths`: each row holds the lengths of the 8 documents of one context in order; they sum to 4096, and the longest is exactly 2048.
All inputs are finite; a program needn't handle non-finite values.
Results may differ from a plain program's by a relative error of at most 0.0065.
Values may be sent and summed in bfloat16 or wider, within the bound.
No kernel may reach another device: no remote copies, remote signals or barrier semaphores. Data moves between devices by JAX's collectives and lax.ppermute only.
A program may use at most 256 MiB of HBM per device.

v0:
```python
import math

import jax
import jax.numpy as jnp
from jax import lax
from jax.sharding import PartitionSpec as P


def passed_along(block, axis, distance):
    devices = range(lax.axis_size(axis))
    route = [(i - distance, i) for i in devices if i - distance in devices]
    return lax.ppermute(block, axis, route)


def reach_of(lengths, positions):
    starts = jnp.cumsum(lengths) - lengths
    before = jnp.where(starts[None, :] <= positions[:, None], starts[None, :], 0)
    return positions - jnp.max(before, axis=1)


def causal(padded, filter_taps, reach):
    tap_count = filter_taps.shape[0]
    out_rows = padded.shape[0] - (tap_count - 1)
    summed = jnp.zeros((out_rows, padded.shape[1]), jnp.float32)
    for offset in range(tap_count):
        window = padded[tap_count - 1 - offset : tap_count - 1 - offset + out_rows].astype(
            jnp.float32
        )
        summed = summed + filter_taps[offset][None, :] * jnp.where(
            (reach >= offset)[:, None], window, 0.0
        )
    return summed


def adjoint(padded, filter_taps, reach_after):
    tap_count = filter_taps.shape[0]
    out_rows = padded.shape[0] - (tap_count - 1)
    summed = jnp.zeros((out_rows, padded.shape[1]), jnp.float32)
    for offset in range(tap_count):
        window = padded[offset : offset + out_rows].astype(jnp.float32)
        masked = reach_after[offset : offset + out_rows] >= offset
        summed = summed + filter_taps[offset][None, :] * jnp.where(masked[:, None], window, 0.0)
    return summed


def tap_grads(adjoint_rows, padded, reach):
    out_rows = adjoint_rows.shape[0]
    tap_count = padded.shape[0] - out_rows + 1
    weights = adjoint_rows.astype(jnp.float32)
    tap_rows = []
    for offset in range(tap_count):
        window = padded[tap_count - 1 - offset : tap_count - 1 - offset + out_rows].astype(
            jnp.float32
        )
        tap_rows.append(
            jnp.sum(jnp.where((reach >= offset)[:, None], weights * window, 0.0), axis=0)
        )
    return jnp.stack(tap_rows)


def on_device(doc_lengths, values, gate_short, gate_long, short_taps, long_taps, cotangent):
    signal = values[0]
    gate_one = gate_short[0]
    gate_two = gate_long[0]
    upstream = cotangent[0]
    rows_here = signal.shape[0]
    short_rim = short_taps.shape[0] - 1
    long_rim = long_taps.shape[0] - 1
    first_row = lax.axis_index("ctx") * rows_here
    reach_span = reach_of(
        doc_lengths[0], first_row - long_rim + jnp.arange(2 * long_rim + rows_here, dtype=jnp.int32)
    )
    reach_own = reach_span[long_rim : long_rim + rows_here]
    reach_after = reach_span[long_rim:]
    before = passed_along(signal[rows_here - short_rim :], "ctx", 1)
    signal_ext = jnp.concatenate([before, signal], axis=0)
    short_mix = causal(signal_ext, short_taps, reach_own)
    mixed_short = (gate_one.astype(jnp.float32) * short_mix).astype(jnp.bfloat16)
    mixed_prev = passed_along(mixed_short[rows_here - long_rim :], "ctx", 1)
    mixed_ext = jnp.concatenate([mixed_prev, mixed_short], axis=0)
    long_mix = causal(mixed_ext, long_taps, reach_own)
    output = (gate_two.astype(jnp.float32) * long_mix).astype(jnp.bfloat16)
    grad_gate_long = (upstream.astype(jnp.float32) * long_mix).astype(jnp.bfloat16)
    adj_long = (upstream.astype(jnp.float32) * gate_two.astype(jnp.float32)).astype(jnp.bfloat16)
    long_next = passed_along(adj_long[:long_rim], "ctx", -1)
    back_long = adjoint(jnp.concatenate([adj_long, long_next], axis=0), long_taps, reach_after)
    long_terms = tap_grads(adj_long, mixed_ext, reach_own)
    grad_gate_short = (back_long * short_mix).astype(jnp.bfloat16)
    adj_short = (back_long * gate_one.astype(jnp.float32)).astype(jnp.bfloat16)
    short_next = passed_along(adj_short[:short_rim], "ctx", -1)
    grad_values = adjoint(
        jnp.concatenate([adj_short, short_next], axis=0),
        short_taps,
        reach_after[: rows_here + short_rim],
    ).astype(jnp.bfloat16)
    short_terms = tap_grads(adj_short, signal_ext, reach_own)
    summed_short, summed_long = lax.psum((short_terms, long_terms), ("dp", "ctx"))
    factor = 1.0 / math.sqrt(lax.axis_size("dp") * lax.axis_size("ctx") * rows_here)
    return (
        output[None],
        grad_gate_short[None],
        grad_values[None],
        grad_gate_long[None],
        summed_short * factor,
        summed_long * factor,
    )


def solution(mesh):
    in_specs = (
        P("dp", None),
        P("dp", "ctx", None),
        P("dp", "ctx", None),
        P("dp", "ctx", None),
        P(),
        P(),
        P("dp", "ctx", None),
    )
    out_specs = (
        P("dp", "ctx", None),
        P("dp", "ctx", None),
        P("dp", "ctx", None),
        P("dp", "ctx", None),
        P(),
        P(),
    )
    return jax.shard_map(
        on_device, mesh=mesh, in_specs=in_specs, out_specs=out_specs, check_vma=False
    )
```

profile of v0, /device:TPU:1, one launch (start us, length us, event | category | flops | bytes accessed | tf_op | source)
XLA Modules:
  0.0 1239.9 jit_solution(4195563972246502237)
XLA Ops:
  54.3 17.5 %collective-permute-done.1 = bf16[127,4096]{1,0:T(8,128)(2,1)S(1)} collective-permute-done((bf16[127,4096]{1,0:T(8,128)(2,1)S(1)}, bf16[127,4096]{1,0:T(8,128)(2,1)S(1)}, u32[]{:S(2)}, u32[]{:S(2)}) %collective-permute-start.1) | collective-permute-done | bytes 1040416 | tf_op jit(solution)/shard_map/ppermute | solution.py:12
  71.8 42.1 %fusion.86 = f32[128,4096]{1,0:T(8,128)} fusion(bf16[128,4096]{1,0:T(8,128)(2,1)S(1)} %get-tuple-element.149, f32[4096]{0:T(1024)} %bitcast.475, f32[4096]{0:T(1024)} %bitcast.477, f32[4096]{0:T(1024)} %bitcast.479, f32[4096]{0:T(1024)} %bitcast.481, f32[4096]{0:T(1024)} %bitcast.483, f32[4096]{0:T(1024)} %bitcast.509, f32[4096]{0:T(1024)} %bitcast.493, ...), kind=kLoop, calls=%fused_computation.877 | loop fusion | flops 177733632 | bytes 4995200 | tf_op jit(solution)/shard_map/add | solution.py:29
  113.9 509.2 %fusion.577 = (bf16[1,128,4096]{2,1,0:T(8,128)(2,1)}, f32[128,4096]{1,0:T(8,128)S(1)}) fusion(bf16[1,128,4096]{2,1,0:T(8,128)(2,1)S(1)} %copy-done.2, bf16[128,4096]{1,0:T(8,128)(2,1)S(1)} %get-tuple-element.149, bf16[127,4096]{1,0:T(8,128)(2,1)S(1)} %collective-permute-done.1, pred[128]{0:T(512)(128)(4,1)} %get-tuple-element.625, f32[4096]{0:T(1024)} %bitcast.433, ...), kind=kLoop, calls=%fused_computation.1372 | loop fusion | flops 291504128 | bytes 9684864 | tf_op jit(solution)/shard_map/broadcast_in_dim | solution.py:103
  626.9 8.2 fusion.549
  635.2 8.8 fusion.547
  644.1 8.1 fusion.545
  652.3 7.7 fusion.543
  660.0 9.0 fusion.541
  669.1 7.8 fusion.539
  677.1 8.1 fusion.537
  685.2 8.0 fusion.535
  693.3 6.9 fusion.573
  700.3 6.8 fusion.571
  707.1 6.5 fusion.569
  713.8 7.2 fusion.567
  721.1 6.6 fusion.565
  727.8 8.3 fusion.563
  736.2 7.2 fusion.561
  743.5 7.2 fusion.559
  750.8 9.1 fusion.557
  759.9 7.9 fusion.555
  767.8 8.0 fusion.553
  776.0 5.3 fusion.575
  781.3 8.9 fusion.551
  794.0 4.9 fusion.634
  803.7 5.1 fusion.636
  834.5 42.9 %multiply_add_fusion.1 = f32[128,4096]{1,0:T(8,128)S(1)} fusion(bf16[128,4096]{1,0:T(8,128)(2,1)S(1)} %get-tuple-element.143, bf16[127,4096]{1,0:T(8,128)(2,1)S(1)} %collective-permute-done.2, f32[4096]{0:T(1024)S(1)} %bitcast.494, f32[4096]{0:T(1024)S(1)} %bitcast.496, f32[4096]{0:T(1024)S(1)} %bitcast.498, f32[4096]{0:T(1024)S(1)} %bitcast.500, ...), kind=kLoop, calls=%fused_computation.1370 | loop fusion | flops 155713536 | bytes 4896128 | tf_op jit(solution)/shard_map/add | solution.py:42
  877.5 51.9 %fusion.576 = (bf16[1,128,4096]{2,1,0:T(8,128)(2,1)}, f32[128,4096]{1,0:T(8,128)S(1)}) fusion(f32[128,4096]{1,0:T(8,128)S(1)} %copy-done.1, bf16[128,4096]{1,0:T(8,128)(2,1)S(1)} %get-tuple-element.233, pred[128]{0:T(512)(128)(4,1)} %get-tuple-element.372, f32[4096]{0:T(1024)} %bitcast.434, bf16[128,4096]{1,0:T(8,128)(2,1)S(1)} %get-tuple-element.234, ...), kind=kLoop, calls=%fused_computation.1371 | loop fusion | flops 177733632 | bytes 98904576 | tf_op jit(solution)/shard_map/broadcast_in_dim | solution.py:101
  936.7 23.9 %stack.547 = f32[128,4096]{1,0:T(8,128)} concatenate(f32[1,4096]{1,0:T(1,128)S(1)} %bitcast.700, f32[1,4096]{1,0:T(1,128)} %bitcast.691, f32[1,4096]{1,0:T(1,128)} %bitcast.689, f32[1,4096]{1,0:T(1,128)} %bitcast.690, f32[1,4096]{1,0:T(1,128)} %bitcast.692, f32[1,4096]{1,0:T(1,128)} %bitcast.693, f32[1,4096]{1,0:T(1,128)} %bitcast.623, f32[1,4096]{1,0:T(1,128)} %bitcast.624, ...), dimensions={0} | concatenate | bytes 4194304 | tf_op jit(solution)/shard_map/stack | solution.py:58
  962.0 5.1 collective-permute-done.3
  967.1 5.6 fusion.841
  972.7 256.3 %all-reduce.3.cloned.1.call-done = (f32[7,4096]{1,0:T(8,128)}, f32[128,4096]{1,0:T(8,128)}) async-done(((f32[7,4096]{1,0:T(8,128)}, f32[128,4096]{1,0:T(8,128)}), (f32[7,4096]{1,0:T(8,128)}, f32[128,4096]{1,0:T(8,128)})) %all-reduce.3.cloned.1.call-update) | async-done | bytes 2211856 | tf_op jit(solution)/shard_map/psum | solution.py:97
  (506 shorter events, 96.9 us)
Async XLA Ops:
  7.2 35.2 %copy-start = (bf16[1,128,4096]{2,1,0:T(8,128)(2,1)S(1)}, bf16[1,128,4096]{2,1,0:T(8,128)(2,1)}, u32[]{:S(2)}) copy-start(bf16[1,128,4096]{2,1,0:T(8,128)(2,1)} %param.8) | copy-start | bytes 3145732
  7.2 34.4 %copy-start.45 = (f32[7,4096]{1,0:T(8,128)S(1)}, f32[7,4096]{1,0:T(8,128)}, u32[]{:S(2)}) copy-start(f32[7,4096]{1,0:T(8,128)} %param.11) | copy-start | bytes 344068
  7.2 35.2 %copy-start.3 = (bf16[1,128,4096]{2,1,0:T(8,128)(2,1)S(1)}, bf16[1,128,4096]{2,1,0:T(8,128)(2,1)}, u32[]{:S(2)}) copy-start(bf16[1,128,4096]{2,1,0:T(8,128)(2,1)} %param.9) | copy-start | bytes 3145732
  7.2 1221.9 %all-reduce.3.cloned.1.call-start = ((), (), s32[]{:S(2)}) async-start(), calls=%async_computation | async-start | bytes 4456448 | tf_op jit(solution)/shard_map/psum | solution.py:97
  8.2 34.1 %collective-permute-start = (bf16[6,4096]{1,0:T(8,128)(2,1)S(1)}, bf16[6,4096]{1,0:T(8,128)(2,1)S(1)}, u32[]{:S(2)}, u32[]{:S(2)}) collective-permute-start(bf16[6,4096]{1,0:T(8,128)(2,1)S(1)} %slice_bitcast_fusion), channel_id=1, source_target_pairs={{0,1},{1,2},{2,3},{3,4},{4,5},{5,6},{6,7},{7,8},{8,9},{9,10},{10,1... | collective-permute-start | bytes 147464 | tf_op jit(solution)/shard_map/ppermute | solution.py:12
  14.5 32.3 %copy-start.88 = (pred[128]{0:T(512)(128)(4,1)}, pred[128]{0:T(512)(128)(4,1)S(1)}, u32[]{:S(2)}) copy-start(pred[128]{0:T(512)(128)(4,1)S(1)} %get-tuple-element.501) | copy-start | bytes 388
  14.5 32.3 %copy-start.90 = (pred[128]{0:T(512)(128)(4,1)}, pred[128]{0:T(512)(128)(4,1)S(1)}, u32[]{:S(2)}) copy-start(pred[128]{0:T(512)(128)(4,1)S(1)} %get-tuple-element.502) | copy-start | bytes 388
  14.5 32.3 %copy-start.92 = (pred[128]{0:T(512)(128)(4,1)}, pred[128]{0:T(512)(128)(4,1)S(1)}, u32[]{:S(2)}) copy-start(pred[128]{0:T(512)(128)(4,1)S(1)} %get-tuple-element.503) | copy-start | bytes 388
  14.5 32.3 %copy-start.94 = (pred[128]{0:T(512)(128)(4,1)}, pred[128]{0:T(512)(128)(4,1)S(1)}, u32[]{:S(2)}) copy-start(pred[128]{0:T(512)(128)(4,1)S(1)} %get-tuple-element.504) | copy-start | bytes 388
  14.6 32.3 %copy-start.96 = (pred[128]{0:T(512)(128)(4,1)}, pred[128]{0:T(512)(128)(4,1)S(1)}, u32[]{:S(2)}) copy-start(pred[128]{0:T(512)(128)(4,1)S(1)} %get-tuple-element.505) | copy-start | bytes 388
  42.3 892.0 %copy-start.86 = (pred[128]{0:T(512)(128)(4,1)}, pred[128]{0:T(512)(128)(4,1)S(1)}, u32[]{:S(2)}) copy-start(pred[128]{0:T(512)(128)(4,1)S(1)} %get-tuple-element.498) | copy-start | bytes 388
  47.1 24.6 %collective-permute-start.1 = (bf16[127,4096]{1,0:T(8,128)(2,1)S(1)}, bf16[127,4096]{1,0:T(8,128)(2,1)S(1)}, u32[]{:S(2)}, u32[]{:S(2)}) collective-permute-start(bf16[127,4096]{1,0:T(8,128)(2,1)S(1)} %slice.2560), channel_id=1, source_target_pairs={{0,1},{1,2},{2,3},{3,4},{4,5},{5,6},{6,7},{7,8},{8,9},{9,10},{10,1... | collective-permute-start | bytes 3121160 | tf_op jit(solution)/shard_map/ppermute | solution.py:12
  71.8 42.2 %copy-start.2 = (bf16[1,128,4096]{2,1,0:T(8,128)(2,1)S(1)}, bf16[1,128,4096]{2,1,0:T(8,128)(2,1)}, u32[]{:S(2)}) copy-start(bf16[1,128,4096]{2,1,0:T(8,128)(2,1)} %param.13) | copy-start | bytes 3145732
  71.8 42.2 %copy-start.98 = (pred[128]{0:T(512)(128)(4,1)S(1)}, pred[128]{0:T(512)(128)(4,1)}, u32[]{:S(2)}) copy-start(pred[128]{0:T(512)(128)(4,1)} %get-tuple-element.604) | copy-start | bytes 388
  113.9 509.2 %copy-start.4 = (bf16[1,128,4096]{2,1,0:T(8,128)(2,1)S(1)}, bf16[1,128,4096]{2,1,0:T(8,128)(2,1)}, u32[]{:S(2)}) copy-start(bf16[1,128,4096]{2,1,0:T(8,128)(2,1)} %param.10) | copy-start | bytes 3145732
  625.6 9.6 copy-start.165
  625.6 9.6 copy-start.166
  625.6 9.6 copy-start.167
  625.6 9.6 copy-start.168
  625.6 9.6 copy-start.169
  625.6 9.6 copy-start.181
  625.6 164.6 %collective-permute-start.2 = (bf16[127,4096]{1,0:T(8,128)(2,1)S(1)}, bf16[127,4096]{1,0:T(8,128)(2,1)S(1)}, u32[]{:S(2)}, u32[]{:S(2)}) collective-permute-start(bf16[127,4096]{1,0:T(8,128)(2,1)S(1)} %bitcast.300), channel_id=1, source_target_pairs={{1,0},{2,1},{3,2},{4,3},{5,4},{6,5},{7,6},{8,7},{9,8},{10,9},{11,1... | collective-permute-start | bytes 3121160 | tf_op jit(solution)/shard_map/ppermute | solution.py:12
  750.7 9.1 copy-start.102
  834.4 43.0 %copy-start.1 = (f32[128,4096]{1,0:T(8,128)S(1)}, f32[128,4096]{1,0:T(8,128)}, u32[]{:S(2)}) copy-start(f32[128,4096]{1,0:T(8,128)} %get-tuple-element.150) | copy-start | bytes 6291460
  834.4 43.0 %copy-start.5 = (f32[1,4096]{1,0:T(1,128)S(1)}, f32[1,4096]{1,0:T(1,128)}, u32[]{:S(2)}) copy-start(f32[1,4096]{1,0:T(1,128)} %get-tuple-element.303) | copy-start | bytes 49156
  834.4 43.0 %copy-start.6 = (f32[1,4096]{1,0:T(1,128)S(1)}, f32[1,4096]{1,0:T(1,128)}, u32[]{:S(2)}) copy-start(f32[1,4096]{1,0:T(1,128)} %get-tuple-element.304) | copy-start | bytes 49156
  834.4 43.0 %copy-start.7 = (f32[1,4096]{1,0:T(1,128)S(1)}, f32[1,4096]{1,0:T(1,128)}, u32[]{:S(2)}) copy-start(f32[1,4096]{1,0:T(1,128)} %get-tuple-element.305) | copy-start | bytes 49156
  834.5 43.0 %copy-start.8 = (f32[1,4096]{1,0:T(1,128)S(1)}, f32[1,4096]{1,0:T(1,128)}, u32[]{:S(2)}) copy-start(f32[1,4096]{1,0:T(1,128)} %get-tuple-element.306) | copy-start | bytes 49156
  834.5 43.0 %copy-start.9 = (f32[1,4096]{1,0:T(1,128)S(1)}, f32[1,4096]{1,0:T(1,128)}, u32[]{:S(2)}) copy-start(f32[1,4096]{1,0:T(1,128)} %get-tuple-element.307) | copy-start | bytes 49156
  834.5 43.0 %copy-start.10 = (f32[1,4096]{1,0:T(1,128)S(1)}, f32[1,4096]{1,0:T(1,128)}, u32[]{:S(2)}) copy-start(f32[1,4096]{1,0:T(1,128)} %get-tuple-element.308) | copy-start | bytes 49156
  834.5 43.0 %copy-start.11 = (f32[1,4096]{1,0:T(1,128)S(1)}, f32[1,4096]{1,0:T(1,128)}, u32[]{:S(2)}) copy-start(f32[1,4096]{1,0:T(1,128)} %get-tuple-element.309) | copy-start | bytes 49156
  960.7 6.4 collective-permute-start.3
  (199 other events, 1031.4 us)
Sparse Core Ops, SparseCore 0:
  960.8 268.2 all-reduce.2
where the time goes:
time: 1250 us; the launch traced here: 1240 us
  other arithmetic  885 us (71%)
  waiting for transfers between devices  279 us (22%)
  local copies, waits for them, and re-layouts  49.4 us (4%)
  between operations  17 us (1%)
    broadcast_in_dim x1, other arithmetic, on_device(): grad_gate_long[None]  509 us
    psum x1, waiting for transfers between devices, on_device(): lax.psum((short_terms, long_terms), ('dp', 'ctx'))  256 us
    reduce_sum x24, other arithmetic, tap_grads(): jnp.sum(jnp.where((reach >= offset)[:, None], weights * window, 0.0), axi...  169 us
    broadcast_in_dim x1, other arithmetic, on_device(): grad_gate_short[None]  51.9 us
    add x1, other arithmetic, adjoint(): summed + filter_taps[offset][None, :] * jnp.where(masked[:, None], window...  42.9 us
    concatenate x10, other arithmetic, on_device(): jnp.concatenate([adj_long, long_next], axis=0)  42.9 us
    add x1, other arithmetic, causal(): summed + filter_taps[offset][None, :] * jnp.where((reach >= offset)[:, No...  42.1 us
  transfers between devices with their start and end apart: 5, of which 3 were waited for; matrix products, arithmetic and copies ran while one was open for 16% of the time, Pallas kernels for 0%

commit v1 on v0

v1 whole, which is shorter than its diff:
```python
import math

import jax
import jax.numpy as jnp
import numpy as np
from jax import lax
from jax.experimental import pallas as pl
from jax.experimental.pallas import tpu as pltpu
from jax.sharding import PartitionSpec as P

BF = jnp.bfloat16
F32 = jnp.float32
LANES = 128


def halves(matrix):
    high = matrix.astype(np.float32).astype(BF)
    low = (matrix - high.astype(np.float64)).astype(np.float32).astype(BF)
    return high, low


def spectra(rows):
    points = 2 * rows
    theta = np.pi * (2 * np.arange(rows) + 1) / points
    angles = theta[:, None] * np.arange(points)[None, :]
    forward = np.concatenate([np.cos(angles), -np.sin(angles)], axis=0)
    inverse = forward.T / rows

    def pack(matrix):
        return np.concatenate(halves(matrix), axis=1)

    first = pack(forward[:, :rows])
    second = pack(forward[:, rows:])
    to_later = pack(inverse[rows:])
    to_first = pack(inverse[:rows])
    to_taps = pack(inverse[rows - np.arange(rows)])
    return first, second, to_later, to_first, to_taps


def passed_along(block, distance):
    devices = range(lax.axis_size("ctx"))
    route = [(i - distance, i) for i in devices if i - distance in devices]
    return lax.ppermute(block, "ctx", route)


def wide(row_mask, columns):
    return jnp.concatenate([row_mask] * (columns // LANES), axis=1)


def mix_kernel(reach_ref, v_ref, before_ref, gs_ref, gl_ref, up_ref, taps_ref,
               mixed_ref, adj_ref, short_ref, ext):
    rows, columns = v_ref.shape
    count = taps_ref.shape[0]
    ext[0:8, :] = before_ref[...].astype(F32)
    ext[8:, :] = v_ref[...].astype(F32)
    reach = wide(reach_ref[...], columns)
    total = taps_ref[0:1, :] * ext[8:, :]
    for j in range(1, count):
        window = ext[8 - j : 8 - j + rows, :]
        total = total + taps_ref[j : j + 1, :] * jnp.where(reach >= j, window, 0.0)
    short_ref[...] = total
    mixed_ref[...] = (gs_ref[...].astype(F32) * total).astype(BF)
    adj_ref[...] = (up_ref[...].astype(F32) * gl_ref[...].astype(F32)).astype(BF)


def times(left, right, conjugate_left):
    half = left.shape[0] // 2
    a, b = left[:half], left[half:]
    c, d = right[:half], right[half:]
    if conjugate_left:
        return jnp.concatenate([a * c + b * d, a * d - b * c], axis=0)
    return jnp.concatenate([a * c - b * d, a * d + b * c], axis=0)


def dot(matrix, data):
    return jnp.dot(matrix, data, preferred_element_type=F32)


def doubled(data):
    return jnp.concatenate([data, data], axis=0)


def main_kernel(meta_ref, reach_ref, left_ref, v_ref, before_ref, gs_ref, gl_ref, up_ref,
                mixed_ref, adj_ref, short_ref, prev_ref, next_ref, staps_ref, ltaps_ref,
                first_ref, second_ref, later_ref, front_ref, totaps_ref,
                out_ref, ggs_ref, gv_ref, ggl_ref, grads_ref, head_ref, tail_ref,
                long_acc, back_acc, spec_acc, taps_spec, ext, adj_ext):
    rows, columns = v_ref.shape
    count = staps_ref.shape[0]
    taps_spec[...] = dot(first_ref[...], doubled(ltaps_ref[...].astype(BF)))
    long_acc[...] = jnp.zeros_like(long_acc)
    back_acc[...] = jnp.zeros_like(back_acc)
    spec_acc[...] = jnp.zeros_like(spec_acc)
    at = lax.broadcasted_iota(jnp.int32, (rows, LANES), 0)

    def document(d, carry):
        begin = meta_ref[2 + d]
        end = meta_ref[3 + d]

        def inside(positions):
            return jnp.where((positions >= begin) & (positions < end), 1.0, 0.0)

        own = wide(inside(at), columns)
        own_bf = own.astype(BF)
        prev = prev_ref[...] * wide(inside(at - rows), columns).astype(BF)
        following = next_ref[...] * wide(inside(at + rows), columns).astype(BF)
        mixed = mixed_ref[...] * own_bf
        adj = adj_ref[...] * own_bf
        x_spec = dot(first_ref[...], doubled(prev)) + dot(second_ref[...], doubled(mixed))
        product = times(taps_spec[...], x_spec, False).astype(BF)
        long_acc[...] += own * dot(later_ref[...], doubled(product))
        a_spec = dot(first_ref[...], doubled(adj))
        spec_acc[...] += times(a_spec, x_spec, True)
        a_spec = a_spec + dot(second_ref[...], doubled(following))
        product = times(taps_spec[...], a_spec, True).astype(BF)
        back_acc[...] += own * dot(front_ref[...], doubled(product))
        return carry

    lax.fori_loop(meta_ref[0], meta_ref[1] + 1, document, 0)
    grads_ref[0:rows, :] = dot(totaps_ref[...], doubled(spec_acc[...].astype(BF))).astype(BF)

    long_mix = long_acc[...]
    out_ref[...] = (gl_ref[...].astype(F32) * long_mix).astype(BF)
    ggl_ref[...] = (up_ref[...].astype(F32) * long_mix).astype(BF)
    back = back_acc[...]
    ggs_ref[...] = (back * short_ref[...]).astype(BF)
    adj_short = (back * gs_ref[...].astype(F32)).astype(BF).astype(F32)
    head_ref[...] = adj_short[0:8].astype(BF)
    adj_ext[0:rows, :] = adj_short
    adj_ext[rows:, :] = jnp.zeros((8, columns), F32)
    ext[0:8, :] = before_ref[...].astype(F32)
    ext[8:, :] = v_ref[...].astype(F32)
    reach = wide(reach_ref[...], columns)
    left = wide(left_ref[...], columns)
    total = staps_ref[0:1, :] * adj_short
    terms = [jnp.sum(adj_short * ext[8:, :], axis=0, keepdims=True)]
    for j in range(1, count):
        total = total + staps_ref[j : j + 1, :] * jnp.where(
            left > j, adj_ext[j : j + rows, :], 0.0)
        window = ext[8 - j : 8 - j + rows, :]
        terms.append(jnp.sum(jnp.where(reach >= j, adj_short * window, 0.0), axis=0, keepdims=True))
    gv_ref[...] = total.astype(BF)
    tail_ref[...] = total[rows - 16 :]
    terms.append(jnp.zeros((8 - count, columns), F32))
    stacked = jnp.concatenate(terms, axis=0)
    grads_ref[rows:, :] = jnp.concatenate([stacked, jnp.zeros_like(stacked)], axis=0).astype(BF)


def on_device(doc_lengths, values, gate_short, gate_long, short_taps, long_taps, cotangent):
    v, gs, gl, up = values[0], gate_short[0], gate_long[0], cotangent[0]
    rows, channels = v.shape
    dp, ctx = lax.axis_size("dp"), lax.axis_size("ctx")
    columns = channels // dp
    lengths = doc_lengths[0]
    documents = lengths.shape[0]
    count = short_taps.shape[0]
    first_row = lax.axis_index("ctx") * rows
    ends = jnp.cumsum(lengths)
    bounds = jnp.concatenate([jnp.zeros((1,), jnp.int32), ends]) - first_row
    at = jnp.arange(rows, dtype=jnp.int32)
    low = jnp.sum((bounds[:documents] <= 0).astype(jnp.int32)) - 1
    high = jnp.sum((bounds[:documents] <= rows - 1).astype(jnp.int32)) - 1
    meta = jnp.concatenate([low[None], high[None], bounds])
    start_at = jnp.max(jnp.where(bounds[None, :documents] <= at[:, None], bounds[None, :documents],
                                 -first_row), axis=1)
    end_at = jnp.min(jnp.where(bounds[None, 1:] > at[:, None], bounds[None, 1:],
                               bounds[documents]), axis=1)
    reach = jnp.broadcast_to((at - start_at)[:, None], (rows, LANES))
    left = jnp.broadcast_to((end_at - at)[:, None], (rows, LANES))

    before = passed_along(v[rows - 8 :], 1)

    whole = lambda r: pl.BlockSpec((r, LANES), lambda i: (0, 0))
    block = lambda r: pl.BlockSpec((r, columns), lambda i: (0, i))
    params = pltpu.CompilerParams(vmem_limit_bytes=48 << 20)
    shaped = lambda r, t: jax.ShapeDtypeStruct((r, channels), t)
    mixed, adj, short = pl.pallas_call(
        mix_kernel,
        grid=(dp,),
        in_specs=[whole(rows), block(rows), block(8), block(rows), block(rows), block(rows), block(count)],
        out_specs=[block(rows)] * 3,
        out_shape=[shaped(rows, BF), shaped(rows, BF), shaped(rows, F32)],
        scratch_shapes=[pltpu.VMEM((rows + 8, columns), F32)],
        compiler_params=params,
    )(reach, v, before, gs, gl, up, short_taps)

    prev = passed_along(mixed, 1)
    following = passed_along(adj, -1)

    matrices = [jnp.asarray(m) for m in spectra(rows)]
    full = lambda m: pl.BlockSpec(m.shape, lambda i: (0, 0))
    out, ggs, gv, ggl, grads, head, tail = pl.pallas_call(
        main_kernel,
        grid=(dp,),
        in_specs=[pl.BlockSpec(memory_space=pltpu.SMEM), whole(rows), whole(rows), block(rows), block(8)]
        + [block(rows)] * 8 + [block(count), block(rows)] + [full(m) for m in matrices],
        out_specs=[block(rows)] * 4
        + [pl.BlockSpec((None, rows + 16, columns), lambda i: (i, 0, 0)), block(8), block(16)],
        out_shape=[shaped(rows, BF)] * 4
        + [jax.ShapeDtypeStruct((dp, rows + 16, columns), BF), shaped(8, BF), shaped(16, F32)],
        scratch_shapes=[
            pltpu.VMEM((rows, columns), F32), pltpu.VMEM((rows, columns), F32),
            pltpu.VMEM((2 * rows, columns), F32), pltpu.VMEM((2 * rows, columns), F32),
            pltpu.VMEM((rows + 8, columns), F32), pltpu.VMEM((rows + 8, columns), F32),
        ],
        compiler_params=params,
    )(meta, reach, left, v, before, gs, gl, up, mixed, adj, short, prev, following,
      short_taps, long_taps, *matrices)

    after = passed_along(head, -1).astype(F32)
    padded = jnp.concatenate([jnp.zeros((16, channels), F32), after, jnp.zeros((8, channels), F32)])
    for j in range(1, count):
        tail = tail + short_taps[j][None, :] * jnp.where(
            (left[rows - 16 :, :1] > j), padded[j : j + 16], 0.0)
    gv = lax.dynamic_update_slice(gv, tail.astype(BF), (rows - 16, 0))

    kept = rows + 8
    factor = 1.0 / math.sqrt(dp * ctx * rows)
    share = lax.all_to_all(grads[:, :kept], "dp", 0, 0, tiled=True)
    share = jnp.sum(share.astype(F32), axis=0).astype(BF)
    share = lax.all_to_all(share.reshape(ctx, -1, LANES), "ctx", 0, 0, tiled=True)
    share = (jnp.sum(share.astype(F32), axis=0) * factor).astype(BF)
    share = lax.all_to_all(jnp.broadcast_to(share[None], (ctx,) + share.shape), "ctx", 0, 0, tiled=True)
    share = share.reshape(1, kept, columns)
    share = lax.all_to_all(jnp.broadcast_to(share, (dp, kept, columns)), "dp", 0, 0, tiled=True)
    total = share.transpose(1, 0, 2).reshape(kept, channels).astype(F32)
    return (out[None], ggs[None], gv[None], ggl[None], total[rows : rows + count], total[:rows])


def solution(mesh):
    rowed = P("dp", "ctx", None)
    return jax.shard_map(
        on_device,
        mesh=mesh,
        in_specs=(P("dp", None), rowed, rowed, rowed, P(), P(), rowed),
        out_specs=(rowed, rowed, rowed, rowed, P(), P()),
        check_vma=False,
    )
```

time: 1250 us -> 184 us (0.15)
  other arithmetic: 885 us -> 3.95 us
  waiting for transfers between devices: 279 us -> 46.1 us
  blocking collectives: 0 us -> 59.7 us
  Pallas kernels: 0 us -> 29.1 us
  local copies, waits for them, and re-layouts: 49.4 us -> 21.4 us
  between operations: 17 us -> 2.15 us
    broadcast_in_dim x3 -> x0, other arithmetic: 567 us -> none  [the longest x1 509 us: on_device(): grad_gate_long[None]]
    psum x1 -> x0, waiting for transfers between devices: 256 us -> none  [on_device(): lax.psum((short_terms, long_terms), ('dp', 'ctx'))]
    reduce_sum x24 -> x3, other arithmetic: 169 us -> 0.84 us  [the longest x1 0.64 us: on_device(): low = jnp.sum((bounds[:documents] <= 0).astype(jnp.int32)) - 1]
    add x3 -> x0, other arithmetic: 85.1 us -> none  [the longest x1 42.9 us: adjoint(): summed + filter_taps[offset][None, :] * jnp.where(masked[:, None], window...]
    all_to_all x0 -> x2, blocking collectives: none -> 59.7 us  [the longest x1 37.1 us: on_device(): lax.all_to_all(share.reshape(ctx, -1, LANES), 'ctx', 0, 0, tiled=True)]
    concatenate x10 -> x2, other arithmetic: 42.9 us -> 0.1 us  [the longest x1 0.08 us: on_device(): meta = jnp.concatenate([low[None], high[None], bounds])]
    pallas_call x0 -> x2, Pallas kernels: none -> 29.1 us  [the longest x1 21.5 us: on_device(): pl.pallas_call(main_kernel, grid=(dp,), in_specs=[pl.BlockSpec(memory_spa...]
    another operation x2 -> x0, local copies, waits for them, and re-layouts: 24.7 us -> none  [tap_grads(): return jnp.stack(tap_rows)]
  transfers between devices with their start and end apart: 5 -> 6, of which waited for: 3 -> 4; matrix products, arithmetic and copies ran while one was open for 16% -> 3% of each run, Pallas kernels for 0% -> 0%
where the time goes in v1:
time: 184 us
  blocking collectives  59.7 us (32%)
  waiting for transfers between devices  46.1 us (25%)
  Pallas kernels  29.1 us (16%)
  starting transfers between devices  22 us (12%)
  local copies, waits for them, and re-layouts  21.4 us (12%)
  other arithmetic  3.95 us (2%)
  between operations  2.15 us (1%)
    all_to_all x1, blocking collectives, on_device(): lax.all_to_all(share.reshape(ctx, -1, LANES), 'ctx', 0, 0, tiled=True)  37.1 us
    ppermute x4, waiting for transfers between devices, passed_along(): return lax.ppermute(block, 'ctx', route)  23 us
    all_to_all x1, blocking collectives, on_device(): share = lax.all_to_all(grads[:, :kept], 'dp', 0, 0, tiled=True)  22.6 us
    pallas_call x1, Pallas kernels, on_device(): pl.pallas_call(main_kernel, grid=(dp,), in_specs=[pl.BlockSpec(memory_spa...  21.5 us
    all_to_all x1, waiting for transfers between devices, on_device(): lax.all_to_all(jnp.broadcast_to(share, (dp, kept, columns)), 'dp', 0, 0,...  14.8 us
    unnamed x37, local copies, waits for them, and re-layouts  13.7 us
    ppermute x4, starting transfers between devices, passed_along(): return lax.ppermute(block, 'ctx', route)  10.6 us
    all_to_all x1, waiting for transfers between devices, on_device(): lax.all_to_all(jnp.broadcast_to(share[None], (ctx,) + share.shape), 'ctx'...  8.4 us
  transfers between devices with their start and end apart: 6, of which 4 were waited for; matrix products, arithmetic and copies ran while one was open for 3% of the time, Pallas kernels for 0%

profile of v1, /device:TPU:1, one launch (start us, length us, event | category | flops | bytes accessed | tf_op | source)
XLA Modules:
  0.0 184.4 jit_solution(1792845819543753307)
XLA Ops:
  0.6 0.8 slice_bitcast_fusion
  1.5 3.9 %collective-permute-start = (bf16[8,4096]{1,0:T(8,128)(2,1)S(1)}, bf16[8,4096]{1,0:T(8,128)(2,1)S(1)}, u32[]{:S(2)}, u32[]{:S(2)}) collective-permute-start(bf16[8,4096]{1,0:T(8,128)(2,1)S(1)} %slice_bitcast_fusion), channel_id=1, source_target_pairs={{0,1},{1,2},{2,3},{3,4},{4,5},{5,6},{6,7},{7,8},{8,9},{9,10},{10,1... | collective-permute-start | bytes 196616 | tf_op jit(solution)/shard_map/ppermute | solution.py:43
  5.4 0.8 reduce-window.9
  7.6 0.7 select_reduce_fusion
  8.4 1.2 copy-done
  9.6 1.2 copy-done.2
  10.8 1.2 copy-done.4
  12.1 0.9 copy-done.7
  13.0 7.6 %shard_map.163 = (bf16[128,4096]{1,0:T(8,128)(2,1)}, bf16[128,4096]{1,0:T(8,128)(2,1)}, f32[128,4096]{1,0:T(8,128)}) custom-call(s32[128,128]{1,0:T(8,128)S(1)} %broadcast_in_dim.114.reach_ref, bf16[128,4096]{1,0:T(8,128)(2,1)S(1)} %bitcast.27, bf16[8,4096]{1,0:T(8,128)(2,1)S(1)} %collective-permute-done.before_ref, bf16[128,4096]{1,0:T(8,128)(2,1)S(1)} %bitcast.29, ...), custom_call_target="tpu_custom_call" | custom-call | tf_op jit(solution)/shard_map/pallas_call | solution.py:177
  20.6 4.1 %collective-permute-start.1 = (bf16[128,4096]{1,0:T(8,128)(2,1)}, bf16[128,4096]{1,0:T(8,128)(2,1)}, u32[]{:S(2)}, u32[]{:S(2)}) collective-permute-start(bf16[128,4096]{1,0:T(8,128)(2,1)} %get-tuple-element.16.mixed_ref), channel_id=1, source_target_pairs={{0,1},{1,2},{2,3},{3,4},{4,5},{5,6},{6,7},{7,8},{8,9},{9,10},{10,1... | collective-permute-start | bytes 3145736 | tf_op jit(solution)/shard_map/ppermute | solution.py:43
  24.7 1.3 collective-permute-start.2
  27.4 18.1 %collective-permute-done.1.prev_ref = bf16[128,4096]{1,0:T(8,128)(2,1)} collective-permute-done((bf16[128,4096]{1,0:T(8,128)(2,1)}, bf16[128,4096]{1,0:T(8,128)(2,1)}, u32[]{:S(2)}, u32[]{:S(2)}) %collective-permute-start.1) | collective-permute-done | bytes 1048608 | tf_op jit(solution)/shard_map/ppermute | solution.py:43
  45.5 4.8 %collective-permute-done.2.next_ref = bf16[128,4096]{1,0:T(8,128)(2,1)} collective-permute-done((bf16[128,4096]{1,0:T(8,128)(2,1)}, bf16[128,4096]{1,0:T(8,128)(2,1)}, u32[]{:S(2)}, u32[]{:S(2)}) %collective-permute-start.2) | collective-permute-done | bytes 1048608 | tf_op jit(solution)/shard_map/ppermute | solution.py:43
  50.5 1.2 copy-done.6
  51.7 0.9 copy-done.12
  52.6 0.9 copy-done.13
  53.5 0.9 copy-done.14
  54.4 0.9 copy-done.15
  55.3 21.5 %shard_map.164 = (bf16[128,4096]{1,0:T(8,128)(2,1)}, bf16[128,4096]{1,0:T(8,128)(2,1)}, bf16[128,4096]{1,0:T(8,128)(2,1)}, bf16[128,4096]{1,0:T(8,128)(2,1)}, bf...) custom-call(s32[11]{0:T(128)S(1)} %pad_add_fusion.meta_ref, ...), custom_call_target="tpu_custom_call" | custom-call | tf_op jit(solution)/shard_map/pallas_call | solution.py:192
  76.8 0.7 copy-done.9
  78.2 1.3 slice.105
  79.5 22.6 %all_to_all.20 = bf16[8,136,512]{2,1,0:T(8,128)(2,1)S(1)} all-to-all(bf16[8,136,512]{2,1,0:T(8,128)(2,1)S(1)} %slice.105), channel_id=1, replica_groups=mesh['dp'=8,'ctx'=32] {'dp'}, dimensions={0} | all-to-all | bytes 2228224 | tf_op jit(solution)/shard_map/all_to_all | solution.py:219
  102.4 37.1 %all_to_all.21 = bf16[32,17,128]{2,1,0:T(8,128)(2,1)S(1)} all-to-all(bf16[32,17,128]{2,1,0:T(8,128)(2,1)S(1)} %reshape.84), channel_id=1, replica_groups=mesh['dp'=8,'ctx'=32] {'ctx'}, dimensions={0} | all-to-all | bytes 278528 | tf_op jit(solution)/shard_map/all_to_all | solution.py:221
  140.2 4.6 %all-to-all-start.2 = ((bf16[32,17,128]{2,1,0:T(8,128)(2,1)}), bf16[32,17,128]{2,1,0:T(8,128)(2,1)S(1)}, u32[]{:S(2)}, u32[]{:S(2)}) async-start(bf16[32,17,128]{2,1,0:T(8,128)(2,1)} %broadcast_in_dim.129), calls=%async_computation.2 | async-start | bytes 393216 | tf_op jit(solution)/shard_map/all_to_all | solution.py:223
  144.9 1.3 collective-permute-start.3
  146.3 8.4 %all-to-all-done.2 = bf16[32,17,128]{2,1,0:T(8,128)(2,1)S(1)} async-done(((bf16[32,17,128]{2,1,0:T(8,128)(2,1)}), bf16[32,17,128]{2,1,0:T(8,128)(2,1)S(1)}, u32[]{:S(2)}, u32[]{:S(2)}) %all-to-all-start.2) | async-done | bytes 139296 | tf_op jit(solution)/shard_map/all_to_all | solution.py:223
  154.8 1.1 broadcast_in_dim.131
  155.9 6.8 %all-to-all-start.3 = ((bf16[8,136,512]{2,1,0:T(8,128)(2,1)}), bf16[8,136,512]{2,1,0:T(8,128)(2,1)S(1)}, u32[]{:S(2)}, u32[]{:S(2)}) async-start(bf16[8,136,512]{2,1,0:T(8,128)(2,1)} %broadcast_in_dim.131), calls=%async_computation.3 | async-start | bytes 2228224 | tf_op jit(solution)/shard_map/all_to_all | solution.py:225
  162.7 1.0 bitcast_dynamic-update-slice_fusion
  163.7 14.8 %all-to-all-done.3 = bf16[8,136,512]{2,1,0:T(8,128)(2,1)S(1)} async-done(((bf16[8,136,512]{2,1,0:T(8,128)(2,1)}), bf16[8,136,512]{2,1,0:T(8,128)(2,1)S(1)}, u32[]{:S(2)}, u32[]{:S(2)}) %all-to-all-start.3) | async-done | bytes 1114144 | tf_op jit(solution)/shard_map/all_to_all | solution.py:225
  179.7 1.8 copy.24
  181.5 2.9 %copy.25 = f32[128,4096]{1,0:T(8,128)} copy(f32[128,4096]{0,1:T(8,128)} %bitcast.35) | data formatting | bytes 4194304
  (48 shorter events, 4.7 us)
Async XLA Ops:
  1.5 6.8 %collective-permute-start = (bf16[8,4096]{1,0:T(8,128)(2,1)S(1)}, bf16[8,4096]{1,0:T(8,128)(2,1)S(1)}, u32[]{:S(2)}, u32[]{:S(2)}) collective-permute-start(bf16[8,4096]{1,0:T(8,128)(2,1)S(1)} %slice_bitcast_fusion), channel_id=1, source_target_pairs={{0,1},{1,2},{2,3},{3,4},{4,5},{5,6},{6,7},{7,8},{8,9},{9,10},{10,1... | collective-permute-start | bytes 196616 | tf_op jit(solution)/shard_map/ppermute | solution.py:43
  8.4 1.2 copy-start
  9.6 1.2 copy-start.2
  10.8 1.2 copy-start.4
  12.1 0.9 copy-start.7
  13.0 37.4 %copy-start.1 = (bf16[1,128,4096]{2,1,0:T(8,128)(2,1)S(1)}, bf16[1,128,4096]{2,1,0:T(8,128)(2,1)}, u32[]{:S(2)}) copy-start(bf16[1,128,4096]{2,1,0:T(8,128)(2,1)} %param.13) | copy-start | bytes 3145732
  13.0 37.5 %copy-start.3 = (bf16[1,128,4096]{2,1,0:T(8,128)(2,1)S(1)}, bf16[1,128,4096]{2,1,0:T(8,128)(2,1)}, u32[]{:S(2)}) copy-start(bf16[1,128,4096]{2,1,0:T(8,128)(2,1)} %param.14) | copy-start | bytes 3145732
  13.0 37.5 %copy-start.5 = (bf16[1,128,4096]{2,1,0:T(8,128)(2,1)S(1)}, bf16[1,128,4096]{2,1,0:T(8,128)(2,1)}, u32[]{:S(2)}) copy-start(bf16[1,128,4096]{2,1,0:T(8,128)(2,1)} %param.15) | copy-start | bytes 3145732
  13.0 37.5 %copy-start.8 = (f32[7,4096]{1,0:T(8,128)S(1)}, f32[7,4096]{1,0:T(8,128)}, u32[]{:S(2)}) copy-start(f32[7,4096]{1,0:T(8,128)} %staps_ref.1) | copy-start | bytes 344068
  13.0 37.5 %copy-start.11 = (bf16[256,256]{1,0:T(8,128)(2,1)S(1)}, bf16[256,256]{1,0:T(8,128)(2,1)}, u32[]{:S(2)}) copy-start(bf16[256,256]{1,0:T(8,128)(2,1)} %constant.58.clone.first_ref) | copy-start | bytes 393220
  20.6 24.9 %collective-permute-start.1 = (bf16[128,4096]{1,0:T(8,128)(2,1)}, bf16[128,4096]{1,0:T(8,128)(2,1)}, u32[]{:S(2)}, u32[]{:S(2)}) collective-permute-start(bf16[128,4096]{1,0:T(8,128)(2,1)} %get-tuple-element.16.mixed_ref), channel_id=1, source_target_pairs={{0,1},{1,2},{2,3},{3,4},{4,5},{5,6},{6,7},{7,8},{8,9},{9,10},{10,1... | collective-permute-start | bytes 3145736 | tf_op jit(solution)/shard_map/ppermute | solution.py:43
  24.7 25.6 %collective-permute-start.2 = (bf16[128,4096]{1,0:T(8,128)(2,1)}, bf16[128,4096]{1,0:T(8,128)(2,1)}, u32[]{:S(2)}, u32[]{:S(2)}) collective-permute-start(bf16[128,4096]{1,0:T(8,128)(2,1)} %get-tuple-element.17.adj_ref), channel_id=1, source_target_pairs={{1,0},{2,1},{3,2},{4,3},{5,4},{6,5},{7,6},{8,7},{9,8},{10,9},{11,1... | collective-permute-start | bytes 3145736 | tf_op jit(solution)/shard_map/ppermute | solution.py:43
  50.5 1.2 copy-start.6
  51.7 0.9 copy-start.12
  52.6 0.9 copy-start.13
  53.5 0.9 copy-start.14
  54.4 0.9 copy-start.15
  76.8 0.7 copy-start.9
  77.5 0.6 copy-start.16
  79.5 65.4 %copy-start.17 = (bf16[8,4096]{1,0:T(8,128)(2,1)S(1)}, bf16[8,4096]{1,0:T(8,128)(2,1)}, u32[]{:S(2)}) copy-start(bf16[8,4096]{1,0:T(8,128)(2,1)} %copy-done.16) | copy-start | bytes 196612
  140.2 14.5 %all-to-all-start.2 = ((bf16[32,17,128]{2,1,0:T(8,128)(2,1)}), bf16[32,17,128]{2,1,0:T(8,128)(2,1)S(1)}, u32[]{:S(2)}, u32[]{:S(2)}) async-start(bf16[32,17,128]{2,1,0:T(8,128)(2,1)} %broadcast_in_dim.129), calls=%async_computation.2 | async-start | bytes 393216 | tf_op jit(solution)/shard_map/all_to_all | solution.py:223
  144.9 17.8 %collective-permute-start.3 = (bf16[8,4096]{1,0:T(8,128)(2,1)S(1)}, bf16[8,4096]{1,0:T(8,128)(2,1)S(1)}, u32[]{:S(2)}, u32[]{:S(2)}) collective-permute-start(bf16[8,4096]{1,0:T(8,128)(2,1)S(1)} %copy-done.17), channel_id=1, source_target_pairs={{1,0},{2,1},{3,2},{4,3},{5,4},{6,5},{7,6},{8,7},{9,8},{10,9},{11,1... | collective-permute-start | bytes 196616 | tf_op jit(solution)/shard_map/ppermute | solution.py:43
  146.3 16.4 %copy-start.10 = (f32[16,4096]{1,0:T(8,128)S(1)}, f32[16,4096]{1,0:T(8,128)}, u32[]{:S(2)}) copy-start(f32[16,4096]{1,0:T(8,128)} %copy-done.9) | copy-start | bytes 786436
  155.9 22.6 %all-to-all-start.3 = ((bf16[8,136,512]{2,1,0:T(8,128)(2,1)}), bf16[8,136,512]{2,1,0:T(8,128)(2,1)S(1)}, u32[]{:S(2)}, u32[]{:S(2)}) async-start(bf16[8,136,512]{2,1,0:T(8,128)(2,1)} %broadcast_in_dim.131), calls=%async_computation.3 | async-start | bytes 2228224 | tf_op jit(solution)/shard_map/all_to_all | solution.py:225

commit v2 on v1

v2 whole, which is shorter than its diff:
```python
import math

import jax
import jax.numpy as jnp
import numpy as np
from jax import lax
from jax.experimental import pallas as pl
from jax.experimental.pallas import tpu as pltpu
from jax.sharding import PartitionSpec as P

BF = jnp.bfloat16
F32 = jnp.float32
LANES = 128
RIM = 8
CTX = ("z", "x")


def halves(matrix):
    high = matrix.astype(np.float32).astype(BF)
    low = (matrix - high.astype(np.float64)).astype(np.float32).astype(BF)
    return high, low


def spectra(rows):
    points = 2 * rows
    theta = np.pi * (2 * np.arange(rows) + 1) / points
    angles = theta[:, None] * np.arange(points)[None, :]
    forward = np.concatenate([np.cos(angles), -np.sin(angles)], axis=0)
    inverse = forward.T / rows

    def pack(matrix):
        return np.concatenate(halves(matrix), axis=1)

    def stack(matrix):
        return np.concatenate(halves(matrix), axis=0)

    first = pack(forward[:, :rows])
    second = pack(forward[:, rows:])
    to_later = stack(inverse[rows:])
    to_first = stack(inverse[:rows])
    to_taps = stack(inverse[rows - np.arange(rows)])
    return first, second, to_later, to_first, to_taps


def passed_along(block, distance):
    devices = range(lax.axis_size(CTX))
    route = [(i - distance, i) for i in devices if i - distance in devices]
    return lax.ppermute(block, CTX, route)


def wide(row_mask, columns):
    return jnp.concatenate([row_mask] * (columns // LANES), axis=1)


def row_ids(rows):
    return lax.broadcasted_iota(jnp.int32, (rows, LANES), 0)


def cuts_of(lengths_ref, rows):
    at = -lax.axis_index(CTX) * rows
    cuts = [at]
    for d in range(lengths_ref.shape[1]):
        at = at + lengths_ref[0, d]
        cuts.append(at)
    return cuts


def begin_at(cuts, at):
    begin = cuts[0]
    for cut in cuts[1:-1]:
        begin = jnp.where(cut <= at, cut, begin)
    return begin


def end_at(cuts, at):
    end = cuts[-1]
    for cut in cuts[-2:0:-1]:
        end = jnp.where(cut > at, cut, end)
    return end


def times(left, right, conjugate_left):
    half = left.shape[0] // 2
    a, b = left[:half], left[half:]
    c, d = right[:half], right[half:]
    if conjugate_left:
        return jnp.concatenate([a * c + b * d, a * d - b * c], axis=0)
    return jnp.concatenate([a * c - b * d, a * d + b * c], axis=0)


def dot(matrix, data):
    return jnp.dot(matrix, jnp.concatenate([data, data], axis=0), preferred_element_type=F32)


def back_dot(matrix, data):
    both = jnp.dot(matrix, data, preferred_element_type=F32)
    half = matrix.shape[0] // 2
    return both[:half] + both[half:]


def on_first_step(fill):
    pl.when(pl.program_id(0) == 0)(fill)


def mix_kernel(lengths_ref, v_ref, before_ref, gs_ref, taps_ref, mixed_ref, short_ref, ext, reach_s):
    rows, columns = v_ref.shape

    @on_first_step
    def _():
        at = row_ids(rows)
        reach_s[...] = at - begin_at(cuts_of(lengths_ref, rows), at)

    ext[0:RIM, :] = before_ref[...].astype(F32)
    ext[RIM:, :] = v_ref[...].astype(F32)
    reach = wide(reach_s[...], columns)
    total = taps_ref[0:1, :] * ext[RIM:, :]
    for j in range(1, taps_ref.shape[0]):
        window = ext[RIM - j : RIM - j + rows, :]
        total = total + taps_ref[j : j + 1, :] * jnp.where(reach >= j, window, 0.0)
    short_ref[...] = total
    mixed_ref[...] = (gs_ref[...].astype(F32) * total).astype(BF)


def own_kernel(lengths_ref, mixed_ref, adj_ref, ltaps_ref, first_ref, second_ref, later_ref,
               front_ref, totaps_ref, long_ref, back_ref, grads_ref, taps_spec, spec_acc, cuts_s):
    rows, columns = mixed_ref.shape
    cuts = cuts_of(lengths_ref, rows)
    low, high = -1, -1
    for d, cut in enumerate(cuts):
        cuts_s[d] = cut
        if d < len(cuts) - 1:
            low = low + (cut <= 0).astype(jnp.int32)
            high = high + (cut <= rows - 1).astype(jnp.int32)
    taps_spec[...] = dot(first_ref[...], ltaps_ref[...].astype(BF))
    long_ref[...] = jnp.zeros_like(long_ref)
    back_ref[...] = jnp.zeros_like(back_ref)
    spec_acc[...] = jnp.zeros_like(spec_acc)
    at = row_ids(rows)

    def document(d, carry):
        inside = jnp.where((at >= cuts_s[d]) & (at < cuts_s[d + 1]), 1.0, 0.0)
        own = wide(inside, columns)
        own_bf = wide(inside.astype(BF), columns)
        x_spec = dot(second_ref[...], mixed_ref[...] * own_bf)
        product = times(taps_spec[...], x_spec, False).astype(BF)
        long_ref[...] += own * back_dot(later_ref[...], product)
        a_spec = dot(first_ref[...], adj_ref[...] * own_bf)
        spec_acc[...] += times(a_spec, x_spec, True)
        product = times(taps_spec[...], a_spec, True).astype(BF)
        back_ref[...] += own * back_dot(front_ref[...], product)
        return carry

    lax.fori_loop(low, high + 1, document, 0)
    grads_ref[...] = back_dot(totaps_ref[...], spec_acc[...].astype(BF))


def grad_kernel(lengths_ref, v_ref, before_ref, gs_ref, adj_ref, short_ref, back_ref, own_grads_ref,
                prev_ref, next_ref, staps_ref, ltaps_ref, first_ref, second_ref, front_ref, totaps_ref,
                ggs_ref, adjs_ref, head_ref, grads_ref, ext, reach_s, masks_s):
    rows, columns = v_ref.shape

    @on_first_step
    def _():
        at = row_ids(rows)
        cuts = cuts_of(lengths_ref, rows)
        reach_s[...] = at - begin_at(cuts, at)
        ones = lambda mask: jnp.where(mask, 1.0, 0.0).astype(BF)
        masks_s[0 * rows : 1 * rows, :] = ones(at < end_at(cuts, 0))
        masks_s[1 * rows : 2 * rows, :] = ones(at - rows >= begin_at(cuts, 0))
        masks_s[2 * rows : 3 * rows, :] = ones(at >= begin_at(cuts, rows - 1))
        masks_s[3 * rows : 4 * rows, :] = ones(at + rows < end_at(cuts, rows - 1))

    mask = lambda k: wide(masks_s[k * rows : (k + 1) * rows, :], columns)
    taps_spec = dot(first_ref[...], ltaps_ref[...].astype(BF))
    next_spec = dot(second_ref[...], next_ref[...] * mask(3))
    product = times(taps_spec, next_spec, True).astype(BF)
    back = back_ref[...] + mask(2).astype(F32) * back_dot(front_ref[...], product)
    prev_spec = dot(first_ref[...], prev_ref[...] * mask(1))
    own_spec = dot(first_ref[...], adj_ref[...] * mask(0))
    product = times(own_spec, prev_spec, True).astype(BF)
    long_terms = own_grads_ref[...] + back_dot(totaps_ref[...], product)

    ggs_ref[...] = (back * short_ref[...]).astype(BF)
    adj_short = (back * gs_ref[...].astype(F32)).astype(BF)
    adjs_ref[...] = adj_short
    adj_short = adj_short.astype(F32)
    head_ref[...] = adj_short[0:RIM].astype(BF)
    ext[0:RIM, :] = before_ref[...].astype(F32)
    ext[RIM:, :] = v_ref[...].astype(F32)
    reach = wide(reach_s[...], columns)
    terms = [jnp.sum(adj_short * ext[RIM:, :], axis=0, keepdims=True)]
    for j in range(1, staps_ref.shape[0]):
        window = ext[RIM - j : RIM - j + rows, :]
        terms.append(jnp.sum(jnp.where(reach >= j, adj_short * window, 0.0), axis=0, keepdims=True))
    terms.append(jnp.zeros((RIM - len(terms), columns), F32))
    terms = jnp.concatenate([long_terms] + terms, axis=0).astype(BF)
    for k in range(columns // LANES):
        grads_ref[k] = terms[:, k * LANES : (k + 1) * LANES]


def long_kernel(lengths_ref, gl_ref, up_ref, long_ref, prev_ref, ltaps_ref, first_ref, later_ref,
                out_ref, ggl_ref, masks_s):
    rows, columns = gl_ref.shape

    @on_first_step
    def _():
        at = row_ids(rows)
        cuts = cuts_of(lengths_ref, rows)
        ones = lambda mask: jnp.where(mask, 1.0, 0.0).astype(BF)
        masks_s[0 * rows : 1 * rows, :] = ones(at < end_at(cuts, 0))
        masks_s[1 * rows : 2 * rows, :] = ones(at - rows >= begin_at(cuts, 0))

    mask = lambda k: wide(masks_s[k * rows : (k + 1) * rows, :], columns)
    taps_spec = dot(first_ref[...], ltaps_ref[...].astype(BF))
    prev_spec = dot(first_ref[...], prev_ref[...] * mask(1))
    product = times(taps_spec, prev_spec, False).astype(BF)
    long_mix = long_ref[...] + mask(0).astype(F32) * back_dot(later_ref[...], product)
    out_ref[...] = (gl_ref[...].astype(F32) * long_mix).astype(BF)
    ggl_ref[...] = (up_ref[...].astype(F32) * long_mix).astype(BF)


def values_kernel(lengths_ref, adjs_ref, after_ref, taps_ref, gv_ref, move):
    rows, columns = adjs_ref.shape
    count = taps_ref.shape[0]

    @on_first_step
    def _():
        at = lax.broadcasted_iota(jnp.int32, (rows, 2 * LANES), 0)
        source = lax.broadcasted_iota(jnp.int32, (rows, 2 * LANES), 1)
        left = end_at(cuts_of(lengths_ref, rows), at) - at
        for j in range(count):
            move[j * rows : (j + 1) * rows, :] = jnp.where(
                (source == at + j) & (left > j), 1.0, 0.0).astype(BF)

    rim = jnp.concatenate([after_ref[...].astype(F32), jnp.zeros((LANES - RIM, columns), F32)], axis=0)
    data = jnp.concatenate([adjs_ref[...], rim.astype(BF)], axis=0)
    moved = jnp.dot(move[...], data, preferred_element_type=F32)
    total = taps_ref[0:1, :] * moved[:rows]
    for j in range(1, count):
        total = total + taps_ref[j : j + 1, :] * moved[j * rows : (j + 1) * rows]
    gv_ref[...] = total.astype(BF)


def spread_kernel(mine_ref, other_ref, short_ref, long_ref):
    rows = long_ref.shape[0]

    def write(blocks):
        for k in range(blocks.shape[0]):
            shares = blocks[k].astype(F32)
            at = slice(k * LANES, (k + 1) * LANES)
            long_ref[:, at] = shares[:rows]
            short_ref[:, at] = shares[rows : rows + short_ref.shape[0]]

    own_turn = pl.program_id(0) == lax.axis_index("core")
    pl.when(own_turn)(lambda: write(mine_ref))
    pl.when(jnp.logical_not(own_turn))(lambda: write(other_ref))


def kernels(rows, channels, count):
    shaped = lambda r, t: jax.ShapeDtypeStruct((r, channels), t)
    first, second, later, front, totaps = [jnp.asarray(m) for m in spectra(rows)]
    parts = channels // LANES

    def call(kernel, parts_per_step, ins, outs, scratch, cost, arrays, mib):
        columns = parts_per_step * LANES

        def spec(shape):
            if shape is None:
                return pl.BlockSpec(memory_space=pltpu.SMEM)
            if isinstance(shape, int):
                return pl.BlockSpec((shape, columns), lambda i: (0, i))
            if len(shape) == 2 and shape[1] == LANES:
                return pl.BlockSpec((parts // 2,) + shape, lambda i: (0, 0, 0))
            if len(shape) == 3:
                return pl.BlockSpec((parts_per_step,) + shape[1:], lambda i: (i, 0, 0))
            return pl.BlockSpec(shape, lambda i: (0, 0))

        return pl.pallas_call(
            kernel,
            grid=(parts // parts_per_step,),
            in_specs=[spec(i) for i in ins],
            out_specs=[spec(o.shape[0] if len(o.shape) == 2 else o.shape) for o in outs],
            out_shape=outs,
            scratch_shapes=[pltpu.VMEM((r, c if c else columns), t) if r else t for r, c, t in scratch],
            compiler_params=pltpu.CompilerParams(vmem_limit_bytes=mib << 20),
            cost_estimate=pl.CostEstimate(
                flops=0, bytes_accessed=int(cost * 3.5e6), transcendentals=0),
        )(*arrays)

    small = min(8, parts // 2)
    large = min(16, parts // 2)
    ext = (rows + RIM, 0, F32)
    spectrum = (2 * rows, 0, F32)
    tables = lambda *chosen: [t.shape for t in chosen]
    grads_shape = jax.ShapeDtypeStruct((parts, rows + RIM, LANES), BF)

    def mix(*arrays):
        return call(mix_kernel, small, [None, rows, RIM, rows, count],
                    [shaped(rows, BF), shaped(rows, F32)], [ext, (rows, LANES, jnp.int32)], 6, arrays, 56)

    def own(*arrays):
        used = (first, second, later, front, totaps)
        return call(own_kernel, large, [None, rows, rows, rows] + tables(*used),
                    [shaped(rows, F32)] * 3,
                    [spectrum, spectrum, (0, 0, pltpu.SMEM((16,), jnp.int32))], 15, arrays + used, 40)

    def grad(*arrays):
        used = (first, second, front, totaps)
        return call(grad_kernel, small, [None, rows, RIM] + [rows] * 7 + [count, rows] + tables(*used),
                    [shaped(rows, BF), shaped(rows, BF), shaped(RIM, BF), grads_shape],
                    [ext, (rows, LANES, jnp.int32), (4 * rows, LANES, BF)], 12, arrays + used, 30)

    def long(*arrays):
        used = (first, later)
        return call(long_kernel, large, [None] + [rows] * 5 + tables(*used),
                    [shaped(rows, BF)] * 2, [(2 * rows, LANES, BF)], 6, arrays + used, 32)

    def values_grad(*arrays):
        return call(values_kernel, large, [None, rows, RIM, count], [shaped(rows, BF)],
                    [(count * rows, 2 * LANES, BF)], 4, arrays, 24)[0]

    def spread(mine, other):
        return call(spread_kernel, parts // 2, [mine.shape[1:], other.shape[1:]],
                    [shaped(count, F32), shaped(rows, F32)], [], 3, (mine, other), 24)

    return mix, own, grad, long, values_grad, spread


def traded(block, axes):
    return lax.all_to_all(block, axes, 0, 0, tiled=True)


def copies(block, axes):
    return traded(jnp.broadcast_to(block[None], (lax.axis_size(axes),) + block.shape), axes)


def added(blocks):
    return jnp.sum(blocks.astype(F32), axis=0)


def swapped(block):
    return lax.ppermute(block, "core", [(0, 1), (1, 0)])


def on_device(lengths, values, gate_short, gate_long, short_taps, long_taps, cotangent):
    v, gs, gl, up = values[0], gate_short[0], gate_long[0], cotangent[0]
    rows, channels = v.shape
    mix, own, grad, long, values_grad, spread = kernels(rows, channels, short_taps.shape[0])
    factor = 1.0 / math.sqrt(lax.axis_size(("y", "core", "z", "x")) * rows)

    before = passed_along(v[rows - RIM :], 1)
    adj = (up.astype(F32) * gl.astype(F32)).astype(BF)
    following = passed_along(adj, -1)
    mixed, short = mix(lengths, v, before, gs, short_taps)
    prev = passed_along(mixed, 1)
    own_long, own_back, own_grads = own(lengths, mixed, adj, long_taps)
    ggs, adjs, head, grads = grad(lengths, v, before, gs, adj, short, own_back, own_grads,
                                  prev, following, short_taps, long_taps)
    after = passed_along(head, -1)

    core = lax.axis_index("core")
    planes = ("y", "x")
    split = grads.reshape((2, grads.shape[0] // 2) + grads.shape[1:])
    pick = lambda i: lax.dynamic_index_in_dim(split, i, 0, keepdims=False)
    half = (pick(core).astype(F32) + swapped(pick(1 - core)).astype(F32)).astype(BF)
    half, own_long, adjs = lax.optimization_barrier((half, own_long, adjs))
    share = half.reshape((lax.axis_size(planes), -1) + half.shape[1:])
    share = added(traded(share, planes)).astype(BF)
    out, ggl = long(lengths, gl, up, own_long, prev, long_taps)
    share, out, ggl, adjs = lax.optimization_barrier((share, out, ggl, adjs))
    share = (added(copies(share, "z")) * factor).astype(BF)
    gv = values_grad(lengths, adjs, after, short_taps)
    share, gv = lax.optimization_barrier((share, gv))
    mine = copies(share, planes).reshape(half.shape)
    grad_short, grad_long = spread(mine, swapped(mine))
    return out[None], ggs[None], gv[None], ggl[None], grad_short, grad_long


def solution(mesh):
    dp, ctx = mesh.shape["dp"], mesh.shape["ctx"]
    cut = jax.sharding.Mesh(mesh.devices.reshape(dp // 2, 2, ctx // 4, 4), ("y", "core", "z", "x"))
    rowed = P(("y", "core"), CTX, None)
    return jax.shard_map(
        on_device,
        mesh=cut,
        in_specs=(P(("y", "core"), None), rowed, rowed, rowed, P(), P(), rowed),
        out_specs=(rowed, rowed, rowed, rowed, P(), P()),
        check_vma=False,
    )
```

time: 184 us -> 126 us (0.68)
  blocking collectives: 59.7 us -> 16.7 us
  waiting for transfers between devices: 46.1 us -> 18.7 us
  starting transfers between devices: 22 us -> 36.9 us
  local copies, waits for them, and re-layouts: 21.4 us -> 12.2 us
  Pallas kernels: 29.1 us -> 34.3 us
    all_to_all x2 -> x1, blocking collectives: 59.7 us -> 16.7 us  [traded(): return lax.all_to_all(block, axes, 0, 0, tiled=True)]
    all_to_all x2, waiting for transfers between devices: 23.2 us -> 3.9 us  [traded(): return lax.all_to_all(block, axes, 0, 0, tiled=True)]
    all_to_all x2, starting transfers between devices: 11.4 us -> 20.2 us  [traded(): return lax.all_to_all(block, axes, 0, 0, tiled=True)]
    ppermute x4 -> x6, waiting for transfers between devices: 23 us -> 14.8 us  [the longest x4 11.3 us: passed_along(): return lax.ppermute(block, CTX, route)]
    ppermute x4 -> x6, starting transfers between devices: 10.6 us -> 16.7 us  [the longest x4 11.6 us: passed_along(): return lax.ppermute(block, CTX, route)]
    pallas_call x2 -> x6, Pallas kernels: 29.1 us -> 34.3 us  [call(): pl.pallas_call(kernel, grid=(parts // parts_per_step,), in_specs=[spec(i)...]
    slice x7 -> x1, local copies, waits for them, and re-layouts: 5.53 us -> 0.85 us  [on_device(): before = passed_along(v[rows - RIM:], 1)]
    unnamed x37 -> x44, local copies, waits for them, and re-layouts: 13.7 us -> 9.73 us
  transfers between devices with their start and end apart: 6 -> 8, of which waited for: 4 -> 6; matrix products, arithmetic and copies ran while one was open for 3% -> 1% of each run, Pallas kernels for 0% -> 18%
where the time goes in v2:
time: 126 us; the launch traced here: 125 us
  starting transfers between devices  36.9 us (29%)
  Pallas kernels  34.3 us (27%)
  waiting for transfers between devices  18.7 us (15%)
  blocking collectives  16.7 us (13%)
  local copies, waits for them, and re-layouts  12.2 us (10%)
  other arithmetic  5.15 us (4%)
    pallas_call x6, Pallas kernels, call(): pl.pallas_call(kernel, grid=(parts // parts_per_step,), in_specs=[spec(i)...  34.3 us
    all_to_all x2, starting transfers between devices, traded(): return lax.all_to_all(block, axes, 0, 0, tiled=True)  20.2 us
    all_to_all x1, blocking collectives, traded(): return lax.all_to_all(block, axes, 0, 0, tiled=True)  16.7 us
    ppermute x4, starting transfers between devices, passed_along(): return lax.ppermute(block, CTX, route)  11.6 us
    ppermute x4, waiting for transfers between devices, passed_along(): return lax.ppermute(block, CTX, route)  11.3 us
    unnamed x44, local copies, waits for them, and re-layouts  9.73 us
    ppermute x2, starting transfers between devices, swapped(): return lax.ppermute(block, 'core', [(0, 1), (1, 0)])  5.06 us
    all_to_all x2, waiting for transfers between devices, traded(): return lax.all_to_all(block, axes, 0, 0, tiled=True)  3.9 us
  transfers between devices with their start and end apart: 8, of which 6 were waited for; matrix products, arithmetic and copies ran while one was open for 1% of the time, Pallas kernels for 18%

profile of v2, /device:TPU:1, one launch (start us, length us, event | category | flops | bytes accessed | tf_op | source)
XLA Modules:
  0.0 124.7 jit_solution(10578551472853610373)
XLA Ops:
  0.6 0.8 slice_bitcast_fusion
  1.5 4.1 %collective-permute-start = (bf16[8,4096]{1,0:T(8,128)(2,1)S(1)}, bf16[8,4096]{1,0:T(8,128)(2,1)S(1)}, u32[]{:S(2)}, u32[]{:S(2)}) collective-permute-start(bf16[8,4096]{1,0:T(8,128)(2,1)S(1)} %slice_bitcast_fusion), channel_id=1, source_target_pairs={{0,1},{1,2},{2,3},{3,4},{4,5},{5,6},{6,7},{7,8},{8,9},{9,10},{10,1... | collective-permute-start | bytes 196616 | tf_op jit(solution)/shard_map/ppermute | solution.py:48
  5.6 1.8 %multiply_convert_fusion.adj_ref = bf16[128,4096]{1,0:T(8,128)(2,1)S(1)} fusion(bf16[1,128,4096]{2,1,0:T(8,128)(2,1)} %param.15, bf16[1,128,4096]{2,1,0:T(8,128)(2,1)} %param.18), kind=kLoop, calls=%fused_computation | loop fusion | flops 2097152 | bytes 3145728 | tf_op jit(solution)/shard_map/convert_element_type | solution.py:352
  7.4 1.3 %collective-permute-start.2 = (bf16[128,4096]{1,0:T(8,128)(2,1)S(1)}, bf16[128,4096]{1,0:T(8,128)(2,1)}, u32[]{:S(2)}, u32[]{:S(2)}) collective-permute-start(bf16[128,4096]{1,0:T(8,128)(2,1)S(1)} %multiply_convert_fusion.adj_ref), channel_id=1, source_target_pairs={{1,0},{2,1},{3,2},{4,3},{5,4},{6,5},{7,6},{8,7},{9,8},{10,9},{11,1... | collective-permute-start | bytes 3145736 | tf_op jit(solution)/shard_map/ppermute | solution.py:48
  9.3 6.2 %shard_map.163 = (bf16[128,4096]{1,0:T(8,128)(2,1)}, f32[128,4096]{1,0:T(8,128)}) custom-call(s32[1,8]{1,0:T(1,128)} %lengths_ref.9, bf16[128,4096]{1,0:T(8,128)(2,1)} %bitcast.25, bf16[8,4096]{1,0:T(8,128)(2,1)} %copy-done.18, bf16[128,4096]{1,0:T(8,128)(2,1)} %bitcast.29, f32[7,4096]{1,0:T(8,128)} %taps_ref.3), custom_call_target="tpu_custom_call" | custom-call | bytes 21000000 | tf_op jit(solution)/shard_map/pallas_call | solution.py:278
  15.5 5.0 %collective-permute-start.1 = (bf16[128,4096]{1,0:T(8,128)(2,1)}, bf16[128,4096]{1,0:T(8,128)(2,1)}, u32[]{:S(2)}, u32[]{:S(2)}) collective-permute-start(bf16[128,4096]{1,0:T(8,128)(2,1)} %get-tuple-element.29.mixed_ref), channel_id=1, source_target_pairs={{0,1},{1,2},{2,3},{3,4},{4,5},{5,6},{6,7},{7,8},{8,9},{9,10},{10,1... | collective-permute-start | bytes 3145736 | tf_op jit(solution)/shard_map/ppermute | solution.py:48
  20.6 1.2 copy-done.11
  21.8 0.9 copy-done.15
  22.7 0.9 copy-done.16
  23.6 0.9 copy-done.17
  24.5 7.8 %shard_map.164 = (f32[128,4096]{1,0:T(8,128)S(1)}, f32[128,4096]{1,0:T(8,128)S(1)}, f32[128,4096]{1,0:T(8,128)S(1)}) custom-call(s32[1,8]{1,0:T(1,128)S(1)} %copy-done.20, bf16[128,4096]{1,0:T(8,128)(2,1)S(1)} %copy-done.11, bf16[128,4096]{1,0:T(8,128)(2,1)S(1)} %multiply_convert_fusion.adj_ref, f32[128,4096]{1,0:T(8,128)S(1)} %copy-done, ...), custom_call_target="tpu_custom_call" | custom-call | bytes 52500000 | tf_op jit(solution)/shard_map/pallas_call | solution.py:278
  32.4 1.3 %copy-done.5 = f32[128,4096]{1,0:T(8,128)} copy-done((f32[128,4096]{1,0:T(8,128)}, f32[128,4096]{1,0:T(8,128)S(1)}, u32[]{:S(2)}) %copy-start.5) | copy-done | bytes 2097176
  33.7 7.3 %collective-permute-done.1.prev_ref = bf16[128,4096]{1,0:T(8,128)(2,1)} collective-permute-done((bf16[128,4096]{1,0:T(8,128)(2,1)}, bf16[128,4096]{1,0:T(8,128)(2,1)}, u32[]{:S(2)}, u32[]{:S(2)}) %collective-permute-start.1) | collective-permute-done | bytes 1048608 | tf_op jit(solution)/shard_map/ppermute | solution.py:48
  41.1 10.2 %shard_map.165 = (bf16[128,4096]{1,0:T(8,128)(2,1)}, bf16[128,4096]{1,0:T(8,128)(2,1)S(1)}, bf16[8,4096]{1,0:T(8,128)(2,1)S(1)}, bf16[32,136,128]{2,1,0:T(8,128)(2,1)S(1)}) custom-call(s32[1,8]{1,0:T(1,128)S(1)} %copy-done.20, bf16[128,4096]{1,0:T(8,128)(2,1)S(1)} %bitcast.26, bf16[8,4096]{1,0:T(8,128)(2,1)S(1)} %copy-done.19, ...), custom_call_target="tpu_custom_call" | custom-call | bytes 42000000 | tf_op jit(solution)/shard_map/pallas_call | solution.py:278
  51.3 1.0 copy-done.10
  53.1 2.2 %collective-permute-start.3 = (bf16[16,136,128]{2,1,0:T(8,128)(2,1)}, bf16[16,136,128]{2,1,0:T(8,128)(2,1)}, u32[]{:S(2)}, u32[]{:S(2)}) collective-permute-start(bf16[16,136,128]{2,1,0:T(8,128)(2,1)} %dynamic-slice_bitcast_fusion), channel_id=1, source_target_pairs={{0,32},{32,0},{1,33},{33,1},{2,34},{34,2},{3,35},{35,3},{4,36},{36... | collective-permute-start | bytes 1671176 | tf_op jit(solution)/shard_map/ppermute | solution.py:342
  55.3 1.9 %collective-permute-done.3 = bf16[16,136,128]{2,1,0:T(8,128)(2,1)} collective-permute-done((bf16[16,136,128]{2,1,0:T(8,128)(2,1)}, bf16[16,136,128]{2,1,0:T(8,128)(2,1)}, u32[]{:S(2)}, u32[]{:S(2)}) %collective-permute-start.3) | collective-permute-done | bytes 557088 | tf_op jit(solution)/shard_map/ppermute | solution.py:342
  57.2 2.2 %fusion = bf16[16,136,128]{2,1,0:T(8,128)(2,1)} fusion(bf16[16,136,128]{2,1,0:T(8,128)(2,1)} %collective-permute-done.3, bf16[2,16,136,128]{3,2,1,0:T(8,128)(2,1)} %bitcast.34, s32[]{:T(128)S(6)} %select_n.7), kind=kLoop, calls=%fused_computation.2 | loop fusion | flops 1114112 | bytes 1671172 | tf_op jit(solution)/shard_map/convert_element_type | solution.py:365
  59.4 9.0 %all-to-all-start = ((bf16[16,1,136,128]{3,2,1,0:T(8,128)(2,1)}), bf16[16,1,136,128]{3,2,1,0:T(8,128)(2,1)}, u32[]{:S(2)}, u32[]{:S(2)}) async-start(bf16[16,1,136,128]{3,2,1,0:T(8,128)(2,1)} %bitcast.35), calls=%async_computation | async-start | bytes 1114112 | tf_op jit(solution)/shard_map/all_to_all | solution.py:330
  68.4 1.2 copy-done.3
  69.6 1.6 %copy-done.6 = f32[128,4096]{1,0:T(8,128)S(1)} copy-done((f32[128,4096]{1,0:T(8,128)S(1)}, f32[128,4096]{1,0:T(8,128)}, u32[]{:S(2)}) %copy-start.6) | copy-done | bytes 2097176
  71.2 4.8 %shard_map.166 = (bf16[128,4096]{1,0:T(8,128)(2,1)}, bf16[128,4096]{1,0:T(8,128)(2,1)}) custom-call(s32[1,8]{1,0:T(1,128)S(1)} %copy-done.20, bf16[128,4096]{1,0:T(8,128)(2,1)S(1)} %bitcast.27, bf16[128,4096]{1,0:T(8,128)(2,1)S(1)} %bitcast.28, f32[128,4096]{1,0:T(8,128)S(1)} %copy-done.6, bf16[128,4096]{1,0:T(8,128)(2,1)} %collective-permute-done.1.prev_ref, ...), custom_call_target="tpu_custom_call" | custom-call | bytes 21000000 | tf_op jit(solution)/shard_map/pallas_call | solution.py:278
  76.0 3.5 %all-to-all-done = bf16[16,1,136,128]{3,2,1,0:T(8,128)(2,1)} async-done(((bf16[16,1,136,128]{3,2,1,0:T(8,128)(2,1)}), bf16[16,1,136,128]{3,2,1,0:T(8,128)(2,1)}, u32[]{:S(2)}, u32[]{:S(2)}) %all-to-all-start) | async-done | bytes 557088 | tf_op jit(solution)/shard_map/all_to_all | solution.py:330
  79.5 1.1 reduce_sum.23
  81.4 11.2 %all-to-all-start.1 = ((bf16[8,1,136,128]{3,2,1,0:T(8,128)(2,1)}), bf16[8,1,136,128]{3,2,1,0:T(8,128)(2,1)S(1)}, u32[]{:S(2)}, u32[]{:S(2)}) async-start(bf16[8,1,136,128]{3,2,1,0:T(8,128)(2,1)} %broadcast_in_dim.31), calls=%async_computation.1 | async-start | bytes 557056 | tf_op jit(solution)/shard_map/all_to_all | solution.py:330
  92.6 1.3 %collective-permute-start.4 = (bf16[8,4096]{1,0:T(8,128)(2,1)}, bf16[8,4096]{1,0:T(8,128)(2,1)S(1)}, u32[]{:S(2)}, u32[]{:S(2)}) collective-permute-start(bf16[8,4096]{1,0:T(8,128)(2,1)} %copy-done.21), channel_id=1, source_target_pairs={{1,0},{2,1},{3,2},{4,3},{5,4},{6,5},{7,6},{8,7},{9,8},{10,9},{11,1... | collective-permute-start | bytes 196616 | tf_op jit(solution)/shard_map/ppermute | solution.py:48
  93.8 3.9 %collective-permute-done.4.after_ref = bf16[8,4096]{1,0:T(8,128)(2,1)S(1)} collective-permute-done((bf16[8,4096]{1,0:T(8,128)(2,1)}, bf16[8,4096]{1,0:T(8,128)(2,1)S(1)}, u32[]{:S(2)}, u32[]{:S(2)}) %collective-permute-start.4) | collective-permute-done | bytes 65568 | tf_op jit(solution)/shard_map/ppermute | solution.py:48
  97.8 3.8 %shard_map.167 = bf16[128,4096]{1,0:T(8,128)(2,1)} custom-call(s32[1,8]{1,0:T(1,128)S(1)} %copy-done.20, bf16[128,4096]{1,0:T(8,128)(2,1)S(1)} %copy-done.13, bf16[8,4096]{1,0:T(8,128)(2,1)S(1)} %collective-permute-done.4.after_ref, f32[7,4096]{1,0:T(8,128)S(1)} %copy-done.9), custom_call_target="tpu_custom_call" | custom-call | bytes 14000000 | tf_op jit(solution)/shard_map/pallas_call | solution.py:278
  102.1 16.7 %all_to_all.15 = bf16[16,1,136,128]{3,2,1,0:T(8,128)(2,1)S(1)} all-to-all(bf16[16,1,136,128]{3,2,1,0:T(8,128)(2,1)S(1)} %broadcast_in_dim.35), channel_id=1, replica_groups=mesh['y'=4,'core'=2,'z'=8,'x'=4] {'y','x'}, dimensions={0} | all-to-all | bytes 1114112 | tf_op jit(solution)/shard_map/all_to_all | solution.py:330
  118.7 2.9 %collective-permute-start.5 = (bf16[16,136,128]{2,1,0:T(8,128)(2,1)S(1)}, bf16[16,136,128]{2,1,0:T(8,128)(2,1)S(1)}, u32[]{:S(2)}, u32[]{:S(2)}) collective-permute-start(bf16[16,136,128]{2,1,0:T(8,128)(2,1)S(1)} %bitcast.31), channel_id=1, source_target_pairs={{0,32},{32,0},{1,33},{33,1},{2,34},{34,2},{3,35},{35,3},{4,36},{36... | collective-permute-start | bytes 1671176 | tf_op jit(solution)/shard_map/ppermute | solution.py:342
  121.7 1.6 %collective-permute-done.5.other_ref = bf16[16,136,128]{2,1,0:T(8,128)(2,1)S(1)} collective-permute-done((bf16[16,136,128]{2,1,0:T(8,128)(2,1)S(1)}, bf16[16,136,128]{2,1,0:T(8,128)(2,1)S(1)}, u32[]{:S(2)}, u32[]{:S(2)}) %collective-permute-start.5) | collective-permute-done | bytes 557088 | tf_op jit(solution)/shard_map/ppermute | solution.py:342
  123.2 1.5 %shard_map.168 = (f32[7,4096]{1,0:T(8,128)}, f32[128,4096]{1,0:T(8,128)}) custom-call(bf16[16,136,128]{2,1,0:T(8,128)(2,1)S(1)} %bitcast.32, bf16[16,136,128]{2,1,0:T(8,128)(2,1)S(1)} %collective-permute-done.5.other_ref), custom_call_target="tpu_custom_call" | custom-call | bytes 10500000 | tf_op jit(solution)/shard_map/pallas_call | solution.py:278
  (44 shorter events, 2.8 us)
Async XLA Ops:
  1.5 19.0 %copy-start = (f32[128,4096]{1,0:T(8,128)S(1)}, f32[128,4096]{1,0:T(8,128)}, u32[]{:S(2)}) copy-start(f32[128,4096]{1,0:T(8,128)} %ltaps_ref.5) | copy-start | bytes 6291460
  1.5 19.1 %copy-start.8 = (bf16[256,256]{1,0:T(8,128)(2,1)S(1)}, bf16[256,256]{1,0:T(8,128)(2,1)}, u32[]{:S(2)}) copy-start(bf16[256,256]{1,0:T(8,128)(2,1)} %constant.34.clone.first_ref) | copy-start | bytes 393220
  1.5 19.0 %copy-start.14 = (bf16[256,256]{1,0:T(8,128)(2,1)S(1)}, bf16[256,256]{1,0:T(8,128)(2,1)}, u32[]{:S(2)}) copy-start(bf16[256,256]{1,0:T(8,128)(2,1)} %constant.36.clone.later_ref) | copy-start | bytes 393220
  1.5 19.0 %copy-start.20 = (s32[1,8]{1,0:T(1,128)S(1)}, s32[1,8]{1,0:T(1,128)}, u32[]{:S(2)}) copy-start(s32[1,8]{1,0:T(1,128)} %lengths_ref.9) | copy-start | bytes 100
  1.5 7.2 %collective-permute-start = (bf16[8,4096]{1,0:T(8,128)(2,1)S(1)}, bf16[8,4096]{1,0:T(8,128)(2,1)S(1)}, u32[]{:S(2)}, u32[]{:S(2)}) collective-permute-start(bf16[8,4096]{1,0:T(8,128)(2,1)S(1)} %slice_bitcast_fusion), channel_id=1, source_target_pairs={{0,1},{1,2},{2,3},{3,4},{4,5},{5,6},{6,7},{7,8},{8,9},{9,10},{10,1... | collective-permute-start | bytes 196616 | tf_op jit(solution)/shard_map/ppermute | solution.py:48
  7.4 26.3 %collective-permute-start.2 = (bf16[128,4096]{1,0:T(8,128)(2,1)S(1)}, bf16[128,4096]{1,0:T(8,128)(2,1)}, u32[]{:S(2)}, u32[]{:S(2)}) collective-permute-start(bf16[128,4096]{1,0:T(8,128)(2,1)S(1)} %multiply_convert_fusion.adj_ref), channel_id=1, source_target_pairs={{1,0},{2,1},{3,2},{4,3},{5,4},{6,5},{7,6},{8,7},{9,8},{10,9},{11,1... | collective-permute-start | bytes 3145736 | tf_op jit(solution)/shard_map/ppermute | solution.py:48
  8.7 0.6 copy-start.18
  15.5 25.5 %collective-permute-start.1 = (bf16[128,4096]{1,0:T(8,128)(2,1)}, bf16[128,4096]{1,0:T(8,128)(2,1)}, u32[]{:S(2)}, u32[]{:S(2)}) collective-permute-start(bf16[128,4096]{1,0:T(8,128)(2,1)} %get-tuple-element.29.mixed_ref), channel_id=1, source_target_pairs={{0,1},{1,2},{2,3},{3,4},{4,5},{5,6},{6,7},{7,8},{8,9},{9,10},{10,1... | collective-permute-start | bytes 3145736 | tf_op jit(solution)/shard_map/ppermute | solution.py:48
  20.5 1.2 copy-start.11
  21.8 0.9 copy-start.15
  22.7 0.9 copy-start.16
  23.6 0.9 copy-start.17
  24.5 16.6 %copy-start.1 = (bf16[1,128,4096]{2,1,0:T(8,128)(2,1)S(1)}, bf16[1,128,4096]{2,1,0:T(8,128)(2,1)}, u32[]{:S(2)}) copy-start(bf16[1,128,4096]{2,1,0:T(8,128)(2,1)} %param.13) | copy-start | bytes 3145732
  24.5 16.6 %copy-start.4 = (bf16[1,128,4096]{2,1,0:T(8,128)(2,1)S(1)}, bf16[1,128,4096]{2,1,0:T(8,128)(2,1)}, u32[]{:S(2)}) copy-start(bf16[1,128,4096]{2,1,0:T(8,128)(2,1)} %param.14) | copy-start | bytes 3145732
  24.5 16.6 %copy-start.7 = (f32[128,4096]{1,0:T(8,128)S(1)}, f32[128,4096]{1,0:T(8,128)}, u32[]{:S(2)}) copy-start(f32[128,4096]{1,0:T(8,128)} %get-tuple-element.28.short_ref) | copy-start | bytes 6291460
  24.5 16.6 %copy-start.9 = (f32[7,4096]{1,0:T(8,128)S(1)}, f32[7,4096]{1,0:T(8,128)}, u32[]{:S(2)}) copy-start(f32[7,4096]{1,0:T(8,128)} %taps_ref.3) | copy-start | bytes 344068
  24.5 16.6 %copy-start.19 = (bf16[8,4096]{1,0:T(8,128)(2,1)S(1)}, bf16[8,4096]{1,0:T(8,128)(2,1)}, u32[]{:S(2)}) copy-start(bf16[8,4096]{1,0:T(8,128)(2,1)} %copy-done.18) | copy-start | bytes 196612
  32.3 1.3 %copy-start.5 = (f32[128,4096]{1,0:T(8,128)}, f32[128,4096]{1,0:T(8,128)S(1)}, u32[]{:S(2)}) copy-start(f32[128,4096]{1,0:T(8,128)S(1)} %get-tuple-element.36.long_ref) | copy-start | bytes 6291460
  51.3 1.0 copy-start.10
  51.3 1.8 %copy-start.12 = (bf16[128,4096]{1,0:T(8,128)(2,1)}, bf16[128,4096]{1,0:T(8,128)(2,1)S(1)}, u32[]{:S(2)}) copy-start(bf16[128,4096]{1,0:T(8,128)(2,1)S(1)} %get-tuple-element.43.adjs_ref) | copy-start | bytes 3145732
  51.3 1.8 %copy-start.21 = (bf16[8,4096]{1,0:T(8,128)(2,1)}, bf16[8,4096]{1,0:T(8,128)(2,1)S(1)}, u32[]{:S(2)}) copy-start(bf16[8,4096]{1,0:T(8,128)(2,1)S(1)} %get-tuple-element.44) | copy-start | bytes 196612
  51.3 17.1 %copy-start.2 = (bf16[1,128,4096]{2,1,0:T(8,128)(2,1)S(1)}, bf16[1,128,4096]{2,1,0:T(8,128)(2,1)}, u32[]{:S(2)}) copy-start(bf16[1,128,4096]{2,1,0:T(8,128)(2,1)} %param.15) | copy-start | bytes 3145732
  53.1 4.1 %collective-permute-start.3 = (bf16[16,136,128]{2,1,0:T(8,128)(2,1)}, bf16[16,136,128]{2,1,0:T(8,128)(2,1)}, u32[]{:S(2)}, u32[]{:S(2)}) collective-permute-start(bf16[16,136,128]{2,1,0:T(8,128)(2,1)} %dynamic-slice_bitcast_fusion), channel_id=1, source_target_pairs={{0,32},{32,0},{1,33},{33,1},{2,34},{34,2},{3,35},{35,3},{4,36},{36... | collective-permute-start | bytes 1671176 | tf_op jit(solution)/shard_map/ppermute | solution.py:342
  59.4 20.1 %all-to-all-start = ((bf16[16,1,136,128]{3,2,1,0:T(8,128)(2,1)}), bf16[16,1,136,128]{3,2,1,0:T(8,128)(2,1)}, u32[]{:S(2)}, u32[]{:S(2)}) async-start(bf16[16,1,136,128]{3,2,1,0:T(8,128)(2,1)} %bitcast.35), calls=%async_computation | async-start | bytes 1114112 | tf_op jit(solution)/shard_map/all_to_all | solution.py:330
  68.4 1.2 copy-start.3
  69.6 1.6 %copy-start.6 = (f32[128,4096]{1,0:T(8,128)S(1)}, f32[128,4096]{1,0:T(8,128)}, u32[]{:S(2)}) copy-start(f32[128,4096]{1,0:T(8,128)} %copy-done.5) | copy-start | bytes 6291460
  76.0 21.8 %copy-start.13 = (bf16[128,4096]{1,0:T(8,128)(2,1)S(1)}, bf16[128,4096]{1,0:T(8,128)(2,1)}, u32[]{:S(2)}) copy-start(bf16[128,4096]{1,0:T(8,128)(2,1)} %copy-done.12) | copy-start | bytes 3145732
  81.4 20.5 %all-to-all-start.1 = ((bf16[8,1,136,128]{3,2,1,0:T(8,128)(2,1)}), bf16[8,1,136,128]{3,2,1,0:T(8,128)(2,1)S(1)}, u32[]{:S(2)}, u32[]{:S(2)}) async-start(bf16[8,1,136,128]{3,2,1,0:T(8,128)(2,1)} %broadcast_in_dim.31), calls=%async_computation.1 | async-start | bytes 557056 | tf_op jit(solution)/shard_map/all_to_all | solution.py:330
  92.6 5.2 %collective-permute-start.4 = (bf16[8,4096]{1,0:T(8,128)(2,1)}, bf16[8,4096]{1,0:T(8,128)(2,1)S(1)}, u32[]{:S(2)}, u32[]{:S(2)}) collective-permute-start(bf16[8,4096]{1,0:T(8,128)(2,1)} %copy-done.21), channel_id=1, source_target_pairs={{1,0},{2,1},{3,2},{4,3},{5,4},{6,5},{7,6},{8,7},{9,8},{10,9},{11,1... | collective-permute-start | bytes 196616 | tf_op jit(solution)/shard_map/ppermute | solution.py:48
  118.7 4.5 %collective-permute-start.5 = (bf16[16,136,128]{2,1,0:T(8,128)(2,1)S(1)}, bf16[16,136,128]{2,1,0:T(8,128)(2,1)S(1)}, u32[]{:S(2)}, u32[]{:S(2)}) collective-permute-start(bf16[16,136,128]{2,1,0:T(8,128)(2,1)S(1)} %bitcast.31), channel_id=1, source_target_pairs={{0,32},{32,0},{1,33},{33,1},{2,34},{34,2},{3,35},{35,3},{4,36},{36... | collective-permute-start | bytes 1671176 | tf_op jit(solution)/shard_map/ppermute | solution.py:342

commit v3 on v2

--- a/solution.py
+++ b/solution.py
@@ -102,7 +102,7 @@
     pl.when(pl.program_id(0) == 0)(fill)
 
 
-def mix_kernel(lengths_ref, v_ref, before_ref, gs_ref, taps_ref, mixed_ref, short_ref, ext, reach_s):
+def mix_kernel(half_ref, lengths_ref, v_ref, before_ref, gs_ref, taps_ref, mixed_ref, short_ref, ext, reach_s):
     rows, columns = v_ref.shape
 
     @on_first_step
@@ -121,7 +121,7 @@
     mixed_ref[...] = (gs_ref[...].astype(F32) * total).astype(BF)
 
 
-def own_kernel(lengths_ref, mixed_ref, adj_ref, ltaps_ref, first_ref, second_ref, later_ref,
+def own_kernel(half_ref, lengths_ref, mixed_ref, adj_ref, ltaps_ref, first_ref, second_ref, later_ref,
                front_ref, totaps_ref, long_ref, back_ref, grads_ref, taps_spec, spec_acc, cuts_s):
     rows, columns = mixed_ref.shape
     cuts = cuts_of(lengths_ref, rows)
@@ -154,9 +154,9 @@
     grads_ref[...] = back_dot(totaps_ref[...], spec_acc[...].astype(BF))
 
 
-def grad_kernel(lengths_ref, v_ref, before_ref, gs_ref, adj_ref, short_ref, back_ref, own_grads_ref,
-                prev_ref, next_ref, staps_ref, ltaps_ref, first_ref, second_ref, front_ref, totaps_ref,
-                ggs_ref, adjs_ref, head_ref, grads_ref, ext, reach_s, masks_s):
+def grad_kernel(half_ref, lengths_ref, v_ref, before_ref, gs_ref, adj_ref, short_ref, back_ref, own_grads_ref,
+                prev_ref, next_ref, staps_ref, ltaps_ref, first_ref, second_ref, front_ref, totaps_ref, *rest):
+    ggs_ref, adjs_ref, head_ref, grads_ref, ext, reach_s, masks_s = rest[-7:]
     rows, columns = v_ref.shape
 
     @on_first_step
@@ -198,8 +198,8 @@
         grads_ref[k] = terms[:, k * LANES : (k + 1) * LANES]
 
 
-def long_kernel(lengths_ref, gl_ref, up_ref, long_ref, prev_ref, ltaps_ref, first_ref, later_ref,
-                out_ref, ggl_ref, masks_s):
+def long_kernel(half_ref, lengths_ref, gl_ref, up_ref, long_ref, prev_ref, ltaps_ref, first_ref, later_ref, *rest):
+    out_ref, ggl_ref, masks_s = rest[-3:]
     rows, columns = gl_ref.shape
 
     @on_first_step
@@ -256,74 +256,108 @@
     pl.when(jnp.logical_not(own_turn))(lambda: write(other_ref))
 
 
-def kernels(rows, channels, count):
-    shaped = lambda r, t: jax.ShapeDtypeStruct((r, channels), t)
-    first, second, later, front, totaps = [jnp.asarray(m) for m in spectra(rows)]
-    parts = channels // LANES
-
-    def call(kernel, parts_per_step, ins, outs, scratch, cost, arrays, mib):
-        columns = parts_per_step * LANES
-
-        def spec(shape):
-            if shape is None:
+class Kernels:
+
+    def __init__(self, rows, channels, count):
+        self.rows, self.channels, self.count = rows, channels, count
+        self.parts = channels // LANES
+        self.tables = [jnp.asarray(m) for m in spectra(rows)]
+
+    def call(self, kernel, step_parts, half, ins, outs, scratch, cost, mib, filled=()):
+        columns = step_parts * LANES
+        steps = self.parts // step_parts
+        if half is not None:
+            steps //= 2
+
+        def spec(kind, shape):
+            if kind == "scalars":
                 return pl.BlockSpec(memory_space=pltpu.SMEM)
-            if isinstance(shape, int):
-                return pl.BlockSpec((shape, columns), lambda i: (0, i))
-            if len(shape) == 2 and shape[1] == LANES:
-                return pl.BlockSpec((parts // 2,) + shape, lambda i: (0, 0, 0))
-            if len(shape) == 3:
-                return pl.BlockSpec((parts_per_step,) + shape[1:], lambda i: (i, 0, 0))
-            return pl.BlockSpec(shape, lambda i: (0, 0))
-
+            if kind == "table":
+                return pl.BlockSpec(shape, lambda i, *h: (0,) * len(shape))
+            if kind == "shares":
+                return pl.BlockSpec((step_parts,) + shape[1:], lambda i, *h: (i, 0, 0))
+            if kind == "whole" and half is not None:
+                return pl.BlockSpec((shape[0], columns), lambda i, h: (0, h[0] * steps + i))
+            return pl.BlockSpec((shape[0], columns), lambda i, *h: (0, i))
+
+        prefetch = 0 if half is None else 1
+        arrays = ([] if half is None else [half]) + [a for _, a in ins] + list(filled)
+        in_specs = [spec(k, a.shape) for k, a in ins] + [pl.BlockSpec(memory_space=pl.ANY)] * len(filled)
         return pl.pallas_call(
             kernel,
-            grid=(parts // parts_per_step,),
-            in_specs=[spec(i) for i in ins],
-            out_specs=[spec(o.shape[0] if len(o.shape) == 2 else o.shape) for o in outs],
-            out_shape=outs,
-            scratch_shapes=[pltpu.VMEM((r, c if c else columns), t) if r else t for r, c, t in scratch],
+            grid_spec=pltpu.PrefetchScalarGridSpec(
+                num_scalar_prefetch=prefetch,
+                grid=(steps,),
+                in_specs=in_specs,
+                out_specs=[spec(k, o.shape) for k, o in outs],
+                scratch_shapes=[pltpu.VMEM((r, c if c else columns), t) if r else t for r, c, t in scratch],
+            ),
+            out_shape=[o for _, o in outs],
+            input_output_aliases={prefetch + len(ins) + k: k for k in range(len(filled))},
             compiler_params=pltpu.CompilerParams(vmem_limit_bytes=mib << 20),
             cost_estimate=pl.CostEstimate(
                 flops=0, bytes_accessed=int(cost * 3.5e6), transcendentals=0),
         )(*arrays)
 
-    small = min(8, parts // 2)
-    large = min(16, parts // 2)
-    ext = (rows + RIM, 0, F32)
-    spectrum = (2 * rows, 0, F32)
-    tables = lambda *chosen: [t.shape for t in chosen]
-    grads_shape = jax.ShapeDtypeStruct((parts, rows + RIM, LANES), BF)
-
-    def mix(*arrays):
-        return call(mix_kernel, small, [None, rows, RIM, rows, count],
-                    [shaped(rows, BF), shaped(rows, F32)], [ext, (rows, LANES, jnp.int32)], 6, arrays, 56)
-
-    def own(*arrays):
-        used = (first, second, later, front, totaps)
-        return call(own_kernel, large, [None, rows, rows, rows] + tables(*used),
-                    [shaped(rows, F32)] * 3,
-                    [spectrum, spectrum, (0, 0, pltpu.SMEM((16,), jnp.int32))], 15, arrays + used, 40)
-
-    def grad(*arrays):
-        used = (first, second, front, totaps)
-        return call(grad_kernel, small, [None, rows, RIM] + [rows] * 7 + [count, rows] + tables(*used),
-                    [shaped(rows, BF), shaped(rows, BF), shaped(RIM, BF), grads_shape],
-                    [ext, (rows, LANES, jnp.int32), (4 * rows, LANES, BF)], 12, arrays + used, 30)
-
-    def long(*arrays):
-        used = (first, later)
-        return call(long_kernel, large, [None] + [rows] * 5 + tables(*used),
-                    [shaped(rows, BF)] * 2, [(2 * rows, LANES, BF)], 6, arrays + used, 32)
-
-    def values_grad(*arrays):
-        return call(values_kernel, large, [None, rows, RIM, count], [shaped(rows, BF)],
-                    [(count * rows, 2 * LANES, BF)], 4, arrays, 24)[0]
-
-    def spread(mine, other):
-        return call(spread_kernel, parts // 2, [mine.shape[1:], other.shape[1:]],
-                    [shaped(count, F32), shaped(rows, F32)], [], 3, (mine, other), 24)
-
-    return mix, own, grad, long, values_grad, spread
+    def shaped(self, rows, kind):
+        width = self.channels // 2 if kind == "half" else self.channels
+        return lambda t: (kind, jax.ShapeDtypeStruct((rows, width), t))
+
+    def small(self):
+        return min(8, self.parts // 4)
+
+    def mix(self, half, lengths, v, before, gs, staps):
+        out = self.shaped(self.rows, "half")
+        return self.call(
+            mix_kernel, self.small(), half,
+            [("scalars", lengths), ("whole", v), ("whole", before), ("whole", gs), ("whole", staps)],
+            [out(BF), out(F32)],
+            [(self.rows + RIM, 0, F32), (self.rows, LANES, jnp.int32)], 3, 20)
+
+    def own(self, half, lengths, mixed, adj, ltaps):
+        out = self.shaped(self.rows, "half")
+        spectrum = (2 * self.rows, 0, F32)
+        return self.call(
+            own_kernel, self.small(), half,
+            [("scalars", lengths), ("half", mixed), ("whole", adj), ("whole", ltaps)]
+            + [("table", t) for t in self.tables],
+            [out(F32)] * 3,
+            [spectrum, spectrum, (0, 0, pltpu.SMEM((16,), jnp.int32))], 1.5, 28)
+
+    def grad(self, half, lengths, v, before, gs, adj, short, back, own_grads, prev, following,
+             staps, ltaps, filled):
+        first, second, _, front, totaps = self.tables
+        rows = self.rows
+        out = self.shaped(rows, "whole")
+        grads = jax.ShapeDtypeStruct((self.parts // 2, rows + RIM, LANES), BF)
+        return self.call(
+            grad_kernel, self.small(), half,
+            [("scalars", lengths), ("whole", v), ("whole", before), ("whole", gs), ("whole", adj),
+             ("half", short), ("half", back), ("half", own_grads), ("half", prev),
+             ("whole", following), ("whole", staps), ("whole", ltaps)]
+            + [("table", t) for t in (first, second, front, totaps)],
+            [out(BF), out(BF), self.shaped(RIM, "whole")(BF), ("shares", grads)],
+            [(rows + RIM, 0, F32), (rows, LANES, jnp.int32), (4 * rows, LANES, BF)], 1.5, 28, filled)
+
+    def long(self, half, lengths, gl, up, own_long, prev, ltaps, filled):
+        out = self.shaped(self.rows, "whole")
+        return self.call(
+            long_kernel, self.small(), half,
+            [("scalars", lengths), ("whole", gl), ("whole", up), ("half", own_long), ("half", prev),
+             ("whole", ltaps), ("table", self.tables[0]), ("table", self.tables[2])],
+            [out(BF)] * 2, [(2 * self.rows, LANES, BF)], 3, 24, filled)
+
+    def values_grad(self, lengths, adjs, after, staps):
+        return self.call(
+            values_kernel, 2 * self.small(), None,
+            [("scalars", lengths), ("whole", adjs), ("whole", after), ("whole", staps)],
+            [self.shaped(self.rows, "whole")(BF)],
+            [(self.count * self.rows, 2 * LANES, BF)], 4, 24)[0]
+
+    def spread(self, mine, other):
+        return self.call(
+            spread_kernel, self.parts // 2, None, [("table", mine), ("table", other)],
+            [self.shaped(self.count, "whole")(F32), self.shaped(self.rows, "whole")(F32)], [], 3, 24)
 
 
 def traded(block, axes):
@@ -345,34 +379,47 @@
 def on_device(lengths, values, gate_short, gate_long, short_taps, long_taps, cotangent):
     v, gs, gl, up = values[0], gate_short[0], gate_long[0], cotangent[0]
     rows, channels = v.shape
-    mix, own, grad, long, values_grad, spread = kernels(rows, channels, short_taps.shape[0])
+    k = Kernels(rows, channels, short_taps.shape[0])
     factor = 1.0 / math.sqrt(lax.axis_size(("y", "core", "z", "x")) * rows)
+    together = lax.optimization_barrier
+
+    core = lax.axis_index("core").astype(jnp.int32)
+    kept = core[None]
+    given = 1 - kept
 
     before = passed_along(v[rows - RIM :], 1)
     adj = (up.astype(F32) * gl.astype(F32)).astype(BF)
     following = passed_along(adj, -1)
-    mixed, short = mix(lengths, v, before, gs, short_taps)
-    prev = passed_along(mixed, 1)
-    own_long, own_back, own_grads = own(lengths, mixed, adj, long_taps)
-    ggs, adjs, head, grads = grad(lengths, v, before, gs, adj, short, own_back, own_grads,
-                                  prev, following, short_taps, long_taps)
-    after = passed_along(head, -1)
-
-    core = lax.axis_index("core")
+    mixed_a, short_a = k.mix(given, lengths, v, before, gs, short_taps)
+    prev_a = passed_along(mixed_a, 1)
+    mixed_b, short_b = k.mix(kept, lengths, v, before, gs, short_taps)
+    long_a, back_a, terms_a = k.own(given, lengths, mixed_a, adj, long_taps)
+    mixed_b, back_a = together((mixed_b, back_a))
+    prev_b = passed_along(mixed_b, 1)
+    long_b, back_b, terms_b = k.own(kept, lengths, mixed_b, adj, long_taps)
+    prev_a, back_b = together((prev_a, back_b))
+    ggs, adjs, head, grads_a = k.grad(given, lengths, v, before, gs, adj, short_a, back_a, terms_a,
+                                      prev_a, following, short_taps, long_taps, ())
+    grads_a, prev_b = together((grads_a, prev_b))
+    got = swapped(grads_a)
+    ggs, adjs, head, grads_b = k.grad(kept, lengths, v, before, gs, adj, short_b, back_b, terms_b,
+                                      prev_b, following, short_taps, long_taps, (ggs, adjs, head))
+
     planes = ("y", "x")
-    split = grads.reshape((2, grads.shape[0] // 2) + grads.shape[1:])
-    pick = lambda i: lax.dynamic_index_in_dim(split, i, 0, keepdims=False)
-    half = (pick(core).astype(F32) + swapped(pick(1 - core)).astype(F32)).astype(BF)
-    half, own_long, adjs = lax.optimization_barrier((half, own_long, adjs))
+    half = (grads_b.astype(F32) + got.astype(F32)).astype(BF)
+    half, long_a, adjs, head = together((half, long_a, adjs, head))
     share = half.reshape((lax.axis_size(planes), -1) + half.shape[1:])
     share = added(traded(share, planes)).astype(BF)
-    out, ggl = long(lengths, gl, up, own_long, prev, long_taps)
-    share, out, ggl, adjs = lax.optimization_barrier((share, out, ggl, adjs))
+    out_ggl = k.long(given, lengths, gl, up, long_a, prev_a, long_taps, ())
+    out, ggl = k.long(kept, lengths, gl, up, long_b, prev_b, long_taps, tuple(out_ggl))
+    share, out, ggl, adjs, head = together((share, out, ggl, adjs, head))
+    after = passed_along(head, -1)
     share = (added(copies(share, "z")) * factor).astype(BF)
-    gv = values_grad(lengths, adjs, after, short_taps)
-    share, gv = lax.optimization_barrier((share, gv))
+    share, after, adjs = together((share, after, adjs))
     mine = copies(share, planes).reshape(half.shape)
-    grad_short, grad_long = spread(mine, swapped(mine))
+    gv = k.values_grad(lengths, adjs, after, short_taps)
+    mine, gv = together((mine, gv))
+    grad_short, grad_long = k.spread(mine, swapped(mine))
     return out[None], ggs[None], gv[None], ggl[None], grad_short, grad_long
 
 

time: 126 us -> 126 us (level)
  blocking collectives: 16.7 us -> 0 us
  starting transfers between devices: 36.9 us -> 50.8 us
  Pallas kernels: 34.3 us -> 38.8 us
  local copies, waits for them, and re-layouts: 12.2 us -> 10.1 us
  waiting for transfers between devices: 18.7 us -> 20 us
    all_to_all x1 -> x0, blocking collectives: 16.7 us -> none  [traded(): return lax.all_to_all(block, axes, 0, 0, tiled=True)]
    all_to_all x2 -> x3, waiting for transfers between devices: 3.9 us -> 17.4 us  [traded(): return lax.all_to_all(block, axes, 0, 0, tiled=True)]
    ppermute x4 -> x5, waiting for transfers between devices: 11.3 us -> 1.03 us  [passed_along(): return lax.ppermute(block, CTX, route)]
    all_to_all x2 -> x3, starting transfers between devices: 20.2 us -> 30.3 us  [traded(): return lax.all_to_all(block, axes, 0, 0, tiled=True)]
    pallas_call x6 -> x10, Pallas kernels: 34.3 us -> 38.8 us  [call(): pl.pallas_call(kernel, grid_spec=pltpu.PrefetchScalarGridSpec(num_scalar_...]
    ppermute x4 -> x5, starting transfers between devices: 11.6 us -> 15.3 us  [passed_along(): return lax.ppermute(block, CTX, route)]
    unnamed x44 -> x54, local copies, waits for them, and re-layouts: 9.73 us -> 7 us
    ppermute x2, waiting for transfers between devices: 3.51 us -> 1.59 us  [swapped(): return lax.ppermute(block, 'core', [(0, 1), (1, 0)])]
  transfers between devices with their start and end apart: 8 -> 10, of which waited for: 6 -> 5; matrix products, arithmetic and copies ran while one was open for 1% -> 1% of each run, Pallas kernels for 18% -> 30%
where the time goes in v3:
time: 126 us; the launch traced here: 125 us
  starting transfers between devices  50.8 us (40%)
  Pallas kernels  38.8 us (31%)
  waiting for transfers between devices  20 us (16%)
  local copies, waits for them, and re-layouts  10.1 us (8%)
  other arithmetic  4.14 us (3%)
    pallas_call x10, Pallas kernels, call(): pl.pallas_call(kernel, grid_spec=pltpu.PrefetchScalarGridSpec(num_scalar_...  38.8 us
    all_to_all x3, starting transfers between devices, traded(): return lax.all_to_all(block, axes, 0, 0, tiled=True)  30.3 us
    all_to_all x3, waiting for transfers between devices, traded(): return lax.all_to_all(block, axes, 0, 0, tiled=True)  17.4 us
    ppermute x5, starting transfers between devices, passed_along(): return lax.ppermute(block, CTX, route)  15.3 us
    unnamed x54, local copies, waits for them, and re-layouts  7 us
    ppermute x2, starting transfers between devices, swapped(): return lax.ppermute(block, 'core', [(0, 1), (1, 0)])  5.22 us
  transfers between devices with their start and end apart: 10, of which 5 were waited for; matrix products, arithmetic and copies ran while one was open for 1% of the time, Pallas kernels for 30%

profile of v3, /device:TPU:1, one launch (start us, length us, event | category | flops | bytes accessed | tf_op | source)
XLA Modules:
  0.0 124.8 jit_solution(12917002320326812115)
XLA Ops:
  0.7 1.9 %multiply_convert_fusion.adj_ref = bf16[128,4096]{1,0:T(8,128)(2,1)S(1)} fusion(bf16[1,128,4096]{2,1,0:T(8,128)(2,1)} %param.15, bf16[1,128,4096]{2,1,0:T(8,128)(2,1)} %param.18), kind=kLoop, calls=%fused_computation | loop fusion | flops 2097152 | bytes 3145728 | tf_op jit(solution)/shard_map/convert_element_type | solution.py:391
  2.6 1.3 %collective-permute-start.2 = (bf16[128,4096]{1,0:T(8,128)(2,1)S(1)}, bf16[128,4096]{1,0:T(8,128)(2,1)}, u32[]{:S(2)}, u32[]{:S(2)}) collective-permute-start(bf16[128,4096]{1,0:T(8,128)(2,1)S(1)} %multiply_convert_fusion.adj_ref), channel_id=1, source_target_pairs={{1,0},{2,1},{3,2},{4,3},{5,4},{6,5},{7,6},{8,7},{9,8},{10,9},{11,1... | collective-permute-start | bytes 3145736 | tf_op jit(solution)/shard_map/ppermute | solution.py:48
  3.9 1.5 %slice_bitcast_fusion = bf16[8,4096]{1,0:T(8,128)(2,1)} fusion(bf16[1,128,4096]{2,1,0:T(8,128)(2,1)} %param.13), kind=kLoop, calls=%fused_computation.4 | loop fusion | bytes 131072 | tf_op jit(solution)/shard_map/slice | solution.py:390
  5.4 5.2 %collective-permute-start = (bf16[8,4096]{1,0:T(8,128)(2,1)}, bf16[8,4096]{1,0:T(8,128)(2,1)}, u32[]{:S(2)}, u32[]{:S(2)}) collective-permute-start(bf16[8,4096]{1,0:T(8,128)(2,1)} %slice_bitcast_fusion), channel_id=1, source_target_pairs={{0,1},{1,2},{2,3},{3,4},{4,5},{5,6},{6,7},{7,8},{8,9},{9,10},{10,1... | collective-permute-start | bytes 196616 | tf_op jit(solution)/shard_map/ppermute | solution.py:48
  11.6 1.2 copy-done.1
  12.8 1.2 copy-done.3
  14.1 3.0 %shard_map.164 = (bf16[128,2048]{1,0:T(8,128)(2,1)S(1)}, f32[128,2048]{1,0:T(8,128)S(1)}) custom-call(s32[1]{0:T(128)S(6)} %sub.3.half_ref, s32[1,8]{1,0:T(1,128)S(1)} %copy-done.26, bf16[128,4096]{1,0:T(8,128)(2,1)S(1)} %bitcast.22, bf16[8,4096]{1,0:T(8,128)(2,1)} %collective-permute-done.before_ref, bf16[128,4096]{1,0:T(8,128)(2,1)S(1)} %bitcast.26, ...), custom_call_target="tpu_custom_call" | custom-call | bytes 10500000 | tf_op jit(solution)/shard_map/pallas_call | solution.py:286
  17.1 4.1 %collective-permute-start.1 = (bf16[128,2048]{1,0:T(8,128)(2,1)S(1)}, bf16[128,2048]{1,0:T(8,128)(2,1)S(1)}, u32[]{:S(2)}, u32[]{:S(2)}) collective-permute-start(bf16[128,2048]{1,0:T(8,128)(2,1)S(1)} %get-tuple-element.51.mixed_ref), channel_id=1, source_target_pairs={{0,1},{1,2},{2,3},{3,4},{4,5},{5,6},{6,7},{7,8},{8,9},{9,10},{10,1... | collective-permute-start | bytes 1572872 | tf_op jit(solution)/shard_map/ppermute | solution.py:48
  21.3 4.8 %shard_map.165 = (f32[128,2048]{1,0:T(8,128)S(1)}, f32[128,2048]{1,0:T(8,128)S(1)}, f32[128,2048]{1,0:T(8,128)S(1)}) custom-call(s32[1]{0:T(128)S(6)} %sub.3.half_ref, s32[1,8]{1,0:T(1,128)S(1)} %copy-done.26, bf16[128,2048]{1,0:T(8,128)(2,1)S(1)} %get-tuple-element.51.mixed_ref, bf16[128,4096]{1,0:T(8,128)(2,1)S(1)} %multiply_convert_fusion.adj_ref, ...), custom_call_target="tpu_custom_call" | custom-call | bytes 5250000 | tf_op jit(solution)/shard_map/pallas_call | solution.py:286
  26.2 3.0 %shard_map.163 = (bf16[128,2048]{1,0:T(8,128)(2,1)S(1)}, f32[128,2048]{1,0:T(8,128)S(1)}) custom-call(s32[1]{0:T(128)} %bitcast.half_ref, s32[1,8]{1,0:T(1,128)S(1)} %copy-done.26, bf16[128,4096]{1,0:T(8,128)(2,1)S(1)} %bitcast.23, bf16[8,4096]{1,0:T(8,128)(2,1)} %collective-permute-done.before_ref, bf16[128,4096]{1,0:T(8,128)(2,1)S(1)} %bitcast.27, ...), custom_call_target="tpu_custom_call" | custom-call | bytes 10500000 | tf_op jit(solution)/shard_map/pallas_call | solution.py:286
  29.2 3.4 %collective-permute-start.3 = (bf16[128,2048]{1,0:T(8,128)(2,1)S(1)}, bf16[128,2048]{1,0:T(8,128)(2,1)S(1)}, u32[]{:S(2)}, u32[]{:S(2)}) collective-permute-start(bf16[128,2048]{1,0:T(8,128)(2,1)S(1)} %get-tuple-element.54.mixed_ref), channel_id=1, source_target_pairs={{0,1},{1,2},{2,3},{3,4},{4,5},{5,6},{6,7},{7,8},{8,9},{9,10},{10,1... | collective-permute-start | bytes 1572872 | tf_op jit(solution)/shard_map/ppermute | solution.py:48
  32.5 4.8 %shard_map.166 = (f32[128,2048]{1,0:T(8,128)S(1)}, f32[128,2048]{1,0:T(8,128)S(1)}, f32[128,2048]{1,0:T(8,128)S(1)}) custom-call(s32[1]{0:T(128)} %bitcast.half_ref, s32[1,8]{1,0:T(1,128)S(1)} %copy-done.26, bf16[128,2048]{1,0:T(8,128)(2,1)S(1)} %get-tuple-element.54.mixed_ref, bf16[128,4096]{1,0:T(8,128)(2,1)S(1)} %multiply_convert_fusion.adj_ref, ...), custom_call_target="tpu_custom_call" | custom-call | bytes 5250000 | tf_op jit(solution)/shard_map/pallas_call | solution.py:286
  37.4 5.9 %shard_map.167 = (bf16[128,4096]{1,0:T(8,128)(2,1)}, bf16[128,4096]{1,0:T(8,128)(2,1)S(1)}, bf16[8,4096]{1,0:T(8,128)(2,1)S(1)}, bf16[16,136,128]{2,1,0:T(8,128)(2,1)S(1)}) custom-call(s32[1]{0:T(128)S(6)} %sub.3.half_ref, s32[1,8]{1,0:T(1,128)S(1)} %copy-done.26, bf16[128,4096]{1,0:T(8,128)(2,1)S(1)} %bitcast.24, ...), custom_call_target="tpu_custom_call" | custom-call | bytes 5250000 | tf_op jit(solution)/shard_map/pallas_call | solution.py:286
  43.4 2.9 %collective-permute-start.4 = (bf16[16,136,128]{2,1,0:T(8,128)(2,1)S(1)}, bf16[16,136,128]{2,1,0:T(8,128)(2,1)S(1)}, u32[]{:S(2)}, u32[]{:S(2)}) collective-permute-start(bf16[16,136,128]{2,1,0:T(8,128)(2,1)S(1)} %get-tuple-element.68), channel_id=1, source_target_pairs={{0,32},{32,0},{1,33},{33,1},{2,34},{34,2},{3,35},{35,3},{4,36},{36... | collective-permute-start | bytes 1671176 | tf_op jit(solution)/shard_map/ppermute | solution.py:376
  46.3 5.7 %shard_map.168 = (bf16[128,4096]{1,0:T(8,128)(2,1)}, bf16[128,4096]{1,0:T(8,128)(2,1)S(1)}, bf16[8,4096]{1,0:T(8,128)(2,1)S(1)}, bf16[16,136,128]{2,1,0:T(8,128)(2,1)S(1)}) custom-call(s32[1]{0:T(128)} %bitcast.half_ref, s32[1,8]{1,0:T(1,128)S(1)} %copy-done.26, ...), custom_call_target="tpu_custom_call", output_to_operand_aliasing={{0}: (17, {}), {1}: (18, {}), {2}: (19, {})} | custom-call | bytes 5250000 | tf_op jit(solution)/shard_map/pallas_call | solution.py:286
  54.0 12.9 %all-to-all-start = ((bf16[16,1,136,128]{3,2,1,0:T(8,128)(2,1)}), bf16[16,1,136,128]{3,2,1,0:T(8,128)(2,1)}, u32[]{:S(2)}, u32[]{:S(2)}) async-start(bf16[16,1,136,128]{3,2,1,0:T(8,128)(2,1)} %bitcast.36), calls=%async_computation | async-start | bytes 1114112 | tf_op jit(solution)/shard_map/all_to_all | solution.py:364
  66.9 1.2 copy-done.6
  68.1 1.0 copy-done.18
  69.2 1.2 copy-done.22
  70.4 3.1 %shard_map.169 = (bf16[128,4096]{1,0:T(8,128)(2,1)}, bf16[128,4096]{1,0:T(8,128)(2,1)}) custom-call(s32[1]{0:T(128)S(6)} %sub.3.half_ref, s32[1,8]{1,0:T(1,128)S(1)} %copy-done.26, bf16[128,4096]{1,0:T(8,128)(2,1)S(1)} %bitcast.30, bf16[128,4096]{1,0:T(8,128)(2,1)S(1)} %bitcast.32, f32[128,2048]{1,0:T(8,128)S(1)} %copy-done.22, ...), custom_call_target="tpu_custom_call" | custom-call | bytes 10500000 | tf_op jit(solution)/shard_map/pallas_call | solution.py:286
  73.5 3.1 %shard_map.170 = (bf16[128,4096]{1,0:T(8,128)(2,1)}, bf16[128,4096]{1,0:T(8,128)(2,1)}) custom-call(s32[1]{0:T(128)} %bitcast.half_ref, s32[1,8]{1,0:T(1,128)S(1)} %copy-done.26, bf16[128,4096]{1,0:T(8,128)(2,1)S(1)} %bitcast.31, bf16[128,4096]{1,0:T(8,128)(2,1)S(1)} %bitcast.33, ...), custom_call_target="tpu_custom_call", output_to_operand_aliasing={{0}: (9, {}), {1}: (10, {})} | custom-call | bytes 10500000 | tf_op jit(solution)/shard_map/pallas_call | solution.py:286
  76.7 1.6 %all-to-all-done = bf16[16,1,136,128]{3,2,1,0:T(8,128)(2,1)} async-done(((bf16[16,1,136,128]{3,2,1,0:T(8,128)(2,1)}), bf16[16,1,136,128]{3,2,1,0:T(8,128)(2,1)}, u32[]{:S(2)}, u32[]{:S(2)}) %all-to-all-start) | async-done | bytes 557088 | tf_op jit(solution)/shard_map/all_to_all | solution.py:364
  78.3 1.1 reduce_sum.23
  80.1 11.0 %all-to-all-start.1 = ((bf16[8,1,136,128]{3,2,1,0:T(8,128)(2,1)}), bf16[8,1,136,128]{3,2,1,0:T(8,128)(2,1)S(1)}, u32[]{:S(2)}, u32[]{:S(2)}) async-start(bf16[8,1,136,128]{3,2,1,0:T(8,128)(2,1)} %broadcast_in_dim.35), calls=%async_computation.1 | async-start | bytes 557056 | tf_op jit(solution)/shard_map/all_to_all | solution.py:364
  91.2 1.3 %collective-permute-start.5 = (bf16[8,4096]{1,0:T(8,128)(2,1)}, bf16[8,4096]{1,0:T(8,128)(2,1)S(1)}, u32[]{:S(2)}, u32[]{:S(2)}) collective-permute-start(bf16[8,4096]{1,0:T(8,128)(2,1)} %copy-done.25), channel_id=1, source_target_pairs={{1,0},{2,1},{3,2},{4,3},{5,4},{6,5},{7,6},{8,7},{9,8},{10,9},{11,1... | collective-permute-start | bytes 196616 | tf_op jit(solution)/shard_map/ppermute | solution.py:48
  92.5 9.1 %all-to-all-done.1 = bf16[8,1,136,128]{3,2,1,0:T(8,128)(2,1)S(1)} async-done(((bf16[8,1,136,128]{3,2,1,0:T(8,128)(2,1)}), bf16[8,1,136,128]{3,2,1,0:T(8,128)(2,1)S(1)}, u32[]{:S(2)}, u32[]{:S(2)}) %all-to-all-start.1) | async-done | bytes 278560 | tf_op jit(solution)/shard_map/all_to_all | solution.py:364
  102.5 6.4 %all-to-all-start.2 = ((bf16[16,1,136,128]{3,2,1,0:T(8,128)(2,1)}), bf16[16,1,136,128]{3,2,1,0:T(8,128)(2,1)S(1)}, u32[]{:S(2)}, u32[]{:S(2)}) async-start(bf16[16,1,136,128]{3,2,1,0:T(8,128)(2,1)} %broadcast_in_dim.37), calls=%async_computation.2 | async-start | bytes 1114112 | tf_op jit(solution)/shard_map/all_to_all | solution.py:364
  108.9 3.8 %shard_map.171 = bf16[128,4096]{1,0:T(8,128)(2,1)} custom-call(s32[1,8]{1,0:T(1,128)S(1)} %copy-done.26, bf16[128,4096]{1,0:T(8,128)(2,1)S(1)} %copy-done.10, bf16[8,4096]{1,0:T(8,128)(2,1)S(1)} %collective-permute-done.5.after_ref, f32[7,4096]{1,0:T(8,128)S(1)} %copy-done.11), custom_call_target="tpu_custom_call" | custom-call | bytes 14000000 | tf_op jit(solution)/shard_map/pallas_call | solution.py:286
  112.7 6.7 %all-to-all-done.2 = bf16[16,1,136,128]{3,2,1,0:T(8,128)(2,1)S(1)} async-done(((bf16[16,1,136,128]{3,2,1,0:T(8,128)(2,1)}), bf16[16,1,136,128]{3,2,1,0:T(8,128)(2,1)S(1)}, u32[]{:S(2)}, u32[]{:S(2)}) %all-to-all-start.2) | async-done | bytes 557088 | tf_op jit(solution)/shard_map/all_to_all | solution.py:364
  119.4 2.3 %collective-permute-start.6 = (bf16[16,136,128]{2,1,0:T(8,128)(2,1)S(1)}, bf16[16,136,128]{2,1,0:T(8,128)(2,1)S(1)}, u32[]{:S(2)}, u32[]{:S(2)}) collective-permute-start(bf16[16,136,128]{2,1,0:T(8,128)(2,1)S(1)} %bitcast.34), channel_id=1, source_target_pairs={{0,32},{32,0},{1,33},{33,1},{2,34},{34,2},{3,35},{35,3},{4,36},{36... | collective-permute-start | bytes 1671176 | tf_op jit(solution)/shard_map/ppermute | solution.py:376
  121.7 1.6 %collective-permute-done.6.other_ref = bf16[16,136,128]{2,1,0:T(8,128)(2,1)S(1)} collective-permute-done((bf16[16,136,128]{2,1,0:T(8,128)(2,1)S(1)}, bf16[16,136,128]{2,1,0:T(8,128)(2,1)S(1)}, u32[]{:S(2)}, u32[]{:S(2)}) %collective-permute-start.6) | collective-permute-done | bytes 557088 | tf_op jit(solution)/shard_map/ppermute | solution.py:376
  123.3 1.5 %shard_map.172 = (f32[7,4096]{1,0:T(8,128)}, f32[128,4096]{1,0:T(8,128)}) custom-call(bf16[16,136,128]{2,1,0:T(8,128)(2,1)S(1)} %bitcast.35, bf16[16,136,128]{2,1,0:T(8,128)(2,1)S(1)} %collective-permute-done.6.other_ref), custom_call_target="tpu_custom_call" | custom-call | bytes 10500000 | tf_op jit(solution)/shard_map/pallas_call | solution.py:286
  (60 shorter events, 4.8 us)
Async XLA Ops:
  0.6 20.6 %copy-start.8 = (bf16[256,256]{1,0:T(8,128)(2,1)S(1)}, bf16[256,256]{1,0:T(8,128)(2,1)}, u32[]{:S(2)}) copy-start(bf16[256,256]{1,0:T(8,128)(2,1)} %constant.24.clone.first_ref) | copy-start | bytes 393220
  0.6 20.6 %copy-start.12 = (bf16[256,256]{1,0:T(8,128)(2,1)S(1)}, bf16[256,256]{1,0:T(8,128)(2,1)}, u32[]{:S(2)}) copy-start(bf16[256,256]{1,0:T(8,128)(2,1)} %constant.28.clone.totaps_ref) | copy-start | bytes 393220
  0.7 11.0 %copy-start.26 = (s32[1,8]{1,0:T(1,128)S(1)}, s32[1,8]{1,0:T(1,128)}, u32[]{:S(2)}) copy-start(s32[1,8]{1,0:T(1,128)} %lengths_ref.17) | copy-start | bytes 100
  0.7 10.9 %copy-start.11 = (f32[7,4096]{1,0:T(8,128)S(1)}, f32[7,4096]{1,0:T(8,128)}, u32[]{:S(2)}) copy-start(f32[7,4096]{1,0:T(8,128)} %taps_ref.5) | copy-start | bytes 344068
  0.7 20.6 %copy-start = (f32[128,4096]{1,0:T(8,128)S(1)}, f32[128,4096]{1,0:T(8,128)}, u32[]{:S(2)}) copy-start(f32[128,4096]{1,0:T(8,128)} %ltaps_ref.11) | copy-start | bytes 6291460
  2.6 34.8 %collective-permute-start.2 = (bf16[128,4096]{1,0:T(8,128)(2,1)S(1)}, bf16[128,4096]{1,0:T(8,128)(2,1)}, u32[]{:S(2)}, u32[]{:S(2)}) collective-permute-start(bf16[128,4096]{1,0:T(8,128)(2,1)S(1)} %multiply_convert_fusion.adj_ref), channel_id=1, source_target_pairs={{1,0},{2,1},{3,2},{4,3},{5,4},{6,5},{7,6},{8,7},{9,8},{10,9},{11,1... | collective-permute-start | bytes 3145736 | tf_op jit(solution)/shard_map/ppermute | solution.py:48
  5.4 6.2 %collective-permute-start = (bf16[8,4096]{1,0:T(8,128)(2,1)}, bf16[8,4096]{1,0:T(8,128)(2,1)}, u32[]{:S(2)}, u32[]{:S(2)}) collective-permute-start(bf16[8,4096]{1,0:T(8,128)(2,1)} %slice_bitcast_fusion), channel_id=1, source_target_pairs={{0,1},{1,2},{2,3},{3,4},{4,5},{5,6},{6,7},{7,8},{8,9},{9,10},{10,1... | collective-permute-start | bytes 196616 | tf_op jit(solution)/shard_map/ppermute | solution.py:48
  11.6 1.2 copy-start.1
  14.1 7.2 %copy-start.13 = (bf16[256,256]{1,0:T(8,128)(2,1)S(1)}, bf16[256,256]{1,0:T(8,128)(2,1)}, u32[]{:S(2)}) copy-start(bf16[256,256]{1,0:T(8,128)(2,1)} %constant.27.clone.front_ref) | copy-start | bytes 393220
  14.1 7.2 %copy-start.14 = (bf16[256,256]{1,0:T(8,128)(2,1)S(1)}, bf16[256,256]{1,0:T(8,128)(2,1)}, u32[]{:S(2)}) copy-start(bf16[256,256]{1,0:T(8,128)(2,1)} %constant.25.clone.second_ref) | copy-start | bytes 393220
  14.1 7.3 %copy-start.15 = (bf16[256,256]{1,0:T(8,128)(2,1)S(1)}, bf16[256,256]{1,0:T(8,128)(2,1)}, u32[]{:S(2)}) copy-start(bf16[256,256]{1,0:T(8,128)(2,1)} %constant.26.clone.later_ref) | copy-start | bytes 393220
  17.1 9.0 %copy-start.2 = (bf16[1,128,4096]{2,1,0:T(8,128)(2,1)S(1)}, bf16[1,128,4096]{2,1,0:T(8,128)(2,1)}, u32[]{:S(2)}) copy-start(bf16[1,128,4096]{2,1,0:T(8,128)(2,1)} %param.13) | copy-start | bytes 3145732
  17.1 9.0 %copy-start.4 = (bf16[1,128,4096]{2,1,0:T(8,128)(2,1)S(1)}, bf16[1,128,4096]{2,1,0:T(8,128)(2,1)}, u32[]{:S(2)}) copy-start(bf16[1,128,4096]{2,1,0:T(8,128)(2,1)} %param.14) | copy-start | bytes 3145732
  17.1 20.2 %collective-permute-start.1 = (bf16[128,2048]{1,0:T(8,128)(2,1)S(1)}, bf16[128,2048]{1,0:T(8,128)(2,1)S(1)}, u32[]{:S(2)}, u32[]{:S(2)}) collective-permute-start(bf16[128,2048]{1,0:T(8,128)(2,1)S(1)} %get-tuple-element.51.mixed_ref), channel_id=1, source_target_pairs={{0,1},{1,2},{2,3},{3,4},{4,5},{5,6},{6,7},{7,8},{8,9},{9,10},{10,1... | collective-permute-start | bytes 1572872 | tf_op jit(solution)/shard_map/ppermute | solution.py:48
  26.2 3.0 %copy-start.21 = (f32[128,2048]{1,0:T(8,128)}, f32[128,2048]{1,0:T(8,128)S(1)}, u32[]{:S(2)}) copy-start(f32[128,2048]{1,0:T(8,128)S(1)} %get-tuple-element.74.long_ref) | copy-start | bytes 3145732
  29.2 14.2 %collective-permute-start.3 = (bf16[128,2048]{1,0:T(8,128)(2,1)S(1)}, bf16[128,2048]{1,0:T(8,128)(2,1)S(1)}, u32[]{:S(2)}, u32[]{:S(2)}) collective-permute-start(bf16[128,2048]{1,0:T(8,128)(2,1)S(1)} %get-tuple-element.54.mixed_ref), channel_id=1, source_target_pairs={{0,1},{1,2},{2,3},{3,4},{4,5},{5,6},{6,7},{7,8},{8,9},{9,10},{10,1... | collective-permute-start | bytes 1572872 | tf_op jit(solution)/shard_map/ppermute | solution.py:48
  37.3 6.0 %copy-start.23 = (f32[128,2048]{1,0:T(8,128)}, f32[128,2048]{1,0:T(8,128)S(1)}, u32[]{:S(2)}) copy-start(f32[128,2048]{1,0:T(8,128)S(1)} %get-tuple-element.73.long_ref) | copy-start | bytes 3145732
  37.4 6.0 %copy-start.17 = (bf16[128,2048]{1,0:T(8,128)(2,1)}, bf16[128,2048]{1,0:T(8,128)(2,1)S(1)}, u32[]{:S(2)}) copy-start(bf16[128,2048]{1,0:T(8,128)(2,1)S(1)} %collective-permute-done.1.prev_ref) | copy-start | bytes 1572868
  43.3 8.6 %copy-start.19 = (bf16[128,2048]{1,0:T(8,128)(2,1)}, bf16[128,2048]{1,0:T(8,128)(2,1)S(1)}, u32[]{:S(2)}) copy-start(bf16[128,2048]{1,0:T(8,128)(2,1)S(1)} %collective-permute-done.3.prev_ref) | copy-start | bytes 1572868
  43.4 9.6 %collective-permute-start.4 = (bf16[16,136,128]{2,1,0:T(8,128)(2,1)S(1)}, bf16[16,136,128]{2,1,0:T(8,128)(2,1)S(1)}, u32[]{:S(2)}, u32[]{:S(2)}) collective-permute-start(bf16[16,136,128]{2,1,0:T(8,128)(2,1)S(1)} %get-tuple-element.68), channel_id=1, source_target_pairs={{0,32},{32,0},{1,33},{33,1},{2,34},{34,2},{3,35},{35,3},{4,36},{36... | collective-permute-start | bytes 1671176 | tf_op jit(solution)/shard_map/ppermute | solution.py:376
  52.9 13.9 %copy-start.5 = (bf16[1,128,4096]{2,1,0:T(8,128)(2,1)S(1)}, bf16[1,128,4096]{2,1,0:T(8,128)(2,1)}, u32[]{:S(2)}) copy-start(bf16[1,128,4096]{2,1,0:T(8,128)(2,1)} %param.15) | copy-start | bytes 3145732
  52.9 14.0 %copy-start.16 = (bf16[256,256]{1,0:T(8,128)(2,1)S(1)}, bf16[256,256]{1,0:T(8,128)(2,1)}, u32[]{:S(2)}) copy-start(bf16[256,256]{1,0:T(8,128)(2,1)} %constant.26.clone.later_ref) | copy-start | bytes 393220
  54.0 24.3 %all-to-all-start = ((bf16[16,1,136,128]{3,2,1,0:T(8,128)(2,1)}), bf16[16,1,136,128]{3,2,1,0:T(8,128)(2,1)}, u32[]{:S(2)}, u32[]{:S(2)}) async-start(bf16[16,1,136,128]{3,2,1,0:T(8,128)(2,1)} %bitcast.36), calls=%async_computation | async-start | bytes 1114112 | tf_op jit(solution)/shard_map/all_to_all | solution.py:364
  66.9 1.2 copy-start.6
  70.4 3.1 %copy-start.7 = (bf16[1,128,4096]{2,1,0:T(8,128)(2,1)S(1)}, bf16[1,128,4096]{2,1,0:T(8,128)(2,1)}, u32[]{:S(2)}) copy-start(bf16[1,128,4096]{2,1,0:T(8,128)(2,1)} %param.18) | copy-start | bytes 3145732
  70.4 3.1 %copy-start.20 = (bf16[128,2048]{1,0:T(8,128)(2,1)S(1)}, bf16[128,2048]{1,0:T(8,128)(2,1)}, u32[]{:S(2)}) copy-start(bf16[128,2048]{1,0:T(8,128)(2,1)} %copy-done.19) | copy-start | bytes 1572868
  70.4 3.1 %copy-start.24 = (f32[128,2048]{1,0:T(8,128)S(1)}, f32[128,2048]{1,0:T(8,128)}, u32[]{:S(2)}) copy-start(f32[128,2048]{1,0:T(8,128)} %copy-done.23) | copy-start | bytes 3145732
  76.7 32.2 %copy-start.10 = (bf16[128,4096]{1,0:T(8,128)(2,1)S(1)}, bf16[128,4096]{1,0:T(8,128)(2,1)}, u32[]{:S(2)}) copy-start(bf16[128,4096]{1,0:T(8,128)(2,1)} %copy-done.9) | copy-start | bytes 3145732
  80.1 21.4 %all-to-all-start.1 = ((bf16[8,1,136,128]{3,2,1,0:T(8,128)(2,1)}), bf16[8,1,136,128]{3,2,1,0:T(8,128)(2,1)S(1)}, u32[]{:S(2)}, u32[]{:S(2)}) async-start(bf16[8,1,136,128]{3,2,1,0:T(8,128)(2,1)} %broadcast_in_dim.35), calls=%async_computation.1 | async-start | bytes 557056 | tf_op jit(solution)/shard_map/all_to_all | solution.py:364
  91.2 10.4 %collective-permute-start.5 = (bf16[8,4096]{1,0:T(8,128)(2,1)}, bf16[8,4096]{1,0:T(8,128)(2,1)S(1)}, u32[]{:S(2)}, u32[]{:S(2)}) collective-permute-start(bf16[8,4096]{1,0:T(8,128)(2,1)} %copy-done.25), channel_id=1, source_target_pairs={{1,0},{2,1},{3,2},{4,3},{5,4},{6,5},{7,6},{8,7},{9,8},{10,9},{11,1... | collective-permute-start | bytes 196616 | tf_op jit(solution)/shard_map/ppermute | solution.py:48
  102.5 16.9 %all-to-all-start.2 = ((bf16[16,1,136,128]{3,2,1,0:T(8,128)(2,1)}), bf16[16,1,136,128]{3,2,1,0:T(8,128)(2,1)S(1)}, u32[]{:S(2)}, u32[]{:S(2)}) async-start(bf16[16,1,136,128]{3,2,1,0:T(8,128)(2,1)} %broadcast_in_dim.37), calls=%async_computation.2 | async-start | bytes 1114112 | tf_op jit(solution)/shard_map/all_to_all | solution.py:364
  119.4 3.9 %collective-permute-start.6 = (bf16[16,136,128]{2,1,0:T(8,128)(2,1)S(1)}, bf16[16,136,128]{2,1,0:T(8,128)(2,1)S(1)}, u32[]{:S(2)}, u32[]{:S(2)}) collective-permute-start(bf16[16,136,128]{2,1,0:T(8,128)(2,1)S(1)} %bitcast.34), channel_id=1, source_target_pairs={{0,32},{32,0},{1,33},{33,1},{2,34},{34,2},{3,35},{35,3},{4,36},{36... | collective-permute-start | bytes 1671176 | tf_op jit(solution)/shard_map/ppermute | solution.py:376
  (5 other events, 5.5 us)

commit v4 on v3

--- a/solution.py
+++ b/solution.py
@@ -306,13 +306,13 @@
     def small(self):
         return min(8, self.parts // 4)
 
-    def mix(self, half, lengths, v, before, gs, staps):
+    def mix(self, half, lengths, v, before, gs, staps, mib):
         out = self.shaped(self.rows, "half")
         return self.call(
             mix_kernel, self.small(), half,
             [("scalars", lengths), ("whole", v), ("whole", before), ("whole", gs), ("whole", staps)],
             [out(BF), out(F32)],
-            [(self.rows + RIM, 0, F32), (self.rows, LANES, jnp.int32)], 3, 20)
+            [(self.rows + RIM, 0, F32), (self.rows, LANES, jnp.int32)], 3, mib)
 
     def own(self, half, lengths, mixed, adj, ltaps):
         out = self.shaped(self.rows, "half")
@@ -345,14 +345,14 @@
             long_kernel, self.small(), half,
             [("scalars", lengths), ("whole", gl), ("whole", up), ("half", own_long), ("half", prev),
              ("whole", ltaps), ("table", self.tables[0]), ("table", self.tables[2])],
-            [out(BF)] * 2, [(2 * self.rows, LANES, BF)], 3, 24, filled)
+            [out(BF)] * 2, [(2 * self.rows, LANES, BF)], 3, 56, filled)
 
     def values_grad(self, lengths, adjs, after, staps):
         return self.call(
             values_kernel, 2 * self.small(), None,
             [("scalars", lengths), ("whole", adjs), ("whole", after), ("whole", staps)],
             [self.shaped(self.rows, "whole")(BF)],
-            [(self.count * self.rows, 2 * LANES, BF)], 4, 24)[0]
+            [(self.count * self.rows, 2 * LANES, BF)], 4, 56)[0]
 
     def spread(self, mine, other):
         return self.call(
@@ -389,10 +389,11 @@
 
     before = passed_along(v[rows - RIM :], 1)
     adj = (up.astype(F32) * gl.astype(F32)).astype(BF)
+    mixed_a, short_a = k.mix(given, lengths, v, before, gs, short_taps, 56)
+    mixed_a, adj = together((mixed_a, adj))
+    prev_a = passed_along(mixed_a, 1)
     following = passed_along(adj, -1)
-    mixed_a, short_a = k.mix(given, lengths, v, before, gs, short_taps)
-    prev_a = passed_along(mixed_a, 1)
-    mixed_b, short_b = k.mix(kept, lengths, v, before, gs, short_taps)
+    mixed_b, short_b = k.mix(kept, lengths, v, before, gs, short_taps, 20)
     long_a, back_a, terms_a = k.own(given, lengths, mixed_a, adj, long_taps)
     mixed_b, back_a = together((mixed_b, back_a))
     prev_b = passed_along(mixed_b, 1)
@@ -407,15 +408,15 @@
 
     planes = ("y", "x")
     half = (grads_b.astype(F32) + got.astype(F32)).astype(BF)
-    half, long_a, adjs, head = together((half, long_a, adjs, head))
+    half, long_a, long_b, head = together((half, long_a, long_b, head))
     share = half.reshape((lax.axis_size(planes), -1) + half.shape[1:])
     share = added(traded(share, planes)).astype(BF)
-    out_ggl = k.long(given, lengths, gl, up, long_a, prev_a, long_taps, ())
-    out, ggl = k.long(kept, lengths, gl, up, long_b, prev_b, long_taps, tuple(out_ggl))
-    share, out, ggl, adjs, head = together((share, out, ggl, adjs, head))
     after = passed_along(head, -1)
+    filled = k.long(given, lengths, gl, up, long_a, prev_a, long_taps, ())
+    share, after, filled, long_b = together((share, after, tuple(filled), long_b))
     share = (added(copies(share, "z")) * factor).astype(BF)
-    share, after, adjs = together((share, after, adjs))
+    out, ggl = k.long(kept, lengths, gl, up, long_b, prev_b, long_taps, filled)
+    share, out, ggl, adjs = together((share, out, ggl, adjs))
     mine = copies(share, planes).reshape(half.shape)
     gv = k.values_grad(lengths, adjs, after, short_taps)
     mine, gv = together((mine, gv))

time: 126 us -> 119 us (0.944); the launches traced: 125 us -> 121 us
  local copies, waits for them, and re-layouts: 10.1 us -> 7.89 us
  Pallas kernels: 38.8 us -> 40.6 us
  starting transfers between devices: 50.8 us -> 49.2 us
  other arithmetic: 4.14 us -> 2.87 us
    all_to_all x3, starting transfers between devices: 30.3 us -> 27.2 us  [traded(): return lax.all_to_all(block, axes, 0, 0, tiled=True)]
    pallas_call x10, Pallas kernels: 38.8 us -> 40.6 us  [call(): pl.pallas_call(kernel, grid_spec=pltpu.PrefetchScalarGridSpec(num_scalar_...]
    unnamed x54 -> x42, local copies, waits for them, and re-layouts: 7 us -> 5.42 us
    ppermute x5, starting transfers between devices: 15.3 us -> 16.6 us  [passed_along(): return lax.ppermute(block, CTX, route)]
  transfers between devices with their start and end apart: 10 -> 10, of which waited for: 5 -> 5; matrix products, arithmetic and copies ran while one was open for 1% -> 2% of each run, Pallas kernels for 30% -> 29%
where the time goes in v4:
time: 119 us; the launch traced here: 121 us
  starting transfers between devices  49.2 us (41%)
  Pallas kernels  40.6 us (34%)
  waiting for transfers between devices  19 us (16%)
  local copies, waits for them, and re-layouts  7.89 us (7%)
  other arithmetic  2.87 us (2%)
    pallas_call x10, Pallas kernels, call(): pl.pallas_call(kernel, grid_spec=pltpu.PrefetchScalarGridSpec(num_scalar_...  40.6 us
    all_to_all x3, starting transfers between devices, traded(): return lax.all_to_all(block, axes, 0, 0, tiled=True)  27.2 us
    ppermute x5, starting transfers between devices, passed_along(): return lax.ppermute(block, CTX, route)  16.6 us
    all_to_all x3, waiting for transfers between devices, traded(): return lax.all_to_all(block, axes, 0, 0, tiled=True)  16.2 us
    ppermute x2, starting transfers between devices, swapped(): return lax.ppermute(block, 'core', [(0, 1), (1, 0)])  5.43 us
    unnamed x42, local copies, waits for them, and re-layouts  5.42 us
  transfers between devices with their start and end apart: 10, of which 5 were waited for; matrix products, arithmetic and copies ran while one was open for 2% of the time, Pallas kernels for 29%

profile of v4, /device:TPU:1, one launch (start us, length us, event | category | flops | bytes accessed | tf_op | source)
XLA Modules:
  0.0 120.7 jit_solution(17380031723841076365)
XLA Ops:
  1.5 4.1 %collective-permute-start = (bf16[8,4096]{1,0:T(8,128)(2,1)S(1)}, bf16[8,4096]{1,0:T(8,128)(2,1)S(1)}, u32[]{:S(2)}, u32[]{:S(2)}) collective-permute-start(bf16[8,4096]{1,0:T(8,128)(2,1)S(1)} %slice_bitcast_fusion), channel_id=1, source_target_pairs={{0,1},{1,2},{2,3},{3,4},{4,5},{5,6},{6,7},{7,8},{8,9},{9,10},{10,1... | collective-permute-start | bytes 196616 | tf_op jit(solution)/shard_map/ppermute | solution.py:48
  5.6 1.8 %multiply_convert_fusion.adj_ref = bf16[128,4096]{1,0:T(8,128)(2,1)S(1)} fusion(bf16[1,128,4096]{2,1,0:T(8,128)(2,1)} %param.15, bf16[1,128,4096]{2,1,0:T(8,128)(2,1)} %param.18), kind=kLoop, calls=%fused_computation | loop fusion | flops 2097152 | bytes 3145728 | tf_op jit(solution)/shard_map/convert_element_type | solution.py:391
  8.0 3.9 %shard_map.163 = (bf16[128,2048]{1,0:T(8,128)(2,1)}, f32[128,2048]{1,0:T(8,128)}) custom-call(s32[1]{0:T(128)S(6)} %sub.3.half_ref, s32[1,8]{1,0:T(1,128)} %lengths_ref.17, bf16[128,4096]{1,0:T(8,128)(2,1)} %bitcast.22, bf16[8,4096]{1,0:T(8,128)(2,1)} %copy-done.13, bf16[128,4096]{1,0:T(8,128)(2,1)} %bitcast.26, f32[7,4096]{1,0:T(8,128)} %taps_ref.5), custom_call_target="tpu_custom_call" | custom-call | bytes 10500000 | tf_op jit(solution)/shard_map/pallas_call | solution.py:286
  12.0 1.4 %collective-permute-start.2 = (bf16[128,4096]{1,0:T(8,128)(2,1)S(1)}, bf16[128,4096]{1,0:T(8,128)(2,1)S(1)}, u32[]{:S(2)}, u32[]{:S(2)}) collective-permute-start(bf16[128,4096]{1,0:T(8,128)(2,1)S(1)} %multiply_convert_fusion.adj_ref), channel_id=1, source_target_pairs={{1,0},{2,1},{3,2},{4,3},{5,4},{6,5},{7,6},{8,7},{9,8},{10,9},{11,1... | collective-permute-start | bytes 3145736 | tf_op jit(solution)/shard_map/ppermute | solution.py:48
  13.4 4.0 %collective-permute-start.1 = (bf16[128,2048]{1,0:T(8,128)(2,1)}, bf16[128,2048]{1,0:T(8,128)(2,1)S(1)}, u32[]{:S(2)}, u32[]{:S(2)}) collective-permute-start(bf16[128,2048]{1,0:T(8,128)(2,1)} %get-tuple-element.56.mixed_ref), channel_id=1, source_target_pairs={{0,1},{1,2},{2,3},{3,4},{4,5},{5,6},{6,7},{7,8},{8,9},{9,10},{10,1... | collective-permute-start | bytes 1572872 | tf_op jit(solution)/shard_map/ppermute | solution.py:48
  17.5 0.9 copy-done.7
  18.4 0.9 copy-done.8
  19.3 0.9 copy-done.9
  20.2 1.0 copy-done.18
  21.3 4.7 %shard_map.165 = (f32[128,2048]{1,0:T(8,128)S(1)}, f32[128,2048]{1,0:T(8,128)S(1)}, f32[128,2048]{1,0:T(8,128)S(1)}) custom-call(s32[1]{0:T(128)S(6)} %sub.3.half_ref, s32[1,8]{1,0:T(1,128)S(1)} %copy-done.19, bf16[128,2048]{1,0:T(8,128)(2,1)S(1)} %copy-done.18, bf16[128,4096]{1,0:T(8,128)(2,1)S(1)} %multiply_convert_fusion.adj_ref, ...), custom_call_target="tpu_custom_call" | custom-call | bytes 5250000 | tf_op jit(solution)/shard_map/pallas_call | solution.py:286
  26.0 2.8 %shard_map.164 = (bf16[128,2048]{1,0:T(8,128)(2,1)S(1)}, f32[128,2048]{1,0:T(8,128)S(1)}) custom-call(s32[1]{0:T(128)} %bitcast.half_ref, s32[1,8]{1,0:T(1,128)S(1)} %copy-done.19, bf16[128,4096]{1,0:T(8,128)(2,1)S(1)} %bitcast.23, bf16[8,4096]{1,0:T(8,128)(2,1)S(1)} %copy-done.14, bf16[128,4096]{1,0:T(8,128)(2,1)S(1)} %bitcast.27, f32[7,4096]{1,0:T(8,128)S(1)} %copy-done.5), custom_call_target="tpu_custom_call" | custom-call | bytes 10500000 | tf_op jit(solution)/shard_map/pallas_call | solution.py:286
  28.9 5.8 %collective-permute-start.3 = (bf16[128,2048]{1,0:T(8,128)(2,1)S(1)}, bf16[128,2048]{1,0:T(8,128)(2,1)S(1)}, u32[]{:S(2)}, u32[]{:S(2)}) collective-permute-start(bf16[128,2048]{1,0:T(8,128)(2,1)S(1)} %get-tuple-element.59.mixed_ref), channel_id=1, source_target_pairs={{0,1},{1,2},{2,3},{3,4},{4,5},{5,6},{6,7},{7,8},{8,9},{9,10},{10,1... | collective-permute-start | bytes 1572872 | tf_op jit(solution)/shard_map/ppermute | solution.py:48
  34.6 4.7 %shard_map.166 = (f32[128,2048]{1,0:T(8,128)S(1)}, f32[128,2048]{1,0:T(8,128)S(1)}, f32[128,2048]{1,0:T(8,128)S(1)}) custom-call(s32[1]{0:T(128)} %bitcast.half_ref, s32[1,8]{1,0:T(1,128)S(1)} %copy-done.19, bf16[128,2048]{1,0:T(8,128)(2,1)S(1)} %get-tuple-element.59.mixed_ref, bf16[128,4096]{1,0:T(8,128)(2,1)S(1)} %multiply_convert_fusion.adj_ref, ...), custom_call_target="tpu_custom_call" | custom-call | bytes 5250000 | tf_op jit(solution)/shard_map/pallas_call | solution.py:286
  39.4 5.3 %shard_map.167 = (bf16[128,4096]{1,0:T(8,128)(2,1)}, bf16[128,4096]{1,0:T(8,128)(2,1)S(1)}, bf16[8,4096]{1,0:T(8,128)(2,1)S(1)}, bf16[16,136,128]{2,1,0:T(8,128)(2,1)S(1)}) custom-call(s32[1]{0:T(128)S(6)} %sub.3.half_ref, s32[1,8]{1,0:T(1,128)S(1)} %copy-done.19, bf16[128,4096]{1,0:T(8,128)(2,1)S(1)} %bitcast.24, bf16[8,4096]{1,0:T(8,128)(2,1)S(1)} %copy-done.14, ...), custom_call_target="tpu_custom_call" | custom-call | bytes 5250000 | tf_op jit(solution)/shard_map/pallas_call | solution.py:286
  44.7 1.3 %collective-permute-done.3.prev_ref = bf16[128,2048]{1,0:T(8,128)(2,1)S(1)} collective-permute-done((bf16[128,2048]{1,0:T(8,128)(2,1)S(1)}, bf16[128,2048]{1,0:T(8,128)(2,1)S(1)}, u32[]{:S(2)}, u32[]{:S(2)}) %collective-permute-start.3) | collective-permute-done | bytes 524320 | tf_op jit(solution)/shard_map/ppermute | solution.py:48
  46.7 5.2 %shard_map.168 = (bf16[128,4096]{1,0:T(8,128)(2,1)}, bf16[128,4096]{1,0:T(8,128)(2,1)S(1)}, bf16[8,4096]{1,0:T(8,128)(2,1)S(1)}, bf16[16,136,128]{2,1,0:T(8,128)(2,1)S(1)}) custom-call(s32[1]{0:T(128)} %bitcast.half_ref, s32[1,8]{1,0:T(1,128)S(1)} %copy-done.19, ...), custom_call_target="tpu_custom_call", output_to_operand_aliasing={{0}: (17, {}), {1}: (18, {}), {2}: (19, {})} | custom-call | bytes 5250000 | tf_op jit(solution)/shard_map/pallas_call | solution.py:286
  52.0 1.0 copy-done.4
  52.9 1.0 add_convert_fusion
  53.9 12.3 %all-to-all-start = ((bf16[16,1,136,128]{3,2,1,0:T(8,128)(2,1)}), bf16[16,1,136,128]{3,2,1,0:T(8,128)(2,1)S(1)}, u32[]{:S(2)}, u32[]{:S(2)}) async-start(bf16[16,1,136,128]{3,2,1,0:T(8,128)(2,1)} %bitcast.7), calls=%async_computation | async-start | bytes 1114112 | tf_op jit(solution)/shard_map/all_to_all | solution.py:364
  66.2 1.3 %collective-permute-start.5 = (bf16[8,4096]{1,0:T(8,128)(2,1)S(1)}, bf16[8,4096]{1,0:T(8,128)(2,1)S(1)}, u32[]{:S(2)}, u32[]{:S(2)}) collective-permute-start(bf16[8,4096]{1,0:T(8,128)(2,1)S(1)} %get-tuple-element.78), channel_id=1, source_target_pairs={{1,0},{2,1},{3,2},{4,3},{5,4},{6,5},{7,6},{8,7},{9,8},{10,9},{11,1... | collective-permute-start | bytes 196616 | tf_op jit(solution)/shard_map/ppermute | solution.py:48
  67.5 4.1 %shard_map.169 = (bf16[128,4096]{1,0:T(8,128)(2,1)}, bf16[128,4096]{1,0:T(8,128)(2,1)}) custom-call(s32[1]{0:T(128)S(6)} %sub.3.half_ref, s32[1,8]{1,0:T(1,128)} %lengths_ref.17, bf16[128,4096]{1,0:T(8,128)(2,1)} %bitcast.32, bf16[128,4096]{1,0:T(8,128)(2,1)} %bitcast.34, f32[128,2048]{1,0:T(8,128)} %copy-done.16, bf16[128,2048]{1,0:T(8,128)(2,1)} %copy-done.12, ...), custom_call_target="tpu_custom_call" | custom-call | bytes 10500000 | tf_op jit(solution)/shard_map/pallas_call | solution.py:286
  71.6 6.0 %all-to-all-done = bf16[16,1,136,128]{3,2,1,0:T(8,128)(2,1)S(1)} async-done(((bf16[16,1,136,128]{3,2,1,0:T(8,128)(2,1)}), bf16[16,1,136,128]{3,2,1,0:T(8,128)(2,1)S(1)}, u32[]{:S(2)}, u32[]{:S(2)}) %all-to-all-start) | async-done | bytes 557088 | tf_op jit(solution)/shard_map/all_to_all | solution.py:364
  78.4 10.3 %all-to-all-start.1 = ((bf16[8,1,136,128]{3,2,1,0:T(8,128)(2,1)}), bf16[8,1,136,128]{3,2,1,0:T(8,128)(2,1)S(1)}, u32[]{:S(2)}, u32[]{:S(2)}) async-start(bf16[8,1,136,128]{3,2,1,0:T(8,128)(2,1)} %broadcast_in_dim.33), calls=%async_computation.1 | async-start | bytes 557056 | tf_op jit(solution)/shard_map/all_to_all | solution.py:364
  88.7 4.1 %shard_map.170 = (bf16[128,4096]{1,0:T(8,128)(2,1)}, bf16[128,4096]{1,0:T(8,128)(2,1)}) custom-call(s32[1]{0:T(128)} %bitcast.half_ref, s32[1,8]{1,0:T(1,128)} %lengths_ref.17, bf16[128,4096]{1,0:T(8,128)(2,1)} %bitcast.33, bf16[128,4096]{1,0:T(8,128)(2,1)} %bitcast.35, f32[128,2048]{1,0:T(8,128)} %copy-done.15, ...), custom_call_target="tpu_custom_call", output_to_operand_aliasing={{0}: (9, {}), {1}: (10, {})} | custom-call | bytes 10500000 | tf_op jit(solution)/shard_map/pallas_call | solution.py:286
  92.8 5.3 %all-to-all-done.1 = bf16[8,1,136,128]{3,2,1,0:T(8,128)(2,1)S(1)} async-done(((bf16[8,1,136,128]{3,2,1,0:T(8,128)(2,1)}), bf16[8,1,136,128]{3,2,1,0:T(8,128)(2,1)S(1)}, u32[]{:S(2)}, u32[]{:S(2)}) %all-to-all-start.1) | async-done | bytes 278560 | tf_op jit(solution)/shard_map/all_to_all | solution.py:364
  98.2 0.9 broadcast_in_dim.37
  99.0 4.6 %all-to-all-start.2 = ((bf16[16,1,136,128]{3,2,1,0:T(8,128)(2,1)}), bf16[16,1,136,128]{3,2,1,0:T(8,128)(2,1)S(1)}, u32[]{:S(2)}, u32[]{:S(2)}) async-start(bf16[16,1,136,128]{3,2,1,0:T(8,128)(2,1)} %broadcast_in_dim.37), calls=%async_computation.2 | async-start | bytes 1114112 | tf_op jit(solution)/shard_map/all_to_all | solution.py:364
  103.7 4.3 %shard_map.171 = bf16[128,4096]{1,0:T(8,128)(2,1)} custom-call(s32[1,8]{1,0:T(1,128)} %lengths_ref.17, bf16[128,4096]{1,0:T(8,128)(2,1)} %copy-done.4, bf16[8,4096]{1,0:T(8,128)(2,1)} %copy-done.20, f32[7,4096]{1,0:T(8,128)} %taps_ref.5), custom_call_target="tpu_custom_call" | custom-call | bytes 14000000 | tf_op jit(solution)/shard_map/pallas_call | solution.py:286
  108.0 4.9 %all-to-all-done.2 = bf16[16,1,136,128]{3,2,1,0:T(8,128)(2,1)S(1)} async-done(((bf16[16,1,136,128]{3,2,1,0:T(8,128)(2,1)}), bf16[16,1,136,128]{3,2,1,0:T(8,128)(2,1)S(1)}, u32[]{:S(2)}, u32[]{:S(2)}) %all-to-all-start.2) | async-done | bytes 557088 | tf_op jit(solution)/shard_map/all_to_all | solution.py:364
  112.9 4.7 %collective-permute-start.6 = (bf16[16,136,128]{2,1,0:T(8,128)(2,1)S(1)}, bf16[16,136,128]{2,1,0:T(8,128)(2,1)S(1)}, u32[]{:S(2)}, u32[]{:S(2)}) collective-permute-start(bf16[16,136,128]{2,1,0:T(8,128)(2,1)S(1)} %bitcast.30), channel_id=1, source_target_pairs={{0,32},{32,0},{1,33},{33,1},{2,34},{34,2},{3,35},{35,3},{4,36},{36... | collective-permute-start | bytes 1671176 | tf_op jit(solution)/shard_map/ppermute | solution.py:376
  117.6 1.6 %collective-permute-done.6.other_ref = bf16[16,136,128]{2,1,0:T(8,128)(2,1)S(1)} collective-permute-done((bf16[16,136,128]{2,1,0:T(8,128)(2,1)S(1)}, bf16[16,136,128]{2,1,0:T(8,128)(2,1)S(1)}, u32[]{:S(2)}, u32[]{:S(2)}) %collective-permute-start.6) | collective-permute-done | bytes 557088 | tf_op jit(solution)/shard_map/ppermute | solution.py:376
  119.2 1.5 %shard_map.172 = (f32[7,4096]{1,0:T(8,128)}, f32[128,4096]{1,0:T(8,128)}) custom-call(bf16[16,136,128]{2,1,0:T(8,128)(2,1)S(1)} %bitcast.31, bf16[16,136,128]{2,1,0:T(8,128)(2,1)S(1)} %collective-permute-done.6.other_ref), custom_call_target="tpu_custom_call" | custom-call | bytes 10500000 | tf_op jit(solution)/shard_map/pallas_call | solution.py:286
  (48 shorter events, 3.2 us)
Async XLA Ops:
  1.5 16.0 %copy-start = (f32[128,4096]{1,0:T(8,128)S(1)}, f32[128,4096]{1,0:T(8,128)}, u32[]{:S(2)}) copy-start(f32[128,4096]{1,0:T(8,128)} %ltaps_ref.11) | copy-start | bytes 6291460
  1.5 16.0 %copy-start.3 = (bf16[256,256]{1,0:T(8,128)(2,1)S(1)}, bf16[256,256]{1,0:T(8,128)(2,1)}, u32[]{:S(2)}) copy-start(bf16[256,256]{1,0:T(8,128)(2,1)} %constant.24.clone.first_ref) | copy-start | bytes 393220
  1.5 16.0 %copy-start.6 = (bf16[256,256]{1,0:T(8,128)(2,1)S(1)}, bf16[256,256]{1,0:T(8,128)(2,1)}, u32[]{:S(2)}) copy-start(bf16[256,256]{1,0:T(8,128)(2,1)} %constant.28.clone.totaps_ref) | copy-start | bytes 393220
  1.5 16.0 %copy-start.19 = (s32[1,8]{1,0:T(1,128)S(1)}, s32[1,8]{1,0:T(1,128)}, u32[]{:S(2)}) copy-start(s32[1,8]{1,0:T(1,128)} %lengths_ref.17) | copy-start | bytes 100
  1.5 5.9 %collective-permute-start = (bf16[8,4096]{1,0:T(8,128)(2,1)S(1)}, bf16[8,4096]{1,0:T(8,128)(2,1)S(1)}, u32[]{:S(2)}, u32[]{:S(2)}) collective-permute-start(bf16[8,4096]{1,0:T(8,128)(2,1)S(1)} %slice_bitcast_fusion), channel_id=1, source_target_pairs={{0,1},{1,2},{2,3},{3,4},{4,5},{5,6},{6,7},{7,8},{8,9},{9,10},{10,1... | collective-permute-start | bytes 196616 | tf_op jit(solution)/shard_map/ppermute | solution.py:48
  7.4 0.6 copy-start.13
  12.0 14.0 %copy-start.1 = (bf16[1,128,4096]{2,1,0:T(8,128)(2,1)S(1)}, bf16[1,128,4096]{2,1,0:T(8,128)(2,1)}, u32[]{:S(2)}) copy-start(bf16[1,128,4096]{2,1,0:T(8,128)(2,1)} %param.13) | copy-start | bytes 3145732
  12.0 14.0 %copy-start.2 = (bf16[1,128,4096]{2,1,0:T(8,128)(2,1)S(1)}, bf16[1,128,4096]{2,1,0:T(8,128)(2,1)}, u32[]{:S(2)}) copy-start(bf16[1,128,4096]{2,1,0:T(8,128)(2,1)} %param.14) | copy-start | bytes 3145732
  12.0 14.0 %copy-start.5 = (f32[7,4096]{1,0:T(8,128)S(1)}, f32[7,4096]{1,0:T(8,128)}, u32[]{:S(2)}) copy-start(f32[7,4096]{1,0:T(8,128)} %taps_ref.5) | copy-start | bytes 344068
  12.0 27.4 %collective-permute-start.2 = (bf16[128,4096]{1,0:T(8,128)(2,1)S(1)}, bf16[128,4096]{1,0:T(8,128)(2,1)S(1)}, u32[]{:S(2)}, u32[]{:S(2)}) collective-permute-start(bf16[128,4096]{1,0:T(8,128)(2,1)S(1)} %multiply_convert_fusion.adj_ref), channel_id=1, source_target_pairs={{1,0},{2,1},{3,2},{4,3},{5,4},{6,5},{7,6},{8,7},{9,8},{10,9},{11,1... | collective-permute-start | bytes 3145736 | tf_op jit(solution)/shard_map/ppermute | solution.py:48
  13.4 25.9 %collective-permute-start.1 = (bf16[128,2048]{1,0:T(8,128)(2,1)}, bf16[128,2048]{1,0:T(8,128)(2,1)S(1)}, u32[]{:S(2)}, u32[]{:S(2)}) collective-permute-start(bf16[128,2048]{1,0:T(8,128)(2,1)} %get-tuple-element.56.mixed_ref), channel_id=1, source_target_pairs={{0,1},{1,2},{2,3},{3,4},{4,5},{5,6},{6,7},{7,8},{8,9},{9,10},{10,1... | collective-permute-start | bytes 1572872 | tf_op jit(solution)/shard_map/ppermute | solution.py:48
  17.5 0.9 copy-start.7
  18.4 0.9 copy-start.8
  19.3 0.9 copy-start.9
  20.2 1.0 copy-start.18
  21.3 4.7 %copy-start.14 = (bf16[8,4096]{1,0:T(8,128)(2,1)S(1)}, bf16[8,4096]{1,0:T(8,128)(2,1)}, u32[]{:S(2)}) copy-start(bf16[8,4096]{1,0:T(8,128)(2,1)} %copy-done.13) | copy-start | bytes 196612
  26.0 2.8 %copy-start.16 = (f32[128,2048]{1,0:T(8,128)}, f32[128,2048]{1,0:T(8,128)S(1)}, u32[]{:S(2)}) copy-start(f32[128,2048]{1,0:T(8,128)S(1)} %get-tuple-element.79.long_ref) | copy-start | bytes 3145732
  26.0 8.6 %copy-start.10 = (bf16[256,256]{1,0:T(8,128)(2,1)S(1)}, bf16[256,256]{1,0:T(8,128)(2,1)}, u32[]{:S(2)}) copy-start(bf16[256,256]{1,0:T(8,128)(2,1)} %constant.26.clone.later_ref) | copy-start | bytes 393220
  28.8 10.6 %copy-start.17 = (f32[128,2048]{1,0:T(8,128)S(1)}, f32[128,2048]{1,0:T(8,128)}, u32[]{:S(2)}) copy-start(f32[128,2048]{1,0:T(8,128)} %get-tuple-element.63.short_ref) | copy-start | bytes 3145732
  28.9 17.1 %collective-permute-start.3 = (bf16[128,2048]{1,0:T(8,128)(2,1)S(1)}, bf16[128,2048]{1,0:T(8,128)(2,1)S(1)}, u32[]{:S(2)}, u32[]{:S(2)}) collective-permute-start(bf16[128,2048]{1,0:T(8,128)(2,1)S(1)} %get-tuple-element.59.mixed_ref), channel_id=1, source_target_pairs={{0,1},{1,2},{2,3},{3,4},{4,5},{5,6},{6,7},{7,8},{8,9},{9,10},{10,1... | collective-permute-start | bytes 1572872 | tf_op jit(solution)/shard_map/ppermute | solution.py:48
  39.4 5.4 %copy-start.15 = (f32[128,2048]{1,0:T(8,128)}, f32[128,2048]{1,0:T(8,128)S(1)}, u32[]{:S(2)}) copy-start(f32[128,2048]{1,0:T(8,128)S(1)} %get-tuple-element.84.long_ref) | copy-start | bytes 3145732
  39.4 5.3 %copy-start.12 = (bf16[128,2048]{1,0:T(8,128)(2,1)}, bf16[128,2048]{1,0:T(8,128)(2,1)S(1)}, u32[]{:S(2)}) copy-start(bf16[128,2048]{1,0:T(8,128)(2,1)S(1)} %collective-permute-done.1.prev_ref) | copy-start | bytes 1572868
  46.0 6.0 %copy-start.11 = (bf16[128,2048]{1,0:T(8,128)(2,1)}, bf16[128,2048]{1,0:T(8,128)(2,1)S(1)}, u32[]{:S(2)}) copy-start(bf16[128,2048]{1,0:T(8,128)(2,1)S(1)} %collective-permute-done.3.prev_ref) | copy-start | bytes 1572868
  46.0 6.9 %collective-permute-start.4 = (bf16[16,136,128]{2,1,0:T(8,128)(2,1)S(1)}, bf16[16,136,128]{2,1,0:T(8,128)(2,1)S(1)}, u32[]{:S(2)}, u32[]{:S(2)}) collective-permute-start(bf16[16,136,128]{2,1,0:T(8,128)(2,1)S(1)} %get-tuple-element.73), channel_id=1, source_target_pairs={{0,32},{32,0},{1,33},{33,1},{2,34},{34,2},{3,35},{35,3},{4,36},{36... | collective-permute-start | bytes 1671176 | tf_op jit(solution)/shard_map/ppermute | solution.py:376
  51.9 1.0 copy-start.4
  53.9 23.7 %all-to-all-start = ((bf16[16,1,136,128]{3,2,1,0:T(8,128)(2,1)}), bf16[16,1,136,128]{3,2,1,0:T(8,128)(2,1)S(1)}, u32[]{:S(2)}, u32[]{:S(2)}) async-start(bf16[16,1,136,128]{3,2,1,0:T(8,128)(2,1)} %bitcast.7), calls=%async_computation | async-start | bytes 1114112 | tf_op jit(solution)/shard_map/all_to_all | solution.py:364
  66.2 11.5 %collective-permute-start.5 = (bf16[8,4096]{1,0:T(8,128)(2,1)S(1)}, bf16[8,4096]{1,0:T(8,128)(2,1)S(1)}, u32[]{:S(2)}, u32[]{:S(2)}) collective-permute-start(bf16[8,4096]{1,0:T(8,128)(2,1)S(1)} %get-tuple-element.78), channel_id=1, source_target_pairs={{1,0},{2,1},{3,2},{4,3},{5,4},{6,5},{7,6},{8,7},{9,8},{10,9},{11,1... | collective-permute-start | bytes 196616 | tf_op jit(solution)/shard_map/ppermute | solution.py:48
  77.7 15.1 %copy-start.20 = (bf16[8,4096]{1,0:T(8,128)(2,1)}, bf16[8,4096]{1,0:T(8,128)(2,1)S(1)}, u32[]{:S(2)}) copy-start(bf16[8,4096]{1,0:T(8,128)(2,1)S(1)} %collective-permute-done.5.after_ref) | copy-start | bytes 196612
  78.4 19.7 %all-to-all-start.1 = ((bf16[8,1,136,128]{3,2,1,0:T(8,128)(2,1)}), bf16[8,1,136,128]{3,2,1,0:T(8,128)(2,1)S(1)}, u32[]{:S(2)}, u32[]{:S(2)}) async-start(bf16[8,1,136,128]{3,2,1,0:T(8,128)(2,1)} %broadcast_in_dim.33), calls=%async_computation.1 | async-start | bytes 557056 | tf_op jit(solution)/shard_map/all_to_all | solution.py:364
  99.0 13.9 %all-to-all-start.2 = ((bf16[16,1,136,128]{3,2,1,0:T(8,128)(2,1)}), bf16[16,1,136,128]{3,2,1,0:T(8,128)(2,1)S(1)}, u32[]{:S(2)}, u32[]{:S(2)}) async-start(bf16[16,1,136,128]{3,2,1,0:T(8,128)(2,1)} %broadcast_in_dim.37), calls=%async_computation.2 | async-start | bytes 1114112 | tf_op jit(solution)/shard_map/all_to_all | solution.py:364
  112.9 6.3 %collective-permute-start.6 = (bf16[16,136,128]{2,1,0:T(8,128)(2,1)S(1)}, bf16[16,136,128]{2,1,0:T(8,128)(2,1)S(1)}, u32[]{:S(2)}, u32[]{:S(2)}) collective-permute-start(bf16[16,136,128]{2,1,0:T(8,128)(2,1)S(1)} %bitcast.30), channel_id=1, source_target_pairs={{0,32},{32,0},{1,33},{33,1},{2,34},{34,2},{3,35},{35,3},{4,36},{36... | collective-permute-start | bytes 1671176 | tf_op jit(solution)/shard_map/ppermute | solution.py:376

commit v5 on v4

--- a/solution.py
+++ b/solution.py
@@ -39,7 +39,12 @@
     to_later = stack(inverse[rows:])
     to_first = stack(inverse[:rows])
     to_taps = stack(inverse[rows - np.arange(rows)])
-    return first, second, to_later, to_first, to_taps
+    return np.concatenate([first, second, to_later, to_first, to_taps], axis=0)
+
+
+def matrices(table_ref):
+    size = table_ref.shape[1]
+    return [lambda at=slice(k * size, (k + 1) * size): table_ref[at, :] for k in range(5)]
 
 
 def passed_along(block, distance):
@@ -121,43 +126,46 @@
     mixed_ref[...] = (gs_ref[...].astype(F32) * total).astype(BF)
 
 
-def own_kernel(half_ref, lengths_ref, mixed_ref, adj_ref, ltaps_ref, first_ref, second_ref, later_ref,
-               front_ref, totaps_ref, long_ref, back_ref, grads_ref, taps_spec, spec_acc, cuts_s):
-    rows, columns = mixed_ref.shape
+def note_cuts(lengths_ref, rows, cuts_s):
+    low, high = -1, -1
     cuts = cuts_of(lengths_ref, rows)
-    low, high = -1, -1
     for d, cut in enumerate(cuts):
         cuts_s[d] = cut
         if d < len(cuts) - 1:
             low = low + (cut <= 0).astype(jnp.int32)
             high = high + (cut <= rows - 1).astype(jnp.int32)
-    taps_spec[...] = dot(first_ref[...], ltaps_ref[...].astype(BF))
-    long_ref[...] = jnp.zeros_like(long_ref)
+    return low, high
+
+
+def own_kernel(half_ref, lengths_ref, mixed_ref, adj_ref, ltaps_ref, table_ref,
+               back_ref, grads_ref, taps_spec, spec_acc, cuts_s):
+    rows, columns = mixed_ref.shape
+    first, second, _, front, totaps = matrices(table_ref)
+    low, high = note_cuts(lengths_ref, rows, cuts_s)
+    taps_spec[...] = dot(first(), ltaps_ref[...].astype(BF))
     back_ref[...] = jnp.zeros_like(back_ref)
     spec_acc[...] = jnp.zeros_like(spec_acc)
     at = row_ids(rows)
 
     def document(d, carry):
         inside = jnp.where((at >= cuts_s[d]) & (at < cuts_s[d + 1]), 1.0, 0.0)
-        own = wide(inside, columns)
         own_bf = wide(inside.astype(BF), columns)
-        x_spec = dot(second_ref[...], mixed_ref[...] * own_bf)
-        product = times(taps_spec[...], x_spec, False).astype(BF)
-        long_ref[...] += own * back_dot(later_ref[...], product)
-        a_spec = dot(first_ref[...], adj_ref[...] * own_bf)
+        x_spec = dot(second(), mixed_ref[...] * own_bf)
+        a_spec = dot(first(), adj_ref[...] * own_bf)
         spec_acc[...] += times(a_spec, x_spec, True)
         product = times(taps_spec[...], a_spec, True).astype(BF)
-        back_ref[...] += own * back_dot(front_ref[...], product)
+        back_ref[...] += wide(inside, columns) * back_dot(front(), product)
         return carry
 
     lax.fori_loop(low, high + 1, document, 0)
-    grads_ref[...] = back_dot(totaps_ref[...], spec_acc[...].astype(BF))
+    grads_ref[...] = back_dot(totaps(), spec_acc[...].astype(BF))
 
 
 def grad_kernel(half_ref, lengths_ref, v_ref, before_ref, gs_ref, adj_ref, short_ref, back_ref, own_grads_ref,
-                prev_ref, next_ref, staps_ref, ltaps_ref, first_ref, second_ref, front_ref, totaps_ref, *rest):
+                prev_ref, next_ref, staps_ref, ltaps_ref, table_ref, *rest):
     ggs_ref, adjs_ref, head_ref, grads_ref, ext, reach_s, masks_s = rest[-7:]
     rows, columns = v_ref.shape
+    first, second, _, front, totaps = matrices(table_ref)
 
     @on_first_step
     def _():
@@ -171,14 +179,14 @@
         masks_s[3 * rows : 4 * rows, :] = ones(at + rows < end_at(cuts, rows - 1))
 
     mask = lambda k: wide(masks_s[k * rows : (k + 1) * rows, :], columns)
-    taps_spec = dot(first_ref[...], ltaps_ref[...].astype(BF))
-    next_spec = dot(second_ref[...], next_ref[...] * mask(3))
+    taps_spec = dot(first(), ltaps_ref[...].astype(BF))
+    next_spec = dot(second(), next_ref[...] * mask(3))
     product = times(taps_spec, next_spec, True).astype(BF)
-    back = back_ref[...] + mask(2).astype(F32) * back_dot(front_ref[...], product)
-    prev_spec = dot(first_ref[...], prev_ref[...] * mask(1))
-    own_spec = dot(first_ref[...], adj_ref[...] * mask(0))
+    back = back_ref[...] + mask(2).astype(F32) * back_dot(front(), product)
+    prev_spec = dot(first(), prev_ref[...] * mask(1))
+    own_spec = dot(first(), adj_ref[...] * mask(0))
     product = times(own_spec, prev_spec, True).astype(BF)
-    long_terms = own_grads_ref[...] + back_dot(totaps_ref[...], product)
+    long_terms = own_grads_ref[...] + back_dot(totaps(), product)
 
     ggs_ref[...] = (back * short_ref[...]).astype(BF)
     adj_short = (back * gs_ref[...].astype(F32)).astype(BF)
@@ -198,23 +206,28 @@
         grads_ref[k] = terms[:, k * LANES : (k + 1) * LANES]
 
 
-def long_kernel(half_ref, lengths_ref, gl_ref, up_ref, long_ref, prev_ref, ltaps_ref, first_ref, later_ref, *rest):
-    out_ref, ggl_ref, masks_s = rest[-3:]
+def long_kernel(half_ref, lengths_ref, gl_ref, up_ref, mixed_ref, prev_ref, ltaps_ref, table_ref, *rest):
+    out_ref, ggl_ref, taps_spec, prev_spec, long_acc, cuts_s = rest[-6:]
     rows, columns = gl_ref.shape
-
-    @on_first_step
-    def _():
-        at = row_ids(rows)
-        cuts = cuts_of(lengths_ref, rows)
-        ones = lambda mask: jnp.where(mask, 1.0, 0.0).astype(BF)
-        masks_s[0 * rows : 1 * rows, :] = ones(at < end_at(cuts, 0))
-        masks_s[1 * rows : 2 * rows, :] = ones(at - rows >= begin_at(cuts, 0))
-
-    mask = lambda k: wide(masks_s[k * rows : (k + 1) * rows, :], columns)
-    taps_spec = dot(first_ref[...], ltaps_ref[...].astype(BF))
-    prev_spec = dot(first_ref[...], prev_ref[...] * mask(1))
-    product = times(taps_spec, prev_spec, False).astype(BF)
-    long_mix = long_ref[...] + mask(0).astype(F32) * back_dot(later_ref[...], product)
+    first, second, later, _, _ = matrices(table_ref)
+    low, high = note_cuts(lengths_ref, rows, cuts_s)
+    at = row_ids(rows)
+    earlier = jnp.where(at - rows >= cuts_s[low], 1.0, 0.0).astype(BF)
+    taps_spec[...] = dot(first(), ltaps_ref[...].astype(BF))
+    prev_spec[...] = dot(first(), prev_ref[...] * wide(earlier, columns))
+    long_acc[...] = jnp.zeros_like(long_acc)
+
+    def document(d, carry):
+        inside = jnp.where((at >= cuts_s[d]) & (at < cuts_s[d + 1]), 1.0, 0.0)
+        reaches_back = jnp.where(d == low, 1.0, 0.0)
+        x_spec = dot(second(), mixed_ref[...] * wide(inside.astype(BF), columns))
+        x_spec = x_spec + reaches_back * prev_spec[...]
+        product = times(taps_spec[...], x_spec, False).astype(BF)
+        long_acc[...] += wide(inside, columns) * back_dot(later(), product)
+        return carry
+
+    lax.fori_loop(low, high + 1, document, 0)
+    long_mix = long_acc[...]
     out_ref[...] = (gl_ref[...].astype(F32) * long_mix).astype(BF)
     ggl_ref[...] = (up_ref[...].astype(F32) * long_mix).astype(BF)
 
@@ -261,7 +274,7 @@
     def __init__(self, rows, channels, count):
         self.rows, self.channels, self.count = rows, channels, count
         self.parts = channels // LANES
-        self.tables = [jnp.asarray(m) for m in spectra(rows)]
+        self.table = jnp.asarray(spectra(rows))
 
     def call(self, kernel, step_parts, half, ins, outs, scratch, cost, mib, filled=()):
         columns = step_parts * LANES
@@ -319,14 +332,13 @@
         spectrum = (2 * self.rows, 0, F32)
         return self.call(
             own_kernel, self.small(), half,
-            [("scalars", lengths), ("half", mixed), ("whole", adj), ("whole", ltaps)]
-            + [("table", t) for t in self.tables],
-            [out(F32)] * 3,
+            [("scalars", lengths), ("half", mixed), ("whole", adj), ("whole", ltaps),
+             ("table", self.table)],
+            [out(F32)] * 2,
             [spectrum, spectrum, (0, 0, pltpu.SMEM((16,), jnp.int32))], 1.5, 28)
 
     def grad(self, half, lengths, v, before, gs, adj, short, back, own_grads, prev, following,
              staps, ltaps, filled):
-        first, second, _, front, totaps = self.tables
         rows = self.rows
         out = self.shaped(rows, "whole")
         grads = jax.ShapeDtypeStruct((self.parts // 2, rows + RIM, LANES), BF)
@@ -334,18 +346,19 @@
             grad_kernel, self.small(), half,
             [("scalars", lengths), ("whole", v), ("whole", before), ("whole", gs), ("whole", adj),
              ("half", short), ("half", back), ("half", own_grads), ("half", prev),
-             ("whole", following), ("whole", staps), ("whole", ltaps)]
-            + [("table", t) for t in (first, second, front, totaps)],
+             ("whole", following), ("whole", staps), ("whole", ltaps), ("table", self.table)],
             [out(BF), out(BF), self.shaped(RIM, "whole")(BF), ("shares", grads)],
             [(rows + RIM, 0, F32), (rows, LANES, jnp.int32), (4 * rows, LANES, BF)], 1.5, 28, filled)
 
-    def long(self, half, lengths, gl, up, own_long, prev, ltaps, filled):
+    def long(self, half, lengths, gl, up, mixed, prev, ltaps, filled):
         out = self.shaped(self.rows, "whole")
+        spectrum = (2 * self.rows, 0, F32)
         return self.call(
             long_kernel, self.small(), half,
-            [("scalars", lengths), ("whole", gl), ("whole", up), ("half", own_long), ("half", prev),
-             ("whole", ltaps), ("table", self.tables[0]), ("table", self.tables[2])],
-            [out(BF)] * 2, [(2 * self.rows, LANES, BF)], 3, 56, filled)
+            [("scalars", lengths), ("whole", gl), ("whole", up), ("half", mixed), ("half", prev),
+             ("whole", ltaps), ("table", self.table)],
+            [out(BF)] * 2,
+            [spectrum, spectrum, (self.rows, 0, F32), (0, 0, pltpu.SMEM((16,), jnp.int32))], 3, 56, filled)
 
     def values_grad(self, lengths, adjs, after, staps):
         return self.call(
@@ -394,10 +407,10 @@
     prev_a = passed_along(mixed_a, 1)
     following = passed_along(adj, -1)
     mixed_b, short_b = k.mix(kept, lengths, v, before, gs, short_taps, 20)
-    long_a, back_a, terms_a = k.own(given, lengths, mixed_a, adj, long_taps)
+    back_a, terms_a = k.own(given, lengths, mixed_a, adj, long_taps)
     mixed_b, back_a = together((mixed_b, back_a))
     prev_b = passed_along(mixed_b, 1)
-    long_b, back_b, terms_b = k.own(kept, lengths, mixed_b, adj, long_taps)
+    back_b, terms_b = k.own(kept, lengths, mixed_b, adj, long_taps)
     prev_a, back_b = together((prev_a, back_b))
     ggs, adjs, head, grads_a = k.grad(given, lengths, v, before, gs, adj, short_a, back_a, terms_a,
                                       prev_a, following, short_taps, long_taps, ())
@@ -408,14 +421,14 @@
 
     planes = ("y", "x")
     half = (grads_b.astype(F32) + got.astype(F32)).astype(BF)
-    half, long_a, long_b, head = together((half, long_a, long_b, head))
+    half, mixed_a, mixed_b, head = together((half, mixed_a, mixed_b, head))
     share = half.reshape((lax.axis_size(planes), -1) + half.shape[1:])
     share = added(traded(share, planes)).astype(BF)
     after = passed_along(head, -1)
-    filled = k.long(given, lengths, gl, up, long_a, prev_a, long_taps, ())
-    share, after, filled, long_b = together((share, after, tuple(filled), long_b))
+    filled = k.long(given, lengths, gl, up, mixed_a, prev_a, long_taps, ())
+    share, after, filled, mixed_b = together((share, after, tuple(filled), mixed_b))
     share = (added(copies(share, "z")) * factor).astype(BF)
-    out, ggl = k.long(kept, lengths, gl, up, long_b, prev_b, long_taps, filled)
+    out, ggl = k.long(kept, lengths, gl, up, mixed_b, prev_b, long_taps, filled)
     share, out, ggl, adjs = together((share, out, ggl, adjs))
     mine = copies(share, planes).reshape(half.shape)
     gv = k.values_grad(lengths, adjs, after, short_taps)

time: 119 us -> 115 us (0.966); the launches traced: 121 us -> 113 us
  starting transfers between devices: 49.2 us -> 42.4 us
  local copies, waits for them, and re-layouts: 7.89 us -> 5.16 us
  waiting for transfers between devices: 19 us -> 21.2 us
    all_to_all x3, starting transfers between devices: 27.2 us -> 21.6 us  [traded(): return lax.all_to_all(block, axes, 0, 0, tiled=True)]
    ppermute x5, waiting for transfers between devices: 1.27 us -> 4.48 us  [passed_along(): return lax.ppermute(block, CTX, route)]
    unnamed x42 -> x30, local copies, waits for them, and re-layouts: 5.42 us -> 2.68 us
    ppermute x5, starting transfers between devices: 16.6 us -> 14.3 us  [passed_along(): return lax.ppermute(block, CTX, route)]
  transfers between devices with their start and end apart: 10 -> 10, of which waited for: 5 -> 5; matrix products, arithmetic and copies ran while one was open for 2% -> 2% of each run, Pallas kernels for 29% -> 31%
where the time goes in v5:
time: 115 us; the launch traced here: 113 us
  starting transfers between devices  42.4 us (37%)
  Pallas kernels  40.5 us (35%)
  waiting for transfers between devices  21.2 us (18%)
  local copies, waits for them, and re-layouts  5.16 us (4%)
  other arithmetic  2.87 us (2%)
    pallas_call x10, Pallas kernels, call(): pl.pallas_call(kernel, grid_spec=pltpu.PrefetchScalarGridSpec(num_scalar_...  40.5 us
    all_to_all x3, starting transfers between devices, traded(): return lax.all_to_all(block, axes, 0, 0, tiled=True)  21.6 us
    all_to_all x3, waiting for transfers between devices, traded(): return lax.all_to_all(block, axes, 0, 0, tiled=True)  15.1 us
    ppermute x5, starting transfers between devices, passed_along(): return lax.ppermute(block, CTX, route)  14.3 us
    ppermute x2, starting transfers between devices, swapped(): return lax.ppermute(block, 'core', [(0, 1), (1, 0)])  6.54 us
    ppermute x5, waiting for transfers between devices, passed_along(): return lax.ppermute(block, CTX, route)  4.48 us
    unnamed x30, local copies, waits for them, and re-layouts  2.68 us
  transfers between devices with their start and end apart: 10, of which 5 were waited for; matrix products, arithmetic and copies ran while one was open for 2% of the time, Pallas kernels for 31%

profile of v5, /device:TPU:1, one launch (start us, length us, event | category | flops | bytes accessed | tf_op | source)
XLA Modules:
  0.0 113.1 jit_solution(973644379859460913)
XLA Ops:
  0.6 0.8 slice_bitcast_fusion
  1.5 4.1 %collective-permute-start = (bf16[8,4096]{1,0:T(8,128)(2,1)S(1)}, bf16[8,4096]{1,0:T(8,128)(2,1)S(1)}, u32[]{:S(2)}, u32[]{:S(2)}) collective-permute-start(bf16[8,4096]{1,0:T(8,128)(2,1)S(1)} %slice_bitcast_fusion), channel_id=1, source_target_pairs={{0,1},{1,2},{2,3},{3,4},{4,5},{5,6},{6,7},{7,8},{8,9},{9,10},{10,1... | collective-permute-start | bytes 196616 | tf_op jit(solution)/shard_map/ppermute | solution.py:53
  5.6 1.8 %multiply_convert_fusion.adj_ref = bf16[128,4096]{1,0:T(8,128)(2,1)S(1)} fusion(bf16[1,128,4096]{2,1,0:T(8,128)(2,1)} %param.11, bf16[1,128,4096]{2,1,0:T(8,128)(2,1)} %param.14), kind=kLoop, calls=%fused_computation | loop fusion | flops 2097152 | bytes 3145728 | tf_op jit(solution)/shard_map/convert_element_type | solution.py:404
  8.0 3.9 %shard_map.127 = (bf16[128,2048]{1,0:T(8,128)(2,1)}, f32[128,2048]{1,0:T(8,128)}) custom-call(s32[1]{0:T(128)S(6)} %sub.3.half_ref, s32[1,8]{1,0:T(1,128)} %lengths_ref.17, bf16[128,4096]{1,0:T(8,128)(2,1)} %bitcast.22, bf16[8,4096]{1,0:T(8,128)(2,1)} %copy-done.10, bf16[128,4096]{1,0:T(8,128)(2,1)} %bitcast.26, f32[7,4096]{1,0:T(8,128)} %taps_ref.5), custom_call_target="tpu_custom_call" | custom-call | bytes 10500000 | tf_op jit(solution)/shard_map/pallas_call | solution.py:299
  12.0 1.4 %collective-permute-start.2 = (bf16[128,4096]{1,0:T(8,128)(2,1)S(1)}, bf16[128,4096]{1,0:T(8,128)(2,1)S(1)}, u32[]{:S(2)}, u32[]{:S(2)}) collective-permute-start(bf16[128,4096]{1,0:T(8,128)(2,1)S(1)} %multiply_convert_fusion.adj_ref), channel_id=1, source_target_pairs={{1,0},{2,1},{3,2},{4,3},{5,4},{6,5},{7,6},{8,7},{9,8},{10,9},{11,1... | collective-permute-start | bytes 3145736 | tf_op jit(solution)/shard_map/ppermute | solution.py:53
  13.4 4.0 %collective-permute-start.1 = (bf16[128,2048]{1,0:T(8,128)(2,1)}, bf16[128,2048]{1,0:T(8,128)(2,1)S(1)}, u32[]{:S(2)}, u32[]{:S(2)}) collective-permute-start(bf16[128,2048]{1,0:T(8,128)(2,1)} %get-tuple-element.75.mixed_ref), channel_id=1, source_target_pairs={{0,1},{1,2},{2,3},{3,4},{4,5},{5,6},{6,7},{7,8},{8,9},{9,10},{10,1... | collective-permute-start | bytes 1572872 | tf_op jit(solution)/shard_map/ppermute | solution.py:53
  17.5 1.0 copy-done.8
  18.5 4.0 %shard_map.129 = (f32[128,2048]{1,0:T(8,128)S(1)}, f32[128,2048]{1,0:T(8,128)S(1)}) custom-call(s32[1]{0:T(128)S(6)} %sub.3.half_ref, s32[1,8]{1,0:T(1,128)S(1)} %copy-done.13, bf16[128,2048]{1,0:T(8,128)(2,1)S(1)} %copy-done.8, bf16[128,4096]{1,0:T(8,128)(2,1)S(1)} %multiply_convert_fusion.adj_ref, f32[128,4096]{1,0:T(8,128)S(1)} %copy-done, ...), custom_call_target="tpu_custom_call" | custom-call | bytes 5250000 | tf_op jit(solution)/shard_map/pallas_call | solution.py:299
  22.6 2.8 %shard_map.128 = (bf16[128,2048]{1,0:T(8,128)(2,1)S(1)}, f32[128,2048]{1,0:T(8,128)S(1)}) custom-call(s32[1]{0:T(128)} %bitcast.half_ref, s32[1,8]{1,0:T(1,128)S(1)} %copy-done.13, bf16[128,4096]{1,0:T(8,128)(2,1)S(1)} %bitcast.23, bf16[8,4096]{1,0:T(8,128)(2,1)S(1)} %copy-done.11, bf16[128,4096]{1,0:T(8,128)(2,1)S(1)} %bitcast.27, f32[7,4096]{1,0:T(8,128)S(1)} %copy-done.5), custom_call_target="tpu_custom_call" | custom-call | bytes 10500000 | tf_op jit(solution)/shard_map/pallas_call | solution.py:299
  25.4 3.3 %collective-permute-start.3 = (bf16[128,2048]{1,0:T(8,128)(2,1)S(1)}, bf16[128,2048]{1,0:T(8,128)(2,1)S(1)}, u32[]{:S(2)}, u32[]{:S(2)}) collective-permute-start(bf16[128,2048]{1,0:T(8,128)(2,1)S(1)} %get-tuple-element.80.mixed_ref), channel_id=1, source_target_pairs={{0,1},{1,2},{2,3},{3,4},{4,5},{5,6},{6,7},{7,8},{8,9},{9,10},{10,1... | collective-permute-start | bytes 1572872 | tf_op jit(solution)/shard_map/ppermute | solution.py:53
  28.8 4.1 %shard_map.130 = (f32[128,2048]{1,0:T(8,128)S(1)}, f32[128,2048]{1,0:T(8,128)S(1)}) custom-call(s32[1]{0:T(128)} %bitcast.half_ref, s32[1,8]{1,0:T(1,128)S(1)} %copy-done.13, bf16[128,2048]{1,0:T(8,128)(2,1)S(1)} %get-tuple-element.80.mixed_ref, bf16[128,4096]{1,0:T(8,128)(2,1)S(1)} %multiply_convert_fusion.adj_ref, f32[128,4096]{1,0:T(8,128)S(1)} %copy-done, ...), custom_call_target="tpu_custom_call" | custom-call | bytes 5250000 | tf_op jit(solution)/shard_map/pallas_call | solution.py:299
  32.9 4.5 %collective-permute-done.2.next_ref = bf16[128,4096]{1,0:T(8,128)(2,1)S(1)} collective-permute-done((bf16[128,4096]{1,0:T(8,128)(2,1)S(1)}, bf16[128,4096]{1,0:T(8,128)(2,1)S(1)}, u32[]{:S(2)}, u32[]{:S(2)}) %collective-permute-start.2) | collective-permute-done | bytes 1048608 | tf_op jit(solution)/shard_map/ppermute | solution.py:53
  37.3 5.0 %shard_map.131 = (bf16[128,4096]{1,0:T(8,128)(2,1)}, bf16[128,4096]{1,0:T(8,128)(2,1)S(1)}, bf16[8,4096]{1,0:T(8,128)(2,1)S(1)}, bf16[16,136,128]{2,1,0:T(8,128)(2,1)S(1)}) custom-call(s32[1]{0:T(128)S(6)} %sub.3.half_ref, s32[1,8]{1,0:T(1,128)S(1)} %copy-done.13, bf16[128,4096]{1,0:T(8,128)(2,1)S(1)} %bitcast.24, bf16[8,4096]{1,0:T(8,128)(2,1)S(1)} %copy-done.11, ...), custom_call_target="tpu_custom_call" | custom-call | bytes 5250000 | tf_op jit(solution)/shard_map/pallas_call | solution.py:299
  42.3 2.4 %collective-permute-start.4 = (bf16[16,136,128]{2,1,0:T(8,128)(2,1)S(1)}, bf16[16,136,128]{2,1,0:T(8,128)(2,1)S(1)}, u32[]{:S(2)}, u32[]{:S(2)}) collective-permute-start(bf16[16,136,128]{2,1,0:T(8,128)(2,1)S(1)} %get-tuple-element.71), channel_id=1, source_target_pairs={{0,32},{32,0},{1,33},{33,1},{2,34},{34,2},{3,35},{35,3},{4,36},{36... | collective-permute-start | bytes 1671176 | tf_op jit(solution)/shard_map/ppermute | solution.py:389
  44.7 4.9 %shard_map.132 = (bf16[128,4096]{1,0:T(8,128)(2,1)}, bf16[128,4096]{1,0:T(8,128)(2,1)S(1)}, bf16[8,4096]{1,0:T(8,128)(2,1)S(1)}, bf16[16,136,128]{2,1,0:T(8,128)(2,1)S(1)}) custom-call(s32[1]{0:T(128)} %bitcast.half_ref, s32[1,8]{1,0:T(1,128)S(1)} %copy-done.13, ...), custom_call_target="tpu_custom_call", output_to_operand_aliasing={{0}: (14, {}), {1}: (15, {}), {2}: (16, {})} | custom-call | bytes 5250000 | tf_op jit(solution)/shard_map/pallas_call | solution.py:299
  49.6 1.0 copy-done.4
  50.6 1.0 add_convert_fusion
  51.6 9.0 %all-to-all-start = ((bf16[16,1,136,128]{3,2,1,0:T(8,128)(2,1)}), bf16[16,1,136,128]{3,2,1,0:T(8,128)(2,1)S(1)}, u32[]{:S(2)}, u32[]{:S(2)}) async-start(bf16[16,1,136,128]{3,2,1,0:T(8,128)(2,1)} %bitcast.7), calls=%async_computation | async-start | bytes 1114112 | tf_op jit(solution)/shard_map/all_to_all | solution.py:377
  60.5 1.5 %collective-permute-start.5 = (bf16[8,4096]{1,0:T(8,128)(2,1)S(1)}, bf16[8,4096]{1,0:T(8,128)(2,1)S(1)}, u32[]{:S(2)}, u32[]{:S(2)}) collective-permute-start(bf16[8,4096]{1,0:T(8,128)(2,1)S(1)} %get-tuple-element.74), channel_id=1, source_target_pairs={{1,0},{2,1},{3,2},{4,3},{5,4},{6,5},{7,6},{8,7},{9,8},{10,9},{11,1... | collective-permute-start | bytes 196616 | tf_op jit(solution)/shard_map/ppermute | solution.py:53
  62.0 5.0 %shard_map.133 = (bf16[128,4096]{1,0:T(8,128)(2,1)}, bf16[128,4096]{1,0:T(8,128)(2,1)}) custom-call(s32[1]{0:T(128)S(6)} %sub.3.half_ref, s32[1,8]{1,0:T(1,128)} %lengths_ref.17, bf16[128,4096]{1,0:T(8,128)(2,1)} %bitcast.32, bf16[128,4096]{1,0:T(8,128)(2,1)} %bitcast.34, bf16[128,2048]{1,0:T(8,128)(2,1)} %get-tuple-element.75.mixed_ref, ...), custom_call_target="tpu_custom_call" | custom-call | bytes 10500000 | tf_op jit(solution)/shard_map/pallas_call | solution.py:299
  67.0 4.9 %all-to-all-done = bf16[16,1,136,128]{3,2,1,0:T(8,128)(2,1)S(1)} async-done(((bf16[16,1,136,128]{3,2,1,0:T(8,128)(2,1)}), bf16[16,1,136,128]{3,2,1,0:T(8,128)(2,1)S(1)}, u32[]{:S(2)}, u32[]{:S(2)}) %all-to-all-start) | async-done | bytes 557088 | tf_op jit(solution)/shard_map/all_to_all | solution.py:377
  72.0 0.7 broadcast_in_dim.33
  72.8 8.5 %all-to-all-start.1 = ((bf16[8,1,136,128]{3,2,1,0:T(8,128)(2,1)}), bf16[8,1,136,128]{3,2,1,0:T(8,128)(2,1)S(1)}, u32[]{:S(2)}, u32[]{:S(2)}) async-start(bf16[8,1,136,128]{3,2,1,0:T(8,128)(2,1)} %broadcast_in_dim.33), calls=%async_computation.1 | async-start | bytes 557056 | tf_op jit(solution)/shard_map/all_to_all | solution.py:377
  81.2 5.0 %shard_map.134 = (bf16[128,4096]{1,0:T(8,128)(2,1)}, bf16[128,4096]{1,0:T(8,128)(2,1)}) custom-call(s32[1]{0:T(128)} %bitcast.half_ref, s32[1,8]{1,0:T(1,128)} %lengths_ref.17, bf16[128,4096]{1,0:T(8,128)(2,1)} %bitcast.33, bf16[128,4096]{1,0:T(8,128)(2,1)} %bitcast.35, bf16[128,2048]{1,0:T(8,128)(2,1)} %copy-done.6, ...), custom_call_target="tpu_custom_call", output_to_operand_aliasing={{0}: (8, {}), {1}: (9, {})} | custom-call | bytes 10500000 | tf_op jit(solution)/shard_map/pallas_call | solution.py:299
  86.2 5.4 %all-to-all-done.1 = bf16[8,1,136,128]{3,2,1,0:T(8,128)(2,1)S(1)} async-done(((bf16[8,1,136,128]{3,2,1,0:T(8,128)(2,1)}), bf16[8,1,136,128]{3,2,1,0:T(8,128)(2,1)S(1)}, u32[]{:S(2)}, u32[]{:S(2)}) %all-to-all-start.1) | async-done | bytes 278560 | tf_op jit(solution)/shard_map/all_to_all | solution.py:377
  91.6 0.9 broadcast_in_dim.37
  92.5 4.1 %all-to-all-start.2 = ((bf16[16,1,136,128]{3,2,1,0:T(8,128)(2,1)}), bf16[16,1,136,128]{3,2,1,0:T(8,128)(2,1)S(1)}, u32[]{:S(2)}, u32[]{:S(2)}) async-start(bf16[16,1,136,128]{3,2,1,0:T(8,128)(2,1)} %broadcast_in_dim.37), calls=%async_computation.2 | async-start | bytes 1114112 | tf_op jit(solution)/shard_map/all_to_all | solution.py:377
  96.7 4.3 %shard_map.135 = bf16[128,4096]{1,0:T(8,128)(2,1)} custom-call(s32[1,8]{1,0:T(1,128)} %lengths_ref.17, bf16[128,4096]{1,0:T(8,128)(2,1)} %copy-done.4, bf16[8,4096]{1,0:T(8,128)(2,1)} %copy-done.14, f32[7,4096]{1,0:T(8,128)} %taps_ref.5), custom_call_target="tpu_custom_call" | custom-call | bytes 14000000 | tf_op jit(solution)/shard_map/pallas_call | solution.py:299
  101.0 4.9 %all-to-all-done.2 = bf16[16,1,136,128]{3,2,1,0:T(8,128)(2,1)S(1)} async-done(((bf16[16,1,136,128]{3,2,1,0:T(8,128)(2,1)}), bf16[16,1,136,128]{3,2,1,0:T(8,128)(2,1)S(1)}, u32[]{:S(2)}, u32[]{:S(2)}) %all-to-all-start.2) | async-done | bytes 557088 | tf_op jit(solution)/shard_map/all_to_all | solution.py:377
  105.8 4.2 %collective-permute-start.6 = (bf16[16,136,128]{2,1,0:T(8,128)(2,1)S(1)}, bf16[16,136,128]{2,1,0:T(8,128)(2,1)S(1)}, u32[]{:S(2)}, u32[]{:S(2)}) collective-permute-start(bf16[16,136,128]{2,1,0:T(8,128)(2,1)S(1)} %bitcast.30), channel_id=1, source_target_pairs={{0,32},{32,0},{1,33},{33,1},{2,34},{34,2},{3,35},{35,3},{4,36},{36... | collective-permute-start | bytes 1671176 | tf_op jit(solution)/shard_map/ppermute | solution.py:389
  110.0 1.6 %collective-permute-done.6.other_ref = bf16[16,136,128]{2,1,0:T(8,128)(2,1)S(1)} collective-permute-done((bf16[16,136,128]{2,1,0:T(8,128)(2,1)S(1)}, bf16[16,136,128]{2,1,0:T(8,128)(2,1)S(1)}, u32[]{:S(2)}, u32[]{:S(2)}) %collective-permute-start.6) | collective-permute-done | bytes 557088 | tf_op jit(solution)/shard_map/ppermute | solution.py:389
  111.6 1.5 %shard_map.136 = (f32[7,4096]{1,0:T(8,128)}, f32[128,4096]{1,0:T(8,128)}) custom-call(bf16[16,136,128]{2,1,0:T(8,128)(2,1)S(1)} %bitcast.31, bf16[16,136,128]{2,1,0:T(8,128)(2,1)S(1)} %collective-permute-done.6.other_ref), custom_call_target="tpu_custom_call" | custom-call | bytes 10500000 | tf_op jit(solution)/shard_map/pallas_call | solution.py:299
  (36 shorter events, 0.8 us)
Async XLA Ops:
  1.5 16.0 %copy-start = (f32[128,4096]{1,0:T(8,128)S(1)}, f32[128,4096]{1,0:T(8,128)}, u32[]{:S(2)}) copy-start(f32[128,4096]{1,0:T(8,128)} %ltaps_ref.11) | copy-start | bytes 6291460
  1.5 16.0 %copy-start.13 = (s32[1,8]{1,0:T(1,128)S(1)}, s32[1,8]{1,0:T(1,128)}, u32[]{:S(2)}) copy-start(s32[1,8]{1,0:T(1,128)} %lengths_ref.17) | copy-start | bytes 100
  1.5 5.9 %collective-permute-start = (bf16[8,4096]{1,0:T(8,128)(2,1)S(1)}, bf16[8,4096]{1,0:T(8,128)(2,1)S(1)}, u32[]{:S(2)}, u32[]{:S(2)}) collective-permute-start(bf16[8,4096]{1,0:T(8,128)(2,1)S(1)} %slice_bitcast_fusion), channel_id=1, source_target_pairs={{0,1},{1,2},{2,3},{3,4},{4,5},{5,6},{6,7},{7,8},{8,9},{9,10},{10,1... | collective-permute-start | bytes 196616 | tf_op jit(solution)/shard_map/ppermute | solution.py:53
  7.4 10.1 %copy-start.1 = (bf16[1280,256]{1,0:T(8,128)(2,1)S(1)}, bf16[1280,256]{1,0:T(8,128)(2,1)}, u32[]{:S(2)}) copy-start(bf16[1280,256]{1,0:T(8,128)(2,1)} %constant.16.clone.table_ref) | copy-start | bytes 1966084
  7.4 0.6 copy-start.10
  12.0 10.6 %copy-start.2 = (bf16[1,128,4096]{2,1,0:T(8,128)(2,1)S(1)}, bf16[1,128,4096]{2,1,0:T(8,128)(2,1)}, u32[]{:S(2)}) copy-start(bf16[1,128,4096]{2,1,0:T(8,128)(2,1)} %param.9) | copy-start | bytes 3145732
  12.0 10.6 %copy-start.3 = (bf16[1,128,4096]{2,1,0:T(8,128)(2,1)S(1)}, bf16[1,128,4096]{2,1,0:T(8,128)(2,1)}, u32[]{:S(2)}) copy-start(bf16[1,128,4096]{2,1,0:T(8,128)(2,1)} %param.10) | copy-start | bytes 3145732
  12.0 10.6 %copy-start.5 = (f32[7,4096]{1,0:T(8,128)S(1)}, f32[7,4096]{1,0:T(8,128)}, u32[]{:S(2)}) copy-start(f32[7,4096]{1,0:T(8,128)} %taps_ref.5) | copy-start | bytes 344068
  12.0 25.3 %collective-permute-start.2 = (bf16[128,4096]{1,0:T(8,128)(2,1)S(1)}, bf16[128,4096]{1,0:T(8,128)(2,1)S(1)}, u32[]{:S(2)}, u32[]{:S(2)}) collective-permute-start(bf16[128,4096]{1,0:T(8,128)(2,1)S(1)} %multiply_convert_fusion.adj_ref), channel_id=1, source_target_pairs={{1,0},{2,1},{3,2},{4,3},{5,4},{6,5},{7,6},{8,7},{9,8},{10,9},{11,1... | collective-permute-start | bytes 3145736 | tf_op jit(solution)/shard_map/ppermute | solution.py:53
  13.4 19.4 %collective-permute-start.1 = (bf16[128,2048]{1,0:T(8,128)(2,1)}, bf16[128,2048]{1,0:T(8,128)(2,1)S(1)}, u32[]{:S(2)}, u32[]{:S(2)}) collective-permute-start(bf16[128,2048]{1,0:T(8,128)(2,1)} %get-tuple-element.75.mixed_ref), channel_id=1, source_target_pairs={{0,1},{1,2},{2,3},{3,4},{4,5},{5,6},{6,7},{7,8},{8,9},{9,10},{10,1... | collective-permute-start | bytes 1572872 | tf_op jit(solution)/shard_map/ppermute | solution.py:53
  17.5 1.0 copy-start.8
  18.5 4.1 %copy-start.11 = (bf16[8,4096]{1,0:T(8,128)(2,1)S(1)}, bf16[8,4096]{1,0:T(8,128)(2,1)}, u32[]{:S(2)}) copy-start(bf16[8,4096]{1,0:T(8,128)(2,1)} %copy-done.10) | copy-start | bytes 196612
  25.4 7.4 %copy-start.6 = (bf16[128,2048]{1,0:T(8,128)(2,1)}, bf16[128,2048]{1,0:T(8,128)(2,1)S(1)}, u32[]{:S(2)}) copy-start(bf16[128,2048]{1,0:T(8,128)(2,1)S(1)} %get-tuple-element.80.mixed_ref) | copy-start | bytes 1572868
  25.4 11.9 %copy-start.12 = (f32[128,2048]{1,0:T(8,128)S(1)}, f32[128,2048]{1,0:T(8,128)}, u32[]{:S(2)}) copy-start(f32[128,2048]{1,0:T(8,128)} %get-tuple-element.61.short_ref) | copy-start | bytes 3145732
  25.4 16.9 %collective-permute-start.3 = (bf16[128,2048]{1,0:T(8,128)(2,1)S(1)}, bf16[128,2048]{1,0:T(8,128)(2,1)S(1)}, u32[]{:S(2)}, u32[]{:S(2)}) collective-permute-start(bf16[128,2048]{1,0:T(8,128)(2,1)S(1)} %get-tuple-element.80.mixed_ref), channel_id=1, source_target_pairs={{0,1},{1,2},{2,3},{3,4},{4,5},{5,6},{6,7},{7,8},{8,9},{9,10},{10,1... | collective-permute-start | bytes 1572872 | tf_op jit(solution)/shard_map/ppermute | solution.py:53
  32.8 9.5 %copy-start.9 = (bf16[128,2048]{1,0:T(8,128)(2,1)}, bf16[128,2048]{1,0:T(8,128)(2,1)S(1)}, u32[]{:S(2)}) copy-start(bf16[128,2048]{1,0:T(8,128)(2,1)S(1)} %collective-permute-done.1.prev_ref) | copy-start | bytes 1572868
  42.3 7.3 %copy-start.7 = (bf16[128,2048]{1,0:T(8,128)(2,1)}, bf16[128,2048]{1,0:T(8,128)(2,1)S(1)}, u32[]{:S(2)}) copy-start(bf16[128,2048]{1,0:T(8,128)(2,1)S(1)} %collective-permute-done.3.prev_ref) | copy-start | bytes 1572868
  42.3 8.3 %collective-permute-start.4 = (bf16[16,136,128]{2,1,0:T(8,128)(2,1)S(1)}, bf16[16,136,128]{2,1,0:T(8,128)(2,1)S(1)}, u32[]{:S(2)}, u32[]{:S(2)}) collective-permute-start(bf16[16,136,128]{2,1,0:T(8,128)(2,1)S(1)} %get-tuple-element.71), channel_id=1, source_target_pairs={{0,32},{32,0},{1,33},{33,1},{2,34},{34,2},{3,35},{35,3},{4,36},{36... | collective-permute-start | bytes 1671176 | tf_op jit(solution)/shard_map/ppermute | solution.py:389
  49.6 1.0 copy-start.4
  51.6 20.3 %all-to-all-start = ((bf16[16,1,136,128]{3,2,1,0:T(8,128)(2,1)}), bf16[16,1,136,128]{3,2,1,0:T(8,128)(2,1)S(1)}, u32[]{:S(2)}, u32[]{:S(2)}) async-start(bf16[16,1,136,128]{3,2,1,0:T(8,128)(2,1)} %bitcast.7), calls=%async_computation | async-start | bytes 1114112 | tf_op jit(solution)/shard_map/all_to_all | solution.py:377
  60.5 11.5 %collective-permute-start.5 = (bf16[8,4096]{1,0:T(8,128)(2,1)S(1)}, bf16[8,4096]{1,0:T(8,128)(2,1)S(1)}, u32[]{:S(2)}, u32[]{:S(2)}) collective-permute-start(bf16[8,4096]{1,0:T(8,128)(2,1)S(1)} %get-tuple-element.74), channel_id=1, source_target_pairs={{1,0},{2,1},{3,2},{4,3},{5,4},{6,5},{7,6},{8,7},{9,8},{10,9},{11,1... | collective-permute-start | bytes 196616 | tf_op jit(solution)/shard_map/ppermute | solution.py:53
  72.0 14.2 %copy-start.14 = (bf16[8,4096]{1,0:T(8,128)(2,1)}, bf16[8,4096]{1,0:T(8,128)(2,1)S(1)}, u32[]{:S(2)}) copy-start(bf16[8,4096]{1,0:T(8,128)(2,1)S(1)} %collective-permute-done.5.after_ref) | copy-start | bytes 196612
  72.8 18.8 %all-to-all-start.1 = ((bf16[8,1,136,128]{3,2,1,0:T(8,128)(2,1)}), bf16[8,1,136,128]{3,2,1,0:T(8,128)(2,1)S(1)}, u32[]{:S(2)}, u32[]{:S(2)}) async-start(bf16[8,1,136,128]{3,2,1,0:T(8,128)(2,1)} %broadcast_in_dim.33), calls=%async_computation.1 | async-start | bytes 557056 | tf_op jit(solution)/shard_map/all_to_all | solution.py:377
  92.5 13.3 %all-to-all-start.2 = ((bf16[16,1,136,128]{3,2,1,0:T(8,128)(2,1)}), bf16[16,1,136,128]{3,2,1,0:T(8,128)(2,1)S(1)}, u32[]{:S(2)}, u32[]{:S(2)}) async-start(bf16[16,1,136,128]{3,2,1,0:T(8,128)(2,1)} %broadcast_in_dim.37), calls=%async_computation.2 | async-start | bytes 1114112 | tf_op jit(solution)/shard_map/all_to_all | solution.py:377
  105.8 5.8 %collective-permute-start.6 = (bf16[16,136,128]{2,1,0:T(8,128)(2,1)S(1)}, bf16[16,136,128]{2,1,0:T(8,128)(2,1)S(1)}, u32[]{:S(2)}, u32[]{:S(2)}) collective-permute-start(bf16[16,136,128]{2,1,0:T(8,128)(2,1)S(1)} %bitcast.30), channel_id=1, source_target_pairs={{0,32},{32,0},{1,33},{33,1},{2,34},{34,2},{3,35},{35,3},{4,36},{36... | collective-permute-start | bytes 1671176 | tf_op jit(solution)/shard_map/ppermute | solution.py:389

commit v6 on v5

--- a/solution.py
+++ b/solution.py
@@ -402,13 +402,13 @@
 
     before = passed_along(v[rows - RIM :], 1)
     adj = (up.astype(F32) * gl.astype(F32)).astype(BF)
+    before, adj = together((before, adj))
+    following = passed_along(adj, -1)
     mixed_a, short_a = k.mix(given, lengths, v, before, gs, short_taps, 56)
-    mixed_a, adj = together((mixed_a, adj))
     prev_a = passed_along(mixed_a, 1)
-    following = passed_along(adj, -1)
+    back_a, terms_a = k.own(given, lengths, mixed_a, adj, long_taps)
+    before, back_a = together((before, back_a))
     mixed_b, short_b = k.mix(kept, lengths, v, before, gs, short_taps, 20)
-    back_a, terms_a = k.own(given, lengths, mixed_a, adj, long_taps)
-    mixed_b, back_a = together((mixed_b, back_a))
     prev_b = passed_along(mixed_b, 1)
     back_b, terms_b = k.own(kept, lengths, mixed_b, adj, long_taps)
     prev_a, back_b = together((prev_a, back_b))

time: 115 us -> 114 us (level); the launches traced: 113 us -> 115 us
  starting transfers between devices: 42.4 us -> 47.9 us
  waiting for transfers between devices: 21.2 us -> 17.6 us
    all_to_all x3, starting transfers between devices: 21.6 us -> 28.9 us  [traded(): return lax.all_to_all(block, axes, 0, 0, tiled=True)]
    ppermute x5, waiting for transfers between devices: 4.48 us -> 0.33 us  [passed_along(): return lax.ppermute(block, CTX, route)]
    ppermute x2, starting transfers between devices: 6.54 us -> 4.64 us  [swapped(): return lax.ppermute(block, 'core', [(0, 1), (1, 0)])]
  transfers between devices with their start and end apart: 10 -> 10, of which waited for: 5 -> 5; matrix products, arithmetic and copies ran while one was open for 2% -> 2% of each run, Pallas kernels for 31% -> 35%
where the time goes in v6:
time: 114 us; the launch traced here: 115 us
  starting transfers between devices  47.9 us (42%)
  Pallas kernels  41.3 us (36%)
  waiting for transfers between devices  17.6 us (15%)
  local copies, waits for them, and re-layouts  4.55 us (4%)
  other arithmetic  2.9 us (3%)
    pallas_call x10, Pallas kernels, call(): pl.pallas_call(kernel, grid_spec=pltpu.PrefetchScalarGridSpec(num_scalar_...  41.3 us
    all_to_all x3, starting transfers between devices, traded(): return lax.all_to_all(block, axes, 0, 0, tiled=True)  28.9 us
    all_to_all x3, waiting for transfers between devices, traded(): return lax.all_to_all(block, axes, 0, 0, tiled=True)  15.7 us
    ppermute x5, starting transfers between devices, passed_along(): return lax.ppermute(block, CTX, route)  14.3 us
    ppermute x2, starting transfers between devices, swapped(): return lax.ppermute(block, 'core', [(0, 1), (1, 0)])  4.64 us
  transfers between devices with their start and end apart: 10, of which 5 were waited for; matrix products, arithmetic and copies ran while one was open for 2% of the time, Pallas kernels for 35%

profile of v6, /device:TPU:1, one launch (start us, length us, event | category | flops | bytes accessed | tf_op | source)
XLA Modules:
  0.0 115.1 jit_solution(7157958336568653613)
XLA Ops:
  0.6 0.8 slice_bitcast_fusion
  1.5 4.1 %collective-permute-start = (bf16[8,4096]{1,0:T(8,128)(2,1)S(1)}, bf16[8,4096]{1,0:T(8,128)(2,1)S(1)}, u32[]{:S(2)}, u32[]{:S(2)}) collective-permute-start(bf16[8,4096]{1,0:T(8,128)(2,1)S(1)} %slice_bitcast_fusion), channel_id=1, source_target_pairs={{0,1},{1,2},{2,3},{3,4},{4,5},{5,6},{6,7},{7,8},{8,9},{9,10},{10,1... | collective-permute-start | bytes 196616 | tf_op jit(solution)/shard_map/ppermute | solution.py:53
  5.6 1.8 %multiply_convert_fusion.adj_ref = bf16[128,4096]{1,0:T(8,128)(2,1)S(1)} fusion(bf16[1,128,4096]{2,1,0:T(8,128)(2,1)} %param.11, bf16[1,128,4096]{2,1,0:T(8,128)(2,1)} %param.14), kind=kLoop, calls=%fused_computation | loop fusion | flops 2097152 | bytes 3145728 | tf_op jit(solution)/shard_map/convert_element_type | solution.py:404
  7.4 1.3 %collective-permute-start.2 = (bf16[128,4096]{1,0:T(8,128)(2,1)S(1)}, bf16[128,4096]{1,0:T(8,128)(2,1)}, u32[]{:S(2)}, u32[]{:S(2)}) collective-permute-start(bf16[128,4096]{1,0:T(8,128)(2,1)S(1)} %multiply_convert_fusion.adj_ref), channel_id=1, source_target_pairs={{1,0},{2,1},{3,2},{4,3},{5,4},{6,5},{7,6},{8,7},{9,8},{10,9},{11,1... | collective-permute-start | bytes 3145736 | tf_op jit(solution)/shard_map/ppermute | solution.py:53
  8.7 4.1 %shard_map.127 = (bf16[128,2048]{1,0:T(8,128)(2,1)}, f32[128,2048]{1,0:T(8,128)}) custom-call(s32[1]{0:T(128)S(6)} %sub.3.half_ref, s32[1,8]{1,0:T(1,128)} %lengths_ref.17, bf16[128,4096]{1,0:T(8,128)(2,1)} %bitcast.22, bf16[8,4096]{1,0:T(8,128)(2,1)} %copy-done.10, bf16[128,4096]{1,0:T(8,128)(2,1)} %bitcast.26, f32[7,4096]{1,0:T(8,128)} %taps_ref.5), custom_call_target="tpu_custom_call" | custom-call | bytes 10500000 | tf_op jit(solution)/shard_map/pallas_call | solution.py:299
  12.8 4.2 %collective-permute-start.1 = (bf16[128,2048]{1,0:T(8,128)(2,1)}, bf16[128,2048]{1,0:T(8,128)(2,1)S(1)}, u32[]{:S(2)}, u32[]{:S(2)}) collective-permute-start(bf16[128,2048]{1,0:T(8,128)(2,1)} %get-tuple-element.75.mixed_ref), channel_id=1, source_target_pairs={{0,1},{1,2},{2,3},{3,4},{4,5},{5,6},{6,7},{7,8},{8,9},{9,10},{10,1... | collective-permute-start | bytes 1572872 | tf_op jit(solution)/shard_map/ppermute | solution.py:53
  17.0 1.0 copy-done.8
  18.0 4.0 %shard_map.128 = (f32[128,2048]{1,0:T(8,128)S(1)}, f32[128,2048]{1,0:T(8,128)S(1)}) custom-call(s32[1]{0:T(128)S(6)} %sub.3.half_ref, s32[1,8]{1,0:T(1,128)S(1)} %copy-done.13, bf16[128,2048]{1,0:T(8,128)(2,1)S(1)} %copy-done.8, bf16[128,4096]{1,0:T(8,128)(2,1)S(1)} %multiply_convert_fusion.adj_ref, f32[128,4096]{1,0:T(8,128)S(1)} %copy-done, ...), custom_call_target="tpu_custom_call" | custom-call | bytes 5250000 | tf_op jit(solution)/shard_map/pallas_call | solution.py:299
  22.1 2.8 %shard_map.129 = (bf16[128,2048]{1,0:T(8,128)(2,1)S(1)}, f32[128,2048]{1,0:T(8,128)S(1)}) custom-call(s32[1]{0:T(128)} %bitcast.half_ref, s32[1,8]{1,0:T(1,128)S(1)} %copy-done.13, bf16[128,4096]{1,0:T(8,128)(2,1)S(1)} %bitcast.23, bf16[8,4096]{1,0:T(8,128)(2,1)S(1)} %copy-done.11, bf16[128,4096]{1,0:T(8,128)(2,1)S(1)} %bitcast.27, f32[7,4096]{1,0:T(8,128)S(1)} %copy-done.5), custom_call_target="tpu_custom_call" | custom-call | bytes 10500000 | tf_op jit(solution)/shard_map/pallas_call | solution.py:299
  24.9 3.3 %collective-permute-start.3 = (bf16[128,2048]{1,0:T(8,128)(2,1)S(1)}, bf16[128,2048]{1,0:T(8,128)(2,1)S(1)}, u32[]{:S(2)}, u32[]{:S(2)}) collective-permute-start(bf16[128,2048]{1,0:T(8,128)(2,1)S(1)} %get-tuple-element.80.mixed_ref), channel_id=1, source_target_pairs={{0,1},{1,2},{2,3},{3,4},{4,5},{5,6},{6,7},{7,8},{8,9},{9,10},{10,1... | collective-permute-start | bytes 1572872 | tf_op jit(solution)/shard_map/ppermute | solution.py:53
  28.3 4.1 %shard_map.130 = (f32[128,2048]{1,0:T(8,128)S(1)}, f32[128,2048]{1,0:T(8,128)S(1)}) custom-call(s32[1]{0:T(128)} %bitcast.half_ref, s32[1,8]{1,0:T(1,128)S(1)} %copy-done.13, bf16[128,2048]{1,0:T(8,128)(2,1)S(1)} %get-tuple-element.80.mixed_ref, bf16[128,4096]{1,0:T(8,128)(2,1)S(1)} %multiply_convert_fusion.adj_ref, f32[128,4096]{1,0:T(8,128)S(1)} %copy-done, ...), custom_call_target="tpu_custom_call" | custom-call | bytes 5250000 | tf_op jit(solution)/shard_map/pallas_call | solution.py:299
  32.4 0.3 collective-permute-done.2.next_ref
  32.7 5.3 %shard_map.131 = (bf16[128,4096]{1,0:T(8,128)(2,1)}, bf16[128,4096]{1,0:T(8,128)(2,1)S(1)}, bf16[8,4096]{1,0:T(8,128)(2,1)S(1)}, bf16[16,136,128]{2,1,0:T(8,128)(2,1)S(1)}) custom-call(s32[1]{0:T(128)S(6)} %sub.3.half_ref, s32[1,8]{1,0:T(1,128)S(1)} %copy-done.13, bf16[128,4096]{1,0:T(8,128)(2,1)S(1)} %bitcast.24, bf16[8,4096]{1,0:T(8,128)(2,1)S(1)} %copy-done.11, ...), custom_call_target="tpu_custom_call" | custom-call | bytes 5250000 | tf_op jit(solution)/shard_map/pallas_call | solution.py:299
  38.0 2.5 %collective-permute-start.4 = (bf16[16,136,128]{2,1,0:T(8,128)(2,1)S(1)}, bf16[16,136,128]{2,1,0:T(8,128)(2,1)S(1)}, u32[]{:S(2)}, u32[]{:S(2)}) collective-permute-start(bf16[16,136,128]{2,1,0:T(8,128)(2,1)S(1)} %get-tuple-element.71), channel_id=1, source_target_pairs={{0,32},{32,0},{1,33},{33,1},{2,34},{34,2},{3,35},{35,3},{4,36},{36... | collective-permute-start | bytes 1671176 | tf_op jit(solution)/shard_map/ppermute | solution.py:389
  40.5 5.3 %shard_map.132 = (bf16[128,4096]{1,0:T(8,128)(2,1)}, bf16[128,4096]{1,0:T(8,128)(2,1)S(1)}, bf16[8,4096]{1,0:T(8,128)(2,1)S(1)}, bf16[16,136,128]{2,1,0:T(8,128)(2,1)S(1)}) custom-call(s32[1]{0:T(128)} %bitcast.half_ref, s32[1,8]{1,0:T(1,128)S(1)} %copy-done.13, ...), custom_call_target="tpu_custom_call", output_to_operand_aliasing={{0}: (14, {}), {1}: (15, {}), {2}: (16, {})} | custom-call | bytes 5250000 | tf_op jit(solution)/shard_map/pallas_call | solution.py:299
  45.8 1.0 copy-done.4
  46.8 1.0 add_convert_fusion
  47.7 11.5 %all-to-all-start = ((bf16[16,1,136,128]{3,2,1,0:T(8,128)(2,1)}), bf16[16,1,136,128]{3,2,1,0:T(8,128)(2,1)S(1)}, u32[]{:S(2)}, u32[]{:S(2)}) async-start(bf16[16,1,136,128]{3,2,1,0:T(8,128)(2,1)} %bitcast.7), calls=%async_computation | async-start | bytes 1114112 | tf_op jit(solution)/shard_map/all_to_all | solution.py:377
  59.2 1.5 %collective-permute-start.5 = (bf16[8,4096]{1,0:T(8,128)(2,1)S(1)}, bf16[8,4096]{1,0:T(8,128)(2,1)S(1)}, u32[]{:S(2)}, u32[]{:S(2)}) collective-permute-start(bf16[8,4096]{1,0:T(8,128)(2,1)S(1)} %get-tuple-element.74), channel_id=1, source_target_pairs={{1,0},{2,1},{3,2},{4,3},{5,4},{6,5},{7,6},{8,7},{9,8},{10,9},{11,1... | collective-permute-start | bytes 196616 | tf_op jit(solution)/shard_map/ppermute | solution.py:53
  60.7 5.0 %shard_map.133 = (bf16[128,4096]{1,0:T(8,128)(2,1)}, bf16[128,4096]{1,0:T(8,128)(2,1)}) custom-call(s32[1]{0:T(128)S(6)} %sub.3.half_ref, s32[1,8]{1,0:T(1,128)} %lengths_ref.17, bf16[128,4096]{1,0:T(8,128)(2,1)} %bitcast.32, bf16[128,4096]{1,0:T(8,128)(2,1)} %bitcast.34, bf16[128,2048]{1,0:T(8,128)(2,1)} %get-tuple-element.75.mixed_ref, ...), custom_call_target="tpu_custom_call" | custom-call | bytes 10500000 | tf_op jit(solution)/shard_map/pallas_call | solution.py:299
  65.7 4.9 %all-to-all-done = bf16[16,1,136,128]{3,2,1,0:T(8,128)(2,1)S(1)} async-done(((bf16[16,1,136,128]{3,2,1,0:T(8,128)(2,1)}), bf16[16,1,136,128]{3,2,1,0:T(8,128)(2,1)S(1)}, u32[]{:S(2)}, u32[]{:S(2)}) %all-to-all-start) | async-done | bytes 557088 | tf_op jit(solution)/shard_map/all_to_all | solution.py:377
  70.7 0.7 broadcast_in_dim.33
  71.5 10.4 %all-to-all-start.1 = ((bf16[8,1,136,128]{3,2,1,0:T(8,128)(2,1)}), bf16[8,1,136,128]{3,2,1,0:T(8,128)(2,1)S(1)}, u32[]{:S(2)}, u32[]{:S(2)}) async-start(bf16[8,1,136,128]{3,2,1,0:T(8,128)(2,1)} %broadcast_in_dim.33), calls=%async_computation.1 | async-start | bytes 557056 | tf_op jit(solution)/shard_map/all_to_all | solution.py:377
  81.9 5.0 %shard_map.134 = (bf16[128,4096]{1,0:T(8,128)(2,1)}, bf16[128,4096]{1,0:T(8,128)(2,1)}) custom-call(s32[1]{0:T(128)} %bitcast.half_ref, s32[1,8]{1,0:T(1,128)} %lengths_ref.17, bf16[128,4096]{1,0:T(8,128)(2,1)} %bitcast.33, bf16[128,4096]{1,0:T(8,128)(2,1)} %bitcast.35, bf16[128,2048]{1,0:T(8,128)(2,1)} %copy-done.6, ...), custom_call_target="tpu_custom_call", output_to_operand_aliasing={{0}: (8, {}), {1}: (9, {})} | custom-call | bytes 10500000 | tf_op jit(solution)/shard_map/pallas_call | solution.py:299
  86.9 4.3 %all-to-all-done.1 = bf16[8,1,136,128]{3,2,1,0:T(8,128)(2,1)S(1)} async-done(((bf16[8,1,136,128]{3,2,1,0:T(8,128)(2,1)}), bf16[8,1,136,128]{3,2,1,0:T(8,128)(2,1)S(1)}, u32[]{:S(2)}, u32[]{:S(2)}) %all-to-all-start.1) | async-done | bytes 278560 | tf_op jit(solution)/shard_map/all_to_all | solution.py:377
  91.3 0.9 broadcast_in_dim.37
  92.2 7.1 %all-to-all-start.2 = ((bf16[16,1,136,128]{3,2,1,0:T(8,128)(2,1)}), bf16[16,1,136,128]{3,2,1,0:T(8,128)(2,1)S(1)}, u32[]{:S(2)}, u32[]{:S(2)}) async-start(bf16[16,1,136,128]{3,2,1,0:T(8,128)(2,1)} %broadcast_in_dim.37), calls=%async_computation.2 | async-start | bytes 1114112 | tf_op jit(solution)/shard_map/all_to_all | solution.py:377
  99.2 4.3 %shard_map.135 = bf16[128,4096]{1,0:T(8,128)(2,1)} custom-call(s32[1,8]{1,0:T(1,128)} %lengths_ref.17, bf16[128,4096]{1,0:T(8,128)(2,1)} %copy-done.4, bf16[8,4096]{1,0:T(8,128)(2,1)} %copy-done.14, f32[7,4096]{1,0:T(8,128)} %taps_ref.5), custom_call_target="tpu_custom_call" | custom-call | bytes 14000000 | tf_op jit(solution)/shard_map/pallas_call | solution.py:299
  103.5 6.4 %all-to-all-done.2 = bf16[16,1,136,128]{3,2,1,0:T(8,128)(2,1)S(1)} async-done(((bf16[16,1,136,128]{3,2,1,0:T(8,128)(2,1)}), bf16[16,1,136,128]{3,2,1,0:T(8,128)(2,1)S(1)}, u32[]{:S(2)}, u32[]{:S(2)}) %all-to-all-start.2) | async-done | bytes 557088 | tf_op jit(solution)/shard_map/all_to_all | solution.py:377
  110.0 2.1 %collective-permute-start.6 = (bf16[16,136,128]{2,1,0:T(8,128)(2,1)S(1)}, bf16[16,136,128]{2,1,0:T(8,128)(2,1)S(1)}, u32[]{:S(2)}, u32[]{:S(2)}) collective-permute-start(bf16[16,136,128]{2,1,0:T(8,128)(2,1)S(1)} %bitcast.30), channel_id=1, source_target_pairs={{0,32},{32,0},{1,33},{33,1},{2,34},{34,2},{3,35},{35,3},{4,36},{36... | collective-permute-start | bytes 1671176 | tf_op jit(solution)/shard_map/ppermute | solution.py:389
  112.1 1.6 %collective-permute-done.6.other_ref = bf16[16,136,128]{2,1,0:T(8,128)(2,1)S(1)} collective-permute-done((bf16[16,136,128]{2,1,0:T(8,128)(2,1)S(1)}, bf16[16,136,128]{2,1,0:T(8,128)(2,1)S(1)}, u32[]{:S(2)}, u32[]{:S(2)}) %collective-permute-start.6) | collective-permute-done | bytes 557088 | tf_op jit(solution)/shard_map/ppermute | solution.py:389
  113.7 1.5 %shard_map.136 = (f32[7,4096]{1,0:T(8,128)}, f32[128,4096]{1,0:T(8,128)}) custom-call(bf16[16,136,128]{2,1,0:T(8,128)(2,1)S(1)} %bitcast.31, bf16[16,136,128]{2,1,0:T(8,128)(2,1)S(1)} %collective-permute-done.6.other_ref), custom_call_target="tpu_custom_call" | custom-call | bytes 10500000 | tf_op jit(solution)/shard_map/pallas_call | solution.py:299
  (36 shorter events, 0.2 us)
Async XLA Ops:
  1.5 15.5 %copy-start = (f32[128,4096]{1,0:T(8,128)S(1)}, f32[128,4096]{1,0:T(8,128)}, u32[]{:S(2)}) copy-start(f32[128,4096]{1,0:T(8,128)} %ltaps_ref.11) | copy-start | bytes 6291460
  1.5 15.5 %copy-start.13 = (s32[1,8]{1,0:T(1,128)S(1)}, s32[1,8]{1,0:T(1,128)}, u32[]{:S(2)}) copy-start(s32[1,8]{1,0:T(1,128)} %lengths_ref.17) | copy-start | bytes 100
  1.5 5.9 %collective-permute-start = (bf16[8,4096]{1,0:T(8,128)(2,1)S(1)}, bf16[8,4096]{1,0:T(8,128)(2,1)S(1)}, u32[]{:S(2)}, u32[]{:S(2)}) collective-permute-start(bf16[8,4096]{1,0:T(8,128)(2,1)S(1)} %slice_bitcast_fusion), channel_id=1, source_target_pairs={{0,1},{1,2},{2,3},{3,4},{4,5},{5,6},{6,7},{7,8},{8,9},{9,10},{10,1... | collective-permute-start | bytes 196616 | tf_op jit(solution)/shard_map/ppermute | solution.py:53
  7.4 1.3 %copy-start.10 = (bf16[8,4096]{1,0:T(8,128)(2,1)}, bf16[8,4096]{1,0:T(8,128)(2,1)S(1)}, u32[]{:S(2)}) copy-start(bf16[8,4096]{1,0:T(8,128)(2,1)S(1)} %collective-permute-done.before_ref) | copy-start | bytes 196612
  7.4 25.3 %collective-permute-start.2 = (bf16[128,4096]{1,0:T(8,128)(2,1)S(1)}, bf16[128,4096]{1,0:T(8,128)(2,1)}, u32[]{:S(2)}, u32[]{:S(2)}) collective-permute-start(bf16[128,4096]{1,0:T(8,128)(2,1)S(1)} %multiply_convert_fusion.adj_ref), channel_id=1, source_target_pairs={{1,0},{2,1},{3,2},{4,3},{5,4},{6,5},{7,6},{8,7},{9,8},{10,9},{11,1... | collective-permute-start | bytes 3145736 | tf_op jit(solution)/shard_map/ppermute | solution.py:53
  8.7 8.3 %copy-start.1 = (bf16[1280,256]{1,0:T(8,128)(2,1)S(1)}, bf16[1280,256]{1,0:T(8,128)(2,1)}, u32[]{:S(2)}) copy-start(bf16[1280,256]{1,0:T(8,128)(2,1)} %constant.16.clone.table_ref) | copy-start | bytes 1966084
  12.8 9.3 %copy-start.2 = (bf16[1,128,4096]{2,1,0:T(8,128)(2,1)S(1)}, bf16[1,128,4096]{2,1,0:T(8,128)(2,1)}, u32[]{:S(2)}) copy-start(bf16[1,128,4096]{2,1,0:T(8,128)(2,1)} %param.9) | copy-start | bytes 3145732
  12.8 9.3 %copy-start.3 = (bf16[1,128,4096]{2,1,0:T(8,128)(2,1)S(1)}, bf16[1,128,4096]{2,1,0:T(8,128)(2,1)}, u32[]{:S(2)}) copy-start(bf16[1,128,4096]{2,1,0:T(8,128)(2,1)} %param.10) | copy-start | bytes 3145732
  12.8 9.3 %copy-start.5 = (f32[7,4096]{1,0:T(8,128)S(1)}, f32[7,4096]{1,0:T(8,128)}, u32[]{:S(2)}) copy-start(f32[7,4096]{1,0:T(8,128)} %taps_ref.5) | copy-start | bytes 344068
  12.8 19.5 %collective-permute-start.1 = (bf16[128,2048]{1,0:T(8,128)(2,1)}, bf16[128,2048]{1,0:T(8,128)(2,1)S(1)}, u32[]{:S(2)}, u32[]{:S(2)}) collective-permute-start(bf16[128,2048]{1,0:T(8,128)(2,1)} %get-tuple-element.75.mixed_ref), channel_id=1, source_target_pairs={{0,1},{1,2},{2,3},{3,4},{4,5},{5,6},{6,7},{7,8},{8,9},{9,10},{10,1... | collective-permute-start | bytes 1572872 | tf_op jit(solution)/shard_map/ppermute | solution.py:53
  17.0 1.0 copy-start.8
  18.0 4.1 %copy-start.11 = (bf16[8,4096]{1,0:T(8,128)(2,1)S(1)}, bf16[8,4096]{1,0:T(8,128)(2,1)}, u32[]{:S(2)}) copy-start(bf16[8,4096]{1,0:T(8,128)(2,1)} %copy-done.10) | copy-start | bytes 196612
  24.9 7.4 %copy-start.6 = (bf16[128,2048]{1,0:T(8,128)(2,1)}, bf16[128,2048]{1,0:T(8,128)(2,1)S(1)}, u32[]{:S(2)}) copy-start(bf16[128,2048]{1,0:T(8,128)(2,1)S(1)} %get-tuple-element.80.mixed_ref) | copy-start | bytes 1572868
  24.9 7.8 %copy-start.12 = (f32[128,2048]{1,0:T(8,128)S(1)}, f32[128,2048]{1,0:T(8,128)}, u32[]{:S(2)}) copy-start(f32[128,2048]{1,0:T(8,128)} %get-tuple-element.61.short_ref) | copy-start | bytes 3145732
  24.9 13.0 %collective-permute-start.3 = (bf16[128,2048]{1,0:T(8,128)(2,1)S(1)}, bf16[128,2048]{1,0:T(8,128)(2,1)S(1)}, u32[]{:S(2)}, u32[]{:S(2)}) collective-permute-start(bf16[128,2048]{1,0:T(8,128)(2,1)S(1)} %get-tuple-element.80.mixed_ref), channel_id=1, source_target_pairs={{0,1},{1,2},{2,3},{3,4},{4,5},{5,6},{6,7},{7,8},{8,9},{9,10},{10,1... | collective-permute-start | bytes 1572872 | tf_op jit(solution)/shard_map/ppermute | solution.py:53
  32.4 5.6 %copy-start.9 = (bf16[128,2048]{1,0:T(8,128)(2,1)}, bf16[128,2048]{1,0:T(8,128)(2,1)S(1)}, u32[]{:S(2)}) copy-start(bf16[128,2048]{1,0:T(8,128)(2,1)S(1)} %collective-permute-done.1.prev_ref) | copy-start | bytes 1572868
  38.0 7.8 %copy-start.7 = (bf16[128,2048]{1,0:T(8,128)(2,1)}, bf16[128,2048]{1,0:T(8,128)(2,1)S(1)}, u32[]{:S(2)}) copy-start(bf16[128,2048]{1,0:T(8,128)(2,1)S(1)} %collective-permute-done.3.prev_ref) | copy-start | bytes 1572868
  38.0 8.8 %collective-permute-start.4 = (bf16[16,136,128]{2,1,0:T(8,128)(2,1)S(1)}, bf16[16,136,128]{2,1,0:T(8,128)(2,1)S(1)}, u32[]{:S(2)}, u32[]{:S(2)}) collective-permute-start(bf16[16,136,128]{2,1,0:T(8,128)(2,1)S(1)} %get-tuple-element.71), channel_id=1, source_target_pairs={{0,32},{32,0},{1,33},{33,1},{2,34},{34,2},{3,35},{35,3},{4,36},{36... | collective-permute-start | bytes 1671176 | tf_op jit(solution)/shard_map/ppermute | solution.py:389
  45.8 1.0 copy-start.4
  47.7 22.9 %all-to-all-start = ((bf16[16,1,136,128]{3,2,1,0:T(8,128)(2,1)}), bf16[16,1,136,128]{3,2,1,0:T(8,128)(2,1)S(1)}, u32[]{:S(2)}, u32[]{:S(2)}) async-start(bf16[16,1,136,128]{3,2,1,0:T(8,128)(2,1)} %bitcast.7), calls=%async_computation | async-start | bytes 1114112 | tf_op jit(solution)/shard_map/all_to_all | solution.py:377
  59.2 11.5 %collective-permute-start.5 = (bf16[8,4096]{1,0:T(8,128)(2,1)S(1)}, bf16[8,4096]{1,0:T(8,128)(2,1)S(1)}, u32[]{:S(2)}, u32[]{:S(2)}) collective-permute-start(bf16[8,4096]{1,0:T(8,128)(2,1)S(1)} %get-tuple-element.74), channel_id=1, source_target_pairs={{1,0},{2,1},{3,2},{4,3},{5,4},{6,5},{7,6},{8,7},{9,8},{10,9},{11,1... | collective-permute-start | bytes 196616 | tf_op jit(solution)/shard_map/ppermute | solution.py:53
  70.7 16.2 %copy-start.14 = (bf16[8,4096]{1,0:T(8,128)(2,1)}, bf16[8,4096]{1,0:T(8,128)(2,1)S(1)}, u32[]{:S(2)}) copy-start(bf16[8,4096]{1,0:T(8,128)(2,1)S(1)} %collective-permute-done.5.after_ref) | copy-start | bytes 196612
  71.5 19.8 %all-to-all-start.1 = ((bf16[8,1,136,128]{3,2,1,0:T(8,128)(2,1)}), bf16[8,1,136,128]{3,2,1,0:T(8,128)(2,1)S(1)}, u32[]{:S(2)}, u32[]{:S(2)}) async-start(bf16[8,1,136,128]{3,2,1,0:T(8,128)(2,1)} %broadcast_in_dim.33), calls=%async_computation.1 | async-start | bytes 557056 | tf_op jit(solution)/shard_map/all_to_all | solution.py:377
  92.2 17.8 %all-to-all-start.2 = ((bf16[16,1,136,128]{3,2,1,0:T(8,128)(2,1)}), bf16[16,1,136,128]{3,2,1,0:T(8,128)(2,1)S(1)}, u32[]{:S(2)}, u32[]{:S(2)}) async-start(bf16[16,1,136,128]{3,2,1,0:T(8,128)(2,1)} %broadcast_in_dim.37), calls=%async_computation.2 | async-start | bytes 1114112 | tf_op jit(solution)/shard_map/all_to_all | solution.py:377
  110.0 3.7 %collective-permute-start.6 = (bf16[16,136,128]{2,1,0:T(8,128)(2,1)S(1)}, bf16[16,136,128]{2,1,0:T(8,128)(2,1)S(1)}, u32[]{:S(2)}, u32[]{:S(2)}) collective-permute-start(bf16[16,136,128]{2,1,0:T(8,128)(2,1)S(1)} %bitcast.30), channel_id=1, source_target_pairs={{0,32},{32,0},{1,33},{33,1},{2,34},{34,2},{3,35},{35,3},{4,36},{36... | collective-permute-start | bytes 1671176 | tf_op jit(solution)/shard_map/ppermute | solution.py:389

commit v7 on v6

--- a/solution.py
+++ b/solution.py
@@ -143,21 +143,22 @@
     first, second, _, front, totaps = matrices(table_ref)
     low, high = note_cuts(lengths_ref, rows, cuts_s)
     taps_spec[...] = dot(first(), ltaps_ref[...].astype(BF))
-    back_ref[...] = jnp.zeros_like(back_ref)
-    spec_acc[...] = jnp.zeros_like(spec_acc)
     at = row_ids(rows)
 
-    def document(d, carry):
+    def document(d, begun):
         inside = jnp.where((at >= cuts_s[d]) & (at < cuts_s[d + 1]), 1.0, 0.0)
         own_bf = wide(inside.astype(BF), columns)
         x_spec = dot(second(), mixed_ref[...] * own_bf)
         a_spec = dot(first(), adj_ref[...] * own_bf)
-        spec_acc[...] += times(a_spec, x_spec, True)
+        terms = times(a_spec, x_spec, True)
+        spec_acc[...] = spec_acc[...] + terms if begun else terms
         product = times(taps_spec[...], a_spec, True).astype(BF)
-        back_ref[...] += wide(inside, columns) * back_dot(front(), product)
-        return carry
-
-    lax.fori_loop(low, high + 1, document, 0)
+        back = wide(inside, columns) * back_dot(front(), product)
+        back_ref[...] = back_ref[...] + back if begun else back
+        return begun
+
+    document(low, 0)
+    lax.fori_loop(low + 1, high + 1, lambda d, carry: document(d, 1), 1)
     grads_ref[...] = back_dot(totaps(), spec_acc[...].astype(BF))
 
 
@@ -207,26 +208,26 @@
 
 
 def long_kernel(half_ref, lengths_ref, gl_ref, up_ref, mixed_ref, prev_ref, ltaps_ref, table_ref, *rest):
-    out_ref, ggl_ref, taps_spec, prev_spec, long_acc, cuts_s = rest[-6:]
+    out_ref, ggl_ref, taps_spec, long_acc, cuts_s = rest[-5:]
     rows, columns = gl_ref.shape
     first, second, later, _, _ = matrices(table_ref)
     low, high = note_cuts(lengths_ref, rows, cuts_s)
     at = row_ids(rows)
     earlier = jnp.where(at - rows >= cuts_s[low], 1.0, 0.0).astype(BF)
     taps_spec[...] = dot(first(), ltaps_ref[...].astype(BF))
-    prev_spec[...] = dot(first(), prev_ref[...] * wide(earlier, columns))
-    long_acc[...] = jnp.zeros_like(long_acc)
-
-    def document(d, carry):
+
+    def document(d, begun):
         inside = jnp.where((at >= cuts_s[d]) & (at < cuts_s[d + 1]), 1.0, 0.0)
-        reaches_back = jnp.where(d == low, 1.0, 0.0)
         x_spec = dot(second(), mixed_ref[...] * wide(inside.astype(BF), columns))
-        x_spec = x_spec + reaches_back * prev_spec[...]
+        if not begun:
+            x_spec = x_spec + dot(first(), prev_ref[...] * wide(earlier, columns))
         product = times(taps_spec[...], x_spec, False).astype(BF)
-        long_acc[...] += wide(inside, columns) * back_dot(later(), product)
-        return carry
-
-    lax.fori_loop(low, high + 1, document, 0)
+        mix = wide(inside, columns) * back_dot(later(), product)
+        long_acc[...] = long_acc[...] + mix if begun else mix
+        return begun
+
+    document(low, 0)
+    lax.fori_loop(low + 1, high + 1, lambda d, carry: document(d, 1), 1)
     long_mix = long_acc[...]
     out_ref[...] = (gl_ref[...].astype(F32) * long_mix).astype(BF)
     ggl_ref[...] = (up_ref[...].astype(F32) * long_mix).astype(BF)
@@ -358,7 +359,7 @@
             [("scalars", lengths), ("whole", gl), ("whole", up), ("half", mixed), ("half", prev),
              ("whole", ltaps), ("table", self.table)],
             [out(BF)] * 2,
-            [spectrum, spectrum, (self.rows, 0, F32), (0, 0, pltpu.SMEM((16,), jnp.int32))], 3, 56, filled)
+            [spectrum, (self.rows, 0, F32), (0, 0, pltpu.SMEM((16,), jnp.int32))], 3, 56, filled)
 
     def values_grad(self, lengths, adjs, after, staps):
         return self.call(

time: 114 us -> 113 us (level); the launches traced: 115 us -> 113 us
  starting transfers between devices: 47.9 us -> 42.7 us
  Pallas kernels: 41.3 us -> 45.4 us
  waiting for transfers between devices: 17.6 us -> 16.3 us
    pallas_call x10, Pallas kernels: 41.3 us -> 45.4 us  [call(): pl.pallas_call(kernel, grid_spec=pltpu.PrefetchScalarGridSpec(num_scalar_...]
    all_to_all x3, starting transfers between devices: 28.9 us -> 25 us  [traded(): return lax.all_to_all(block, axes, 0, 0, tiled=True)]
    ppermute x5, starting transfers between devices: 14.3 us -> 12.3 us  [passed_along(): return lax.ppermute(block, CTX, route)]
  transfers between devices with their start and end apart: 10 -> 10, of which waited for: 5 -> 4; matrix products, arithmetic and copies ran while one was open for 2% -> 2% of each run, Pallas kernels for 35% -> 39%
where the time goes in v7:
time: 113 us
  Pallas kernels  45.4 us (40%)
  starting transfers between devices  42.7 us (38%)
  waiting for transfers between devices  16.3 us (14%)
  local copies, waits for them, and re-layouts  4.55 us (4%)
  other arithmetic  2.9 us (3%)
    pallas_call x10, Pallas kernels, call(): pl.pallas_call(kernel, grid_spec=pltpu.PrefetchScalarGridSpec(num_scalar_...  45.4 us
    all_to_all x3, starting transfers between devices, traded(): return lax.all_to_all(block, axes, 0, 0, tiled=True)  25 us
    all_to_all x3, waiting for transfers between devices, traded(): return lax.all_to_all(block, axes, 0, 0, tiled=True)  14.7 us
    ppermute x5, starting transfers between devices, passed_along(): return lax.ppermute(block, CTX, route)  12.3 us
    ppermute x2, starting transfers between devices, swapped(): return lax.ppermute(block, 'core', [(0, 1), (1, 0)])  5.47 us
  transfers between devices with their start and end apart: 10, of which 4 were waited for; matrix products, arithmetic and copies ran while one was open for 2% of the time, Pallas kernels for 39%

profile of v7, /device:TPU:1, one launch (start us, length us, event | category | flops | bytes accessed | tf_op | source)
XLA Modules:
  0.0 112.8 jit_solution(77104737754758646)
XLA Ops:
  0.6 0.8 slice_bitcast_fusion
  1.5 4.1 %collective-permute-start = (bf16[8,4096]{1,0:T(8,128)(2,1)S(1)}, bf16[8,4096]{1,0:T(8,128)(2,1)S(1)}, u32[]{:S(2)}, u32[]{:S(2)}) collective-permute-start(bf16[8,4096]{1,0:T(8,128)(2,1)S(1)} %slice_bitcast_fusion), channel_id=1, source_target_pairs={{0,1},{1,2},{2,3},{3,4},{4,5},{5,6},{6,7},{7,8},{8,9},{9,10},{10,1... | collective-permute-start | bytes 196616 | tf_op jit(solution)/shard_map/ppermute | solution.py:53
  5.6 1.8 %multiply_convert_fusion.adj_ref = bf16[128,4096]{1,0:T(8,128)(2,1)S(1)} fusion(bf16[1,128,4096]{2,1,0:T(8,128)(2,1)} %param.11, bf16[1,128,4096]{2,1,0:T(8,128)(2,1)} %param.14), kind=kLoop, calls=%fused_computation | loop fusion | flops 2097152 | bytes 3145728 | tf_op jit(solution)/shard_map/convert_element_type | solution.py:405
  7.4 1.3 %collective-permute-start.2 = (bf16[128,4096]{1,0:T(8,128)(2,1)S(1)}, bf16[128,4096]{1,0:T(8,128)(2,1)}, u32[]{:S(2)}, u32[]{:S(2)}) collective-permute-start(bf16[128,4096]{1,0:T(8,128)(2,1)S(1)} %multiply_convert_fusion.adj_ref), channel_id=1, source_target_pairs={{1,0},{2,1},{3,2},{4,3},{5,4},{6,5},{7,6},{8,7},{9,8},{10,9},{11,1... | collective-permute-start | bytes 3145736 | tf_op jit(solution)/shard_map/ppermute | solution.py:53
  8.7 4.1 %shard_map.127 = (bf16[128,2048]{1,0:T(8,128)(2,1)}, f32[128,2048]{1,0:T(8,128)}) custom-call(s32[1]{0:T(128)S(6)} %sub.3.half_ref, s32[1,8]{1,0:T(1,128)} %lengths_ref.17, bf16[128,4096]{1,0:T(8,128)(2,1)} %bitcast.22, bf16[8,4096]{1,0:T(8,128)(2,1)} %copy-done.10, bf16[128,4096]{1,0:T(8,128)(2,1)} %bitcast.26, f32[7,4096]{1,0:T(8,128)} %taps_ref.5), custom_call_target="tpu_custom_call" | custom-call | bytes 10500000 | tf_op jit(solution)/shard_map/pallas_call | solution.py:300
  12.8 4.2 %collective-permute-start.1 = (bf16[128,2048]{1,0:T(8,128)(2,1)}, bf16[128,2048]{1,0:T(8,128)(2,1)S(1)}, u32[]{:S(2)}, u32[]{:S(2)}) collective-permute-start(bf16[128,2048]{1,0:T(8,128)(2,1)} %get-tuple-element.75.mixed_ref), channel_id=1, source_target_pairs={{0,1},{1,2},{2,3},{3,4},{4,5},{5,6},{6,7},{7,8},{8,9},{9,10},{10,1... | collective-permute-start | bytes 1572872 | tf_op jit(solution)/shard_map/ppermute | solution.py:53
  17.0 1.0 copy-done.8
  18.0 5.4 %shard_map.128 = (f32[128,2048]{1,0:T(8,128)S(1)}, f32[128,2048]{1,0:T(8,128)S(1)}) custom-call(s32[1]{0:T(128)S(6)} %sub.3.half_ref, s32[1,8]{1,0:T(1,128)S(1)} %copy-done.13, bf16[128,2048]{1,0:T(8,128)(2,1)S(1)} %copy-done.8, bf16[128,4096]{1,0:T(8,128)(2,1)S(1)} %multiply_convert_fusion.adj_ref, f32[128,4096]{1,0:T(8,128)S(1)} %copy-done, ...), custom_call_target="tpu_custom_call" | custom-call | bytes 5250000 | tf_op jit(solution)/shard_map/pallas_call | solution.py:300
  23.5 2.8 %shard_map.129 = (bf16[128,2048]{1,0:T(8,128)(2,1)S(1)}, f32[128,2048]{1,0:T(8,128)S(1)}) custom-call(s32[1]{0:T(128)} %bitcast.half_ref, s32[1,8]{1,0:T(1,128)S(1)} %copy-done.13, bf16[128,4096]{1,0:T(8,128)(2,1)S(1)} %bitcast.23, bf16[8,4096]{1,0:T(8,128)(2,1)S(1)} %copy-done.11, bf16[128,4096]{1,0:T(8,128)(2,1)S(1)} %bitcast.27, f32[7,4096]{1,0:T(8,128)S(1)} %copy-done.5), custom_call_target="tpu_custom_call" | custom-call | bytes 10500000 | tf_op jit(solution)/shard_map/pallas_call | solution.py:300
  26.3 1.5 %collective-permute-start.3 = (bf16[128,2048]{1,0:T(8,128)(2,1)S(1)}, bf16[128,2048]{1,0:T(8,128)(2,1)S(1)}, u32[]{:S(2)}, u32[]{:S(2)}) collective-permute-start(bf16[128,2048]{1,0:T(8,128)(2,1)S(1)} %get-tuple-element.80.mixed_ref), channel_id=1, source_target_pairs={{0,1},{1,2},{2,3},{3,4},{4,5},{5,6},{6,7},{7,8},{8,9},{9,10},{10,1... | collective-permute-start | bytes 1572872 | tf_op jit(solution)/shard_map/ppermute | solution.py:53
  27.8 5.4 %shard_map.130 = (f32[128,2048]{1,0:T(8,128)S(1)}, f32[128,2048]{1,0:T(8,128)S(1)}) custom-call(s32[1]{0:T(128)} %bitcast.half_ref, s32[1,8]{1,0:T(1,128)S(1)} %copy-done.13, bf16[128,2048]{1,0:T(8,128)(2,1)S(1)} %get-tuple-element.80.mixed_ref, bf16[128,4096]{1,0:T(8,128)(2,1)S(1)} %multiply_convert_fusion.adj_ref, f32[128,4096]{1,0:T(8,128)S(1)} %copy-done, ...), custom_call_target="tpu_custom_call" | custom-call | bytes 5250000 | tf_op jit(solution)/shard_map/pallas_call | solution.py:300
  33.2 5.4 %shard_map.131 = (bf16[128,4096]{1,0:T(8,128)(2,1)}, bf16[128,4096]{1,0:T(8,128)(2,1)S(1)}, bf16[8,4096]{1,0:T(8,128)(2,1)S(1)}, bf16[16,136,128]{2,1,0:T(8,128)(2,1)S(1)}) custom-call(s32[1]{0:T(128)S(6)} %sub.3.half_ref, s32[1,8]{1,0:T(1,128)S(1)} %copy-done.13, bf16[128,4096]{1,0:T(8,128)(2,1)S(1)} %bitcast.24, bf16[8,4096]{1,0:T(8,128)(2,1)S(1)} %copy-done.11, ...), custom_call_target="tpu_custom_call" | custom-call | bytes 5250000 | tf_op jit(solution)/shard_map/pallas_call | solution.py:300
  38.6 2.9 %collective-permute-start.4 = (bf16[16,136,128]{2,1,0:T(8,128)(2,1)S(1)}, bf16[16,136,128]{2,1,0:T(8,128)(2,1)S(1)}, u32[]{:S(2)}, u32[]{:S(2)}) collective-permute-start(bf16[16,136,128]{2,1,0:T(8,128)(2,1)S(1)} %get-tuple-element.71), channel_id=1, source_target_pairs={{0,32},{32,0},{1,33},{33,1},{2,34},{34,2},{3,35},{35,3},{4,36},{36... | collective-permute-start | bytes 1671176 | tf_op jit(solution)/shard_map/ppermute | solution.py:390
  41.5 5.3 %shard_map.132 = (bf16[128,4096]{1,0:T(8,128)(2,1)}, bf16[128,4096]{1,0:T(8,128)(2,1)S(1)}, bf16[8,4096]{1,0:T(8,128)(2,1)S(1)}, bf16[16,136,128]{2,1,0:T(8,128)(2,1)S(1)}) custom-call(s32[1]{0:T(128)} %bitcast.half_ref, s32[1,8]{1,0:T(1,128)S(1)} %copy-done.13, ...), custom_call_target="tpu_custom_call", output_to_operand_aliasing={{0}: (14, {}), {1}: (15, {}), {2}: (16, {})} | custom-call | bytes 5250000 | tf_op jit(solution)/shard_map/pallas_call | solution.py:300
  46.8 1.0 copy-done.4
  47.7 1.0 add_convert_fusion
  48.7 10.5 %all-to-all-start = ((bf16[16,1,136,128]{3,2,1,0:T(8,128)(2,1)}), bf16[16,1,136,128]{3,2,1,0:T(8,128)(2,1)S(1)}, u32[]{:S(2)}, u32[]{:S(2)}) async-start(bf16[16,1,136,128]{3,2,1,0:T(8,128)(2,1)} %bitcast.7), calls=%async_computation | async-start | bytes 1114112 | tf_op jit(solution)/shard_map/all_to_all | solution.py:378
  59.2 1.3 %collective-permute-start.5 = (bf16[8,4096]{1,0:T(8,128)(2,1)S(1)}, bf16[8,4096]{1,0:T(8,128)(2,1)S(1)}, u32[]{:S(2)}, u32[]{:S(2)}) collective-permute-start(bf16[8,4096]{1,0:T(8,128)(2,1)S(1)} %get-tuple-element.74), channel_id=1, source_target_pairs={{1,0},{2,1},{3,2},{4,3},{5,4},{6,5},{7,6},{8,7},{9,8},{10,9},{11,1... | collective-permute-start | bytes 196616 | tf_op jit(solution)/shard_map/ppermute | solution.py:53
  60.5 5.7 %shard_map.133 = (bf16[128,4096]{1,0:T(8,128)(2,1)}, bf16[128,4096]{1,0:T(8,128)(2,1)}) custom-call(s32[1]{0:T(128)S(6)} %sub.3.half_ref, s32[1,8]{1,0:T(1,128)} %lengths_ref.17, bf16[128,4096]{1,0:T(8,128)(2,1)} %bitcast.32, bf16[128,4096]{1,0:T(8,128)(2,1)} %bitcast.34, bf16[128,2048]{1,0:T(8,128)(2,1)} %get-tuple-element.75.mixed_ref, ...), custom_call_target="tpu_custom_call" | custom-call | bytes 10500000 | tf_op jit(solution)/shard_map/pallas_call | solution.py:300
  66.2 4.4 %all-to-all-done = bf16[16,1,136,128]{3,2,1,0:T(8,128)(2,1)S(1)} async-done(((bf16[16,1,136,128]{3,2,1,0:T(8,128)(2,1)}), bf16[16,1,136,128]{3,2,1,0:T(8,128)(2,1)S(1)}, u32[]{:S(2)}, u32[]{:S(2)}) %all-to-all-start) | async-done | bytes 557088 | tf_op jit(solution)/shard_map/all_to_all | solution.py:378
  70.6 0.1 reduce_sum.23
  70.7 0.7 broadcast_in_dim.33
  71.4 8.9 %all-to-all-start.1 = ((bf16[8,1,136,128]{3,2,1,0:T(8,128)(2,1)}), bf16[8,1,136,128]{3,2,1,0:T(8,128)(2,1)S(1)}, u32[]{:S(2)}, u32[]{:S(2)}) async-start(bf16[8,1,136,128]{3,2,1,0:T(8,128)(2,1)} %broadcast_in_dim.33), calls=%async_computation.1 | async-start | bytes 557056 | tf_op jit(solution)/shard_map/all_to_all | solution.py:378
  80.3 5.7 %shard_map.134 = (bf16[128,4096]{1,0:T(8,128)(2,1)}, bf16[128,4096]{1,0:T(8,128)(2,1)}) custom-call(s32[1]{0:T(128)} %bitcast.half_ref, s32[1,8]{1,0:T(1,128)} %lengths_ref.17, bf16[128,4096]{1,0:T(8,128)(2,1)} %bitcast.33, bf16[128,4096]{1,0:T(8,128)(2,1)} %bitcast.35, bf16[128,2048]{1,0:T(8,128)(2,1)} %copy-done.6, ...), custom_call_target="tpu_custom_call", output_to_operand_aliasing={{0}: (8, {}), {1}: (9, {})} | custom-call | bytes 10500000 | tf_op jit(solution)/shard_map/pallas_call | solution.py:300
  86.0 4.3 %all-to-all-done.1 = bf16[8,1,136,128]{3,2,1,0:T(8,128)(2,1)S(1)} async-done(((bf16[8,1,136,128]{3,2,1,0:T(8,128)(2,1)}), bf16[8,1,136,128]{3,2,1,0:T(8,128)(2,1)S(1)}, u32[]{:S(2)}, u32[]{:S(2)}) %all-to-all-start.1) | async-done | bytes 278560 | tf_op jit(solution)/shard_map/all_to_all | solution.py:378
  90.4 0.9 broadcast_in_dim.37
  91.3 5.6 %all-to-all-start.2 = ((bf16[16,1,136,128]{3,2,1,0:T(8,128)(2,1)}), bf16[16,1,136,128]{3,2,1,0:T(8,128)(2,1)S(1)}, u32[]{:S(2)}, u32[]{:S(2)}) async-start(bf16[16,1,136,128]{3,2,1,0:T(8,128)(2,1)} %broadcast_in_dim.37), calls=%async_computation.2 | async-start | bytes 1114112 | tf_op jit(solution)/shard_map/all_to_all | solution.py:378
  96.9 4.3 %shard_map.135 = bf16[128,4096]{1,0:T(8,128)(2,1)} custom-call(s32[1,8]{1,0:T(1,128)} %lengths_ref.17, bf16[128,4096]{1,0:T(8,128)(2,1)} %copy-done.4, bf16[8,4096]{1,0:T(8,128)(2,1)} %copy-done.14, f32[7,4096]{1,0:T(8,128)} %taps_ref.5), custom_call_target="tpu_custom_call" | custom-call | bytes 14000000 | tf_op jit(solution)/shard_map/pallas_call | solution.py:300
  101.2 6.0 %all-to-all-done.2 = bf16[16,1,136,128]{3,2,1,0:T(8,128)(2,1)S(1)} async-done(((bf16[16,1,136,128]{3,2,1,0:T(8,128)(2,1)}), bf16[16,1,136,128]{3,2,1,0:T(8,128)(2,1)S(1)}, u32[]{:S(2)}, u32[]{:S(2)}) %all-to-all-start.2) | async-done | bytes 557088 | tf_op jit(solution)/shard_map/all_to_all | solution.py:378
  107.2 2.6 %collective-permute-start.6 = (bf16[16,136,128]{2,1,0:T(8,128)(2,1)S(1)}, bf16[16,136,128]{2,1,0:T(8,128)(2,1)S(1)}, u32[]{:S(2)}, u32[]{:S(2)}) collective-permute-start(bf16[16,136,128]{2,1,0:T(8,128)(2,1)S(1)} %bitcast.30), channel_id=1, source_target_pairs={{0,32},{32,0},{1,33},{33,1},{2,34},{34,2},{3,35},{35,3},{4,36},{36... | collective-permute-start | bytes 1671176 | tf_op jit(solution)/shard_map/ppermute | solution.py:390
  109.8 1.6 %collective-permute-done.6.other_ref = bf16[16,136,128]{2,1,0:T(8,128)(2,1)S(1)} collective-permute-done((bf16[16,136,128]{2,1,0:T(8,128)(2,1)S(1)}, bf16[16,136,128]{2,1,0:T(8,128)(2,1)S(1)}, u32[]{:S(2)}, u32[]{:S(2)}) %collective-permute-start.6) | collective-permute-done | bytes 557088 | tf_op jit(solution)/shard_map/ppermute | solution.py:390
  111.3 1.5 %shard_map.136 = (f32[7,4096]{1,0:T(8,128)}, f32[128,4096]{1,0:T(8,128)}) custom-call(bf16[16,136,128]{2,1,0:T(8,128)(2,1)S(1)} %bitcast.31, bf16[16,136,128]{2,1,0:T(8,128)(2,1)S(1)} %collective-permute-done.6.other_ref), custom_call_target="tpu_custom_call" | custom-call | bytes 10500000 | tf_op jit(solution)/shard_map/pallas_call | solution.py:300
  (36 shorter events, 0.1 us)
Async XLA Ops:
  1.5 15.5 %copy-start = (f32[128,4096]{1,0:T(8,128)S(1)}, f32[128,4096]{1,0:T(8,128)}, u32[]{:S(2)}) copy-start(f32[128,4096]{1,0:T(8,128)} %ltaps_ref.11) | copy-start | bytes 6291460
  1.5 15.5 %copy-start.13 = (s32[1,8]{1,0:T(1,128)S(1)}, s32[1,8]{1,0:T(1,128)}, u32[]{:S(2)}) copy-start(s32[1,8]{1,0:T(1,128)} %lengths_ref.17) | copy-start | bytes 100
  1.5 5.9 %collective-permute-start = (bf16[8,4096]{1,0:T(8,128)(2,1)S(1)}, bf16[8,4096]{1,0:T(8,128)(2,1)S(1)}, u32[]{:S(2)}, u32[]{:S(2)}) collective-permute-start(bf16[8,4096]{1,0:T(8,128)(2,1)S(1)} %slice_bitcast_fusion), channel_id=1, source_target_pairs={{0,1},{1,2},{2,3},{3,4},{4,5},{5,6},{6,7},{7,8},{8,9},{9,10},{10,1... | collective-permute-start | bytes 196616 | tf_op jit(solution)/shard_map/ppermute | solution.py:53
  7.4 1.3 %copy-start.10 = (bf16[8,4096]{1,0:T(8,128)(2,1)}, bf16[8,4096]{1,0:T(8,128)(2,1)S(1)}, u32[]{:S(2)}) copy-start(bf16[8,4096]{1,0:T(8,128)(2,1)S(1)} %collective-permute-done.before_ref) | copy-start | bytes 196612
  7.4 25.8 %collective-permute-start.2 = (bf16[128,4096]{1,0:T(8,128)(2,1)S(1)}, bf16[128,4096]{1,0:T(8,128)(2,1)}, u32[]{:S(2)}, u32[]{:S(2)}) collective-permute-start(bf16[128,4096]{1,0:T(8,128)(2,1)S(1)} %multiply_convert_fusion.adj_ref), channel_id=1, source_target_pairs={{1,0},{2,1},{3,2},{4,3},{5,4},{6,5},{7,6},{8,7},{9,8},{10,9},{11,1... | collective-permute-start | bytes 3145736 | tf_op jit(solution)/shard_map/ppermute | solution.py:53
  8.7 8.3 %copy-start.1 = (bf16[1280,256]{1,0:T(8,128)(2,1)S(1)}, bf16[1280,256]{1,0:T(8,128)(2,1)}, u32[]{:S(2)}) copy-start(bf16[1280,256]{1,0:T(8,128)(2,1)} %constant.16.clone.table_ref) | copy-start | bytes 1966084
  12.8 10.7 %copy-start.2 = (bf16[1,128,4096]{2,1,0:T(8,128)(2,1)S(1)}, bf16[1,128,4096]{2,1,0:T(8,128)(2,1)}, u32[]{:S(2)}) copy-start(bf16[1,128,4096]{2,1,0:T(8,128)(2,1)} %param.9) | copy-start | bytes 3145732
  12.8 10.7 %copy-start.3 = (bf16[1,128,4096]{2,1,0:T(8,128)(2,1)S(1)}, bf16[1,128,4096]{2,1,0:T(8,128)(2,1)}, u32[]{:S(2)}) copy-start(bf16[1,128,4096]{2,1,0:T(8,128)(2,1)} %param.10) | copy-start | bytes 3145732
  12.8 10.7 %copy-start.5 = (f32[7,4096]{1,0:T(8,128)S(1)}, f32[7,4096]{1,0:T(8,128)}, u32[]{:S(2)}) copy-start(f32[7,4096]{1,0:T(8,128)} %taps_ref.5) | copy-start | bytes 344068
  12.8 20.4 %collective-permute-start.1 = (bf16[128,2048]{1,0:T(8,128)(2,1)}, bf16[128,2048]{1,0:T(8,128)(2,1)S(1)}, u32[]{:S(2)}, u32[]{:S(2)}) collective-permute-start(bf16[128,2048]{1,0:T(8,128)(2,1)} %get-tuple-element.75.mixed_ref), channel_id=1, source_target_pairs={{0,1},{1,2},{2,3},{3,4},{4,5},{5,6},{6,7},{7,8},{8,9},{9,10},{10,1... | collective-permute-start | bytes 1572872 | tf_op jit(solution)/shard_map/ppermute | solution.py:53
  17.0 1.0 copy-start.8
  18.0 5.4 %copy-start.11 = (bf16[8,4096]{1,0:T(8,128)(2,1)S(1)}, bf16[8,4096]{1,0:T(8,128)(2,1)}, u32[]{:S(2)}) copy-start(bf16[8,4096]{1,0:T(8,128)(2,1)} %copy-done.10) | copy-start | bytes 196612
  26.3 6.9 %copy-start.6 = (bf16[128,2048]{1,0:T(8,128)(2,1)}, bf16[128,2048]{1,0:T(8,128)(2,1)S(1)}, u32[]{:S(2)}) copy-start(bf16[128,2048]{1,0:T(8,128)(2,1)S(1)} %get-tuple-element.80.mixed_ref) | copy-start | bytes 1572868
  26.3 6.9 %copy-start.12 = (f32[128,2048]{1,0:T(8,128)S(1)}, f32[128,2048]{1,0:T(8,128)}, u32[]{:S(2)}) copy-start(f32[128,2048]{1,0:T(8,128)} %get-tuple-element.61.short_ref) | copy-start | bytes 3145732
  26.3 12.3 %collective-permute-start.3 = (bf16[128,2048]{1,0:T(8,128)(2,1)S(1)}, bf16[128,2048]{1,0:T(8,128)(2,1)S(1)}, u32[]{:S(2)}, u32[]{:S(2)}) collective-permute-start(bf16[128,2048]{1,0:T(8,128)(2,1)S(1)} %get-tuple-element.80.mixed_ref), channel_id=1, source_target_pairs={{0,1},{1,2},{2,3},{3,4},{4,5},{5,6},{6,7},{7,8},{8,9},{9,10},{10,1... | collective-permute-start | bytes 1572872 | tf_op jit(solution)/shard_map/ppermute | solution.py:53
  33.2 5.4 %copy-start.9 = (bf16[128,2048]{1,0:T(8,128)(2,1)}, bf16[128,2048]{1,0:T(8,128)(2,1)S(1)}, u32[]{:S(2)}) copy-start(bf16[128,2048]{1,0:T(8,128)(2,1)S(1)} %collective-permute-done.1.prev_ref) | copy-start | bytes 1572868
  38.6 8.2 %copy-start.7 = (bf16[128,2048]{1,0:T(8,128)(2,1)}, bf16[128,2048]{1,0:T(8,128)(2,1)S(1)}, u32[]{:S(2)}) copy-start(bf16[128,2048]{1,0:T(8,128)(2,1)S(1)} %collective-permute-done.3.prev_ref) | copy-start | bytes 1572868
  38.6 9.1 %collective-permute-start.4 = (bf16[16,136,128]{2,1,0:T(8,128)(2,1)S(1)}, bf16[16,136,128]{2,1,0:T(8,128)(2,1)S(1)}, u32[]{:S(2)}, u32[]{:S(2)}) collective-permute-start(bf16[16,136,128]{2,1,0:T(8,128)(2,1)S(1)} %get-tuple-element.71), channel_id=1, source_target_pairs={{0,32},{32,0},{1,33},{33,1},{2,34},{34,2},{3,35},{35,3},{4,36},{36... | collective-permute-start | bytes 1671176 | tf_op jit(solution)/shard_map/ppermute | solution.py:390
  46.8 1.0 copy-start.4
  48.7 21.9 %all-to-all-start = ((bf16[16,1,136,128]{3,2,1,0:T(8,128)(2,1)}), bf16[16,1,136,128]{3,2,1,0:T(8,128)(2,1)S(1)}, u32[]{:S(2)}, u32[]{:S(2)}) async-start(bf16[16,1,136,128]{3,2,1,0:T(8,128)(2,1)} %bitcast.7), calls=%async_computation | async-start | bytes 1114112 | tf_op jit(solution)/shard_map/all_to_all | solution.py:378
  59.2 11.5 %collective-permute-start.5 = (bf16[8,4096]{1,0:T(8,128)(2,1)S(1)}, bf16[8,4096]{1,0:T(8,128)(2,1)S(1)}, u32[]{:S(2)}, u32[]{:S(2)}) collective-permute-start(bf16[8,4096]{1,0:T(8,128)(2,1)S(1)} %get-tuple-element.74), channel_id=1, source_target_pairs={{1,0},{2,1},{3,2},{4,3},{5,4},{6,5},{7,6},{8,7},{9,8},{10,9},{11,1... | collective-permute-start | bytes 196616 | tf_op jit(solution)/shard_map/ppermute | solution.py:53
  70.7 15.3 %copy-start.14 = (bf16[8,4096]{1,0:T(8,128)(2,1)}, bf16[8,4096]{1,0:T(8,128)(2,1)S(1)}, u32[]{:S(2)}) copy-start(bf16[8,4096]{1,0:T(8,128)(2,1)S(1)} %collective-permute-done.5.after_ref) | copy-start | bytes 196612
  71.4 18.9 %all-to-all-start.1 = ((bf16[8,1,136,128]{3,2,1,0:T(8,128)(2,1)}), bf16[8,1,136,128]{3,2,1,0:T(8,128)(2,1)S(1)}, u32[]{:S(2)}, u32[]{:S(2)}) async-start(bf16[8,1,136,128]{3,2,1,0:T(8,128)(2,1)} %broadcast_in_dim.33), calls=%async_computation.1 | async-start | bytes 557056 | tf_op jit(solution)/shard_map/all_to_all | solution.py:378
  91.3 15.9 %all-to-all-start.2 = ((bf16[16,1,136,128]{3,2,1,0:T(8,128)(2,1)}), bf16[16,1,136,128]{3,2,1,0:T(8,128)(2,1)S(1)}, u32[]{:S(2)}, u32[]{:S(2)}) async-start(bf16[16,1,136,128]{3,2,1,0:T(8,128)(2,1)} %broadcast_in_dim.37), calls=%async_computation.2 | async-start | bytes 1114112 | tf_op jit(solution)/shard_map/all_to_all | solution.py:378
  107.2 4.2 %collective-permute-start.6 = (bf16[16,136,128]{2,1,0:T(8,128)(2,1)S(1)}, bf16[16,136,128]{2,1,0:T(8,128)(2,1)S(1)}, u32[]{:S(2)}, u32[]{:S(2)}) collective-permute-start(bf16[16,136,128]{2,1,0:T(8,128)(2,1)S(1)} %bitcast.30), channel_id=1, source_target_pairs={{0,32},{32,0},{1,33},{33,1},{2,34},{34,2},{3,35},{35,3},{4,36},{36... | collective-permute-start | bytes 1671176 | tf_op jit(solution)/shard_map/ppermute | solution.py:390

commit v8 on v7

--- a/solution.py
+++ b/solution.py
@@ -332,7 +332,7 @@
         out = self.shaped(self.rows, "half")
         spectrum = (2 * self.rows, 0, F32)
         return self.call(
-            own_kernel, self.small(), half,
+            own_kernel, 2 * self.small(), half,
             [("scalars", lengths), ("half", mixed), ("whole", adj), ("whole", ltaps),
              ("table", self.table)],
             [out(F32)] * 2,

time: 113 us -> 113 us (level)
  Pallas kernels: 45.4 us -> 43.7 us
  starting transfers between devices: 42.7 us -> 44 us
    ppermute x5, starting transfers between devices: 12.3 us -> 14.1 us  [passed_along(): return lax.ppermute(block, CTX, route)]
    pallas_call x10, Pallas kernels: 45.4 us -> 43.7 us  [call(): pl.pallas_call(kernel, grid_spec=pltpu.PrefetchScalarGridSpec(num_scalar_...]
  transfers between devices with their start and end apart: 10 -> 10, of which waited for: 4 -> 5; matrix products, arithmetic and copies ran while one was open for 2% -> 2% of each run, Pallas kernels for 39% -> 38%
where the time goes in v8:
time: 113 us; the launch traced here: 112 us
  starting transfers between devices  44 us (39%)
  Pallas kernels  43.7 us (39%)
  waiting for transfers between devices  15.7 us (14%)
  local copies, waits for them, and re-layouts  4.55 us (4%)
  other arithmetic  2.9 us (3%)
    pallas_call x10, Pallas kernels, call(): pl.pallas_call(kernel, grid_spec=pltpu.PrefetchScalarGridSpec(num_scalar_...  43.7 us
    all_to_all x3, starting transfers between devices, traded(): return lax.all_to_all(block, axes, 0, 0, tiled=True)  23.9 us
    ppermute x5, starting transfers between devices, passed_along(): return lax.ppermute(block, CTX, route)  14.1 us
    all_to_all x3, waiting for transfers between devices, traded(): return lax.all_to_all(block, axes, 0, 0, tiled=True)  13.6 us
    ppermute x2, starting transfers between devices, swapped(): return lax.ppermute(block, 'core', [(0, 1), (1, 0)])  6.03 us
  transfers between devices with their start and end apart: 10, of which 5 were waited for; matrix products, arithmetic and copies ran while one was open for 2% of the time, Pallas kernels for 38%

profile of v8, /device:TPU:1, one launch (start us, length us, event | category | flops | bytes accessed | tf_op | source)
XLA Modules:
  0.0 111.8 jit_solution(16665470815900746960)
XLA Ops:
  0.6 0.8 slice_bitcast_fusion
  1.5 4.1 %collective-permute-start = (bf16[8,4096]{1,0:T(8,128)(2,1)S(1)}, bf16[8,4096]{1,0:T(8,128)(2,1)S(1)}, u32[]{:S(2)}, u32[]{:S(2)}) collective-permute-start(bf16[8,4096]{1,0:T(8,128)(2,1)S(1)} %slice_bitcast_fusion), channel_id=1, source_target_pairs={{0,1},{1,2},{2,3},{3,4},{4,5},{5,6},{6,7},{7,8},{8,9},{9,10},{10,1... | collective-permute-start | bytes 196616 | tf_op jit(solution)/shard_map/ppermute | solution.py:53
  5.6 1.8 %multiply_convert_fusion.adj_ref = bf16[128,4096]{1,0:T(8,128)(2,1)S(1)} fusion(bf16[1,128,4096]{2,1,0:T(8,128)(2,1)} %param.11, bf16[1,128,4096]{2,1,0:T(8,128)(2,1)} %param.14), kind=kLoop, calls=%fused_computation | loop fusion | flops 2097152 | bytes 3145728 | tf_op jit(solution)/shard_map/convert_element_type | solution.py:405
  7.4 1.3 %collective-permute-start.2 = (bf16[128,4096]{1,0:T(8,128)(2,1)S(1)}, bf16[128,4096]{1,0:T(8,128)(2,1)}, u32[]{:S(2)}, u32[]{:S(2)}) collective-permute-start(bf16[128,4096]{1,0:T(8,128)(2,1)S(1)} %multiply_convert_fusion.adj_ref), channel_id=1, source_target_pairs={{1,0},{2,1},{3,2},{4,3},{5,4},{6,5},{7,6},{8,7},{9,8},{10,9},{11,1... | collective-permute-start | bytes 3145736 | tf_op jit(solution)/shard_map/ppermute | solution.py:53
  8.7 4.1 %shard_map.127 = (bf16[128,2048]{1,0:T(8,128)(2,1)}, f32[128,2048]{1,0:T(8,128)}) custom-call(s32[1]{0:T(128)S(6)} %sub.3.half_ref, s32[1,8]{1,0:T(1,128)} %lengths_ref.17, bf16[128,4096]{1,0:T(8,128)(2,1)} %bitcast.22, bf16[8,4096]{1,0:T(8,128)(2,1)} %copy-done.10, bf16[128,4096]{1,0:T(8,128)(2,1)} %bitcast.26, f32[7,4096]{1,0:T(8,128)} %taps_ref.5), custom_call_target="tpu_custom_call" | custom-call | bytes 10500000 | tf_op jit(solution)/shard_map/pallas_call | solution.py:300
  12.8 4.2 %collective-permute-start.1 = (bf16[128,2048]{1,0:T(8,128)(2,1)}, bf16[128,2048]{1,0:T(8,128)(2,1)S(1)}, u32[]{:S(2)}, u32[]{:S(2)}) collective-permute-start(bf16[128,2048]{1,0:T(8,128)(2,1)} %get-tuple-element.75.mixed_ref), channel_id=1, source_target_pairs={{0,1},{1,2},{2,3},{3,4},{4,5},{5,6},{6,7},{7,8},{8,9},{9,10},{10,1... | collective-permute-start | bytes 1572872 | tf_op jit(solution)/shard_map/ppermute | solution.py:53
  17.0 1.0 copy-done.8
  18.0 4.5 %shard_map.128 = (f32[128,2048]{1,0:T(8,128)S(1)}, f32[128,2048]{1,0:T(8,128)S(1)}) custom-call(s32[1]{0:T(128)S(6)} %sub.3.half_ref, s32[1,8]{1,0:T(1,128)S(1)} %copy-done.13, bf16[128,2048]{1,0:T(8,128)(2,1)S(1)} %copy-done.8, bf16[128,4096]{1,0:T(8,128)(2,1)S(1)} %multiply_convert_fusion.adj_ref, f32[128,4096]{1,0:T(8,128)S(1)} %copy-done, ...), custom_call_target="tpu_custom_call" | custom-call | bytes 5250000 | tf_op jit(solution)/shard_map/pallas_call | solution.py:300
  22.6 2.8 %shard_map.129 = (bf16[128,2048]{1,0:T(8,128)(2,1)S(1)}, f32[128,2048]{1,0:T(8,128)S(1)}) custom-call(s32[1]{0:T(128)} %bitcast.half_ref, s32[1,8]{1,0:T(1,128)S(1)} %copy-done.13, bf16[128,4096]{1,0:T(8,128)(2,1)S(1)} %bitcast.23, bf16[8,4096]{1,0:T(8,128)(2,1)S(1)} %copy-done.11, bf16[128,4096]{1,0:T(8,128)(2,1)S(1)} %bitcast.27, f32[7,4096]{1,0:T(8,128)S(1)} %copy-done.5), custom_call_target="tpu_custom_call" | custom-call | bytes 10500000 | tf_op jit(solution)/shard_map/pallas_call | solution.py:300
  25.4 3.3 %collective-permute-start.3 = (bf16[128,2048]{1,0:T(8,128)(2,1)S(1)}, bf16[128,2048]{1,0:T(8,128)(2,1)S(1)}, u32[]{:S(2)}, u32[]{:S(2)}) collective-permute-start(bf16[128,2048]{1,0:T(8,128)(2,1)S(1)} %get-tuple-element.80.mixed_ref), channel_id=1, source_target_pairs={{0,1},{1,2},{2,3},{3,4},{4,5},{5,6},{6,7},{7,8},{8,9},{9,10},{10,1... | collective-permute-start | bytes 1572872 | tf_op jit(solution)/shard_map/ppermute | solution.py:53
  28.7 4.6 %shard_map.130 = (f32[128,2048]{1,0:T(8,128)S(1)}, f32[128,2048]{1,0:T(8,128)S(1)}) custom-call(s32[1]{0:T(128)} %bitcast.half_ref, s32[1,8]{1,0:T(1,128)S(1)} %copy-done.13, bf16[128,2048]{1,0:T(8,128)(2,1)S(1)} %get-tuple-element.80.mixed_ref, bf16[128,4096]{1,0:T(8,128)(2,1)S(1)} %multiply_convert_fusion.adj_ref, f32[128,4096]{1,0:T(8,128)S(1)} %copy-done, ...), custom_call_target="tpu_custom_call" | custom-call | bytes 5250000 | tf_op jit(solution)/shard_map/pallas_call | solution.py:300
  33.4 5.3 %shard_map.131 = (bf16[128,4096]{1,0:T(8,128)(2,1)}, bf16[128,4096]{1,0:T(8,128)(2,1)S(1)}, bf16[8,4096]{1,0:T(8,128)(2,1)S(1)}, bf16[16,136,128]{2,1,0:T(8,128)(2,1)S(1)}) custom-call(s32[1]{0:T(128)S(6)} %sub.3.half_ref, s32[1,8]{1,0:T(1,128)S(1)} %copy-done.13, bf16[128,4096]{1,0:T(8,128)(2,1)S(1)} %bitcast.24, bf16[8,4096]{1,0:T(8,128)(2,1)S(1)} %copy-done.11, ...), custom_call_target="tpu_custom_call" | custom-call | bytes 5250000 | tf_op jit(solution)/shard_map/pallas_call | solution.py:300
  38.7 0.5 collective-permute-done.3.prev_ref
  39.2 1.6 %collective-permute-start.4 = (bf16[16,136,128]{2,1,0:T(8,128)(2,1)S(1)}, bf16[16,136,128]{2,1,0:T(8,128)(2,1)S(1)}, u32[]{:S(2)}, u32[]{:S(2)}) collective-permute-start(bf16[16,136,128]{2,1,0:T(8,128)(2,1)S(1)} %get-tuple-element.71), channel_id=1, source_target_pairs={{0,32},{32,0},{1,33},{33,1},{2,34},{34,2},{3,35},{35,3},{4,36},{36... | collective-permute-start | bytes 1671176 | tf_op jit(solution)/shard_map/ppermute | solution.py:390
  40.8 5.3 %shard_map.132 = (bf16[128,4096]{1,0:T(8,128)(2,1)}, bf16[128,4096]{1,0:T(8,128)(2,1)S(1)}, bf16[8,4096]{1,0:T(8,128)(2,1)S(1)}, bf16[16,136,128]{2,1,0:T(8,128)(2,1)S(1)}) custom-call(s32[1]{0:T(128)} %bitcast.half_ref, s32[1,8]{1,0:T(1,128)S(1)} %copy-done.13, ...), custom_call_target="tpu_custom_call", output_to_operand_aliasing={{0}: (14, {}), {1}: (15, {}), {2}: (16, {})} | custom-call | bytes 5250000 | tf_op jit(solution)/shard_map/pallas_call | solution.py:300
  46.1 1.0 copy-done.4
  47.1 1.0 add_convert_fusion
  48.0 11.1 %all-to-all-start = ((bf16[16,1,136,128]{3,2,1,0:T(8,128)(2,1)}), bf16[16,1,136,128]{3,2,1,0:T(8,128)(2,1)S(1)}, u32[]{:S(2)}, u32[]{:S(2)}) async-start(bf16[16,1,136,128]{3,2,1,0:T(8,128)(2,1)} %bitcast.7), calls=%async_computation | async-start | bytes 1114112 | tf_op jit(solution)/shard_map/all_to_all | solution.py:378
  59.2 1.3 %collective-permute-start.5 = (bf16[8,4096]{1,0:T(8,128)(2,1)S(1)}, bf16[8,4096]{1,0:T(8,128)(2,1)S(1)}, u32[]{:S(2)}, u32[]{:S(2)}) collective-permute-start(bf16[8,4096]{1,0:T(8,128)(2,1)S(1)} %get-tuple-element.74), channel_id=1, source_target_pairs={{1,0},{2,1},{3,2},{4,3},{5,4},{6,5},{7,6},{8,7},{9,8},{10,9},{11,1... | collective-permute-start | bytes 196616 | tf_op jit(solution)/shard_map/ppermute | solution.py:53
  60.5 5.7 %shard_map.133 = (bf16[128,4096]{1,0:T(8,128)(2,1)}, bf16[128,4096]{1,0:T(8,128)(2,1)}) custom-call(s32[1]{0:T(128)S(6)} %sub.3.half_ref, s32[1,8]{1,0:T(1,128)} %lengths_ref.17, bf16[128,4096]{1,0:T(8,128)(2,1)} %bitcast.32, bf16[128,4096]{1,0:T(8,128)(2,1)} %bitcast.34, bf16[128,2048]{1,0:T(8,128)(2,1)} %get-tuple-element.75.mixed_ref, ...), custom_call_target="tpu_custom_call" | custom-call | bytes 10500000 | tf_op jit(solution)/shard_map/pallas_call | solution.py:300
  66.2 4.4 %all-to-all-done = bf16[16,1,136,128]{3,2,1,0:T(8,128)(2,1)S(1)} async-done(((bf16[16,1,136,128]{3,2,1,0:T(8,128)(2,1)}), bf16[16,1,136,128]{3,2,1,0:T(8,128)(2,1)S(1)}, u32[]{:S(2)}, u32[]{:S(2)}) %all-to-all-start) | async-done | bytes 557088 | tf_op jit(solution)/shard_map/all_to_all | solution.py:378
  70.7 0.7 broadcast_in_dim.33
  71.4 8.7 %all-to-all-start.1 = ((bf16[8,1,136,128]{3,2,1,0:T(8,128)(2,1)}), bf16[8,1,136,128]{3,2,1,0:T(8,128)(2,1)S(1)}, u32[]{:S(2)}, u32[]{:S(2)}) async-start(bf16[8,1,136,128]{3,2,1,0:T(8,128)(2,1)} %broadcast_in_dim.33), calls=%async_computation.1 | async-start | bytes 557056 | tf_op jit(solution)/shard_map/all_to_all | solution.py:378
  80.1 5.7 %shard_map.134 = (bf16[128,4096]{1,0:T(8,128)(2,1)}, bf16[128,4096]{1,0:T(8,128)(2,1)}) custom-call(s32[1]{0:T(128)} %bitcast.half_ref, s32[1,8]{1,0:T(1,128)} %lengths_ref.17, bf16[128,4096]{1,0:T(8,128)(2,1)} %bitcast.33, bf16[128,4096]{1,0:T(8,128)(2,1)} %bitcast.35, bf16[128,2048]{1,0:T(8,128)(2,1)} %copy-done.6, ...), custom_call_target="tpu_custom_call", output_to_operand_aliasing={{0}: (8, {}), {1}: (9, {})} | custom-call | bytes 10500000 | tf_op jit(solution)/shard_map/pallas_call | solution.py:300
  85.8 4.3 %all-to-all-done.1 = bf16[8,1,136,128]{3,2,1,0:T(8,128)(2,1)S(1)} async-done(((bf16[8,1,136,128]{3,2,1,0:T(8,128)(2,1)}), bf16[8,1,136,128]{3,2,1,0:T(8,128)(2,1)S(1)}, u32[]{:S(2)}, u32[]{:S(2)}) %all-to-all-start.1) | async-done | bytes 278560 | tf_op jit(solution)/shard_map/all_to_all | solution.py:378
  90.2 0.9 broadcast_in_dim.37
  91.1 4.0 %all-to-all-start.2 = ((bf16[16,1,136,128]{3,2,1,0:T(8,128)(2,1)}), bf16[16,1,136,128]{3,2,1,0:T(8,128)(2,1)S(1)}, u32[]{:S(2)}, u32[]{:S(2)}) async-start(bf16[16,1,136,128]{3,2,1,0:T(8,128)(2,1)} %broadcast_in_dim.37), calls=%async_computation.2 | async-start | bytes 1114112 | tf_op jit(solution)/shard_map/all_to_all | solution.py:378
  95.1 4.3 %shard_map.135 = bf16[128,4096]{1,0:T(8,128)(2,1)} custom-call(s32[1,8]{1,0:T(1,128)} %lengths_ref.17, bf16[128,4096]{1,0:T(8,128)(2,1)} %copy-done.4, bf16[8,4096]{1,0:T(8,128)(2,1)} %copy-done.14, f32[7,4096]{1,0:T(8,128)} %taps_ref.5), custom_call_target="tpu_custom_call" | custom-call | bytes 14000000 | tf_op jit(solution)/shard_map/pallas_call | solution.py:300
  99.4 4.9 %all-to-all-done.2 = bf16[16,1,136,128]{3,2,1,0:T(8,128)(2,1)S(1)} async-done(((bf16[16,1,136,128]{3,2,1,0:T(8,128)(2,1)}), bf16[16,1,136,128]{3,2,1,0:T(8,128)(2,1)S(1)}, u32[]{:S(2)}, u32[]{:S(2)}) %all-to-all-start.2) | async-done | bytes 557088 | tf_op jit(solution)/shard_map/all_to_all | solution.py:378
  104.3 4.4 %collective-permute-start.6 = (bf16[16,136,128]{2,1,0:T(8,128)(2,1)S(1)}, bf16[16,136,128]{2,1,0:T(8,128)(2,1)S(1)}, u32[]{:S(2)}, u32[]{:S(2)}) collective-permute-start(bf16[16,136,128]{2,1,0:T(8,128)(2,1)S(1)} %bitcast.30), channel_id=1, source_target_pairs={{0,32},{32,0},{1,33},{33,1},{2,34},{34,2},{3,35},{35,3},{4,36},{36... | collective-permute-start | bytes 1671176 | tf_op jit(solution)/shard_map/ppermute | solution.py:390
  108.7 1.6 %collective-permute-done.6.other_ref = bf16[16,136,128]{2,1,0:T(8,128)(2,1)S(1)} collective-permute-done((bf16[16,136,128]{2,1,0:T(8,128)(2,1)S(1)}, bf16[16,136,128]{2,1,0:T(8,128)(2,1)S(1)}, u32[]{:S(2)}, u32[]{:S(2)}) %collective-permute-start.6) | collective-permute-done | bytes 557088 | tf_op jit(solution)/shard_map/ppermute | solution.py:390
  110.3 1.5 %shard_map.136 = (f32[7,4096]{1,0:T(8,128)}, f32[128,4096]{1,0:T(8,128)}) custom-call(bf16[16,136,128]{2,1,0:T(8,128)(2,1)S(1)} %bitcast.31, bf16[16,136,128]{2,1,0:T(8,128)(2,1)S(1)} %collective-permute-done.6.other_ref), custom_call_target="tpu_custom_call" | custom-call | bytes 10500000 | tf_op jit(solution)/shard_map/pallas_call | solution.py:300
  (36 shorter events, 0.2 us)
Async XLA Ops:
  1.5 15.5 %copy-start = (f32[128,4096]{1,0:T(8,128)S(1)}, f32[128,4096]{1,0:T(8,128)}, u32[]{:S(2)}) copy-start(f32[128,4096]{1,0:T(8,128)} %ltaps_ref.11) | copy-start | bytes 6291460
  1.5 15.5 %copy-start.13 = (s32[1,8]{1,0:T(1,128)S(1)}, s32[1,8]{1,0:T(1,128)}, u32[]{:S(2)}) copy-start(s32[1,8]{1,0:T(1,128)} %lengths_ref.17) | copy-start | bytes 100
  1.5 5.9 %collective-permute-start = (bf16[8,4096]{1,0:T(8,128)(2,1)S(1)}, bf16[8,4096]{1,0:T(8,128)(2,1)S(1)}, u32[]{:S(2)}, u32[]{:S(2)}) collective-permute-start(bf16[8,4096]{1,0:T(8,128)(2,1)S(1)} %slice_bitcast_fusion), channel_id=1, source_target_pairs={{0,1},{1,2},{2,3},{3,4},{4,5},{5,6},{6,7},{7,8},{8,9},{9,10},{10,1... | collective-permute-start | bytes 196616 | tf_op jit(solution)/shard_map/ppermute | solution.py:53
  7.4 1.3 %copy-start.10 = (bf16[8,4096]{1,0:T(8,128)(2,1)}, bf16[8,4096]{1,0:T(8,128)(2,1)S(1)}, u32[]{:S(2)}) copy-start(bf16[8,4096]{1,0:T(8,128)(2,1)S(1)} %collective-permute-done.before_ref) | copy-start | bytes 196612
  7.4 26.0 %collective-permute-start.2 = (bf16[128,4096]{1,0:T(8,128)(2,1)S(1)}, bf16[128,4096]{1,0:T(8,128)(2,1)}, u32[]{:S(2)}, u32[]{:S(2)}) collective-permute-start(bf16[128,4096]{1,0:T(8,128)(2,1)S(1)} %multiply_convert_fusion.adj_ref), channel_id=1, source_target_pairs={{1,0},{2,1},{3,2},{4,3},{5,4},{6,5},{7,6},{8,7},{9,8},{10,9},{11,1... | collective-permute-start | bytes 3145736 | tf_op jit(solution)/shard_map/ppermute | solution.py:53
  8.7 8.3 %copy-start.1 = (bf16[1280,256]{1,0:T(8,128)(2,1)S(1)}, bf16[1280,256]{1,0:T(8,128)(2,1)}, u32[]{:S(2)}) copy-start(bf16[1280,256]{1,0:T(8,128)(2,1)} %constant.16.clone.table_ref) | copy-start | bytes 1966084
  12.8 9.7 %copy-start.2 = (bf16[1,128,4096]{2,1,0:T(8,128)(2,1)S(1)}, bf16[1,128,4096]{2,1,0:T(8,128)(2,1)}, u32[]{:S(2)}) copy-start(bf16[1,128,4096]{2,1,0:T(8,128)(2,1)} %param.9) | copy-start | bytes 3145732
  12.8 9.7 %copy-start.3 = (bf16[1,128,4096]{2,1,0:T(8,128)(2,1)S(1)}, bf16[1,128,4096]{2,1,0:T(8,128)(2,1)}, u32[]{:S(2)}) copy-start(bf16[1,128,4096]{2,1,0:T(8,128)(2,1)} %param.10) | copy-start | bytes 3145732
  12.8 9.7 %copy-start.5 = (f32[7,4096]{1,0:T(8,128)S(1)}, f32[7,4096]{1,0:T(8,128)}, u32[]{:S(2)}) copy-start(f32[7,4096]{1,0:T(8,128)} %taps_ref.5) | copy-start | bytes 344068
  12.8 20.5 %collective-permute-start.1 = (bf16[128,2048]{1,0:T(8,128)(2,1)}, bf16[128,2048]{1,0:T(8,128)(2,1)S(1)}, u32[]{:S(2)}, u32[]{:S(2)}) collective-permute-start(bf16[128,2048]{1,0:T(8,128)(2,1)} %get-tuple-element.75.mixed_ref), channel_id=1, source_target_pairs={{0,1},{1,2},{2,3},{3,4},{4,5},{5,6},{6,7},{7,8},{8,9},{9,10},{10,1... | collective-permute-start | bytes 1572872 | tf_op jit(solution)/shard_map/ppermute | solution.py:53
  17.0 1.0 copy-start.8
  18.0 4.5 %copy-start.11 = (bf16[8,4096]{1,0:T(8,128)(2,1)S(1)}, bf16[8,4096]{1,0:T(8,128)(2,1)}, u32[]{:S(2)}) copy-start(bf16[8,4096]{1,0:T(8,128)(2,1)} %copy-done.10) | copy-start | bytes 196612
  25.4 8.0 %copy-start.6 = (bf16[128,2048]{1,0:T(8,128)(2,1)}, bf16[128,2048]{1,0:T(8,128)(2,1)S(1)}, u32[]{:S(2)}) copy-start(bf16[128,2048]{1,0:T(8,128)(2,1)S(1)} %get-tuple-element.80.mixed_ref) | copy-start | bytes 1572868
  25.4 8.0 %copy-start.12 = (f32[128,2048]{1,0:T(8,128)S(1)}, f32[128,2048]{1,0:T(8,128)}, u32[]{:S(2)}) copy-start(f32[128,2048]{1,0:T(8,128)} %get-tuple-element.61.short_ref) | copy-start | bytes 3145732
  25.4 13.8 %collective-permute-start.3 = (bf16[128,2048]{1,0:T(8,128)(2,1)S(1)}, bf16[128,2048]{1,0:T(8,128)(2,1)S(1)}, u32[]{:S(2)}, u32[]{:S(2)}) collective-permute-start(bf16[128,2048]{1,0:T(8,128)(2,1)S(1)} %get-tuple-element.80.mixed_ref), channel_id=1, source_target_pairs={{0,1},{1,2},{2,3},{3,4},{4,5},{5,6},{6,7},{7,8},{8,9},{9,10},{10,1... | collective-permute-start | bytes 1572872 | tf_op jit(solution)/shard_map/ppermute | solution.py:53
  33.4 5.4 %copy-start.9 = (bf16[128,2048]{1,0:T(8,128)(2,1)}, bf16[128,2048]{1,0:T(8,128)(2,1)S(1)}, u32[]{:S(2)}) copy-start(bf16[128,2048]{1,0:T(8,128)(2,1)S(1)} %collective-permute-done.1.prev_ref) | copy-start | bytes 1572868
  39.2 6.9 %copy-start.7 = (bf16[128,2048]{1,0:T(8,128)(2,1)}, bf16[128,2048]{1,0:T(8,128)(2,1)S(1)}, u32[]{:S(2)}) copy-start(bf16[128,2048]{1,0:T(8,128)(2,1)S(1)} %collective-permute-done.3.prev_ref) | copy-start | bytes 1572868
  39.2 7.9 %collective-permute-start.4 = (bf16[16,136,128]{2,1,0:T(8,128)(2,1)S(1)}, bf16[16,136,128]{2,1,0:T(8,128)(2,1)S(1)}, u32[]{:S(2)}, u32[]{:S(2)}) collective-permute-start(bf16[16,136,128]{2,1,0:T(8,128)(2,1)S(1)} %get-tuple-element.71), channel_id=1, source_target_pairs={{0,32},{32,0},{1,33},{33,1},{2,34},{34,2},{3,35},{35,3},{4,36},{36... | collective-permute-start | bytes 1671176 | tf_op jit(solution)/shard_map/ppermute | solution.py:390
  46.1 1.0 copy-start.4
  48.0 22.5 %all-to-all-start = ((bf16[16,1,136,128]{3,2,1,0:T(8,128)(2,1)}), bf16[16,1,136,128]{3,2,1,0:T(8,128)(2,1)S(1)}, u32[]{:S(2)}, u32[]{:S(2)}) async-start(bf16[16,1,136,128]{3,2,1,0:T(8,128)(2,1)} %bitcast.7), calls=%async_computation | async-start | bytes 1114112 | tf_op jit(solution)/shard_map/all_to_all | solution.py:378
  59.2 11.5 %collective-permute-start.5 = (bf16[8,4096]{1,0:T(8,128)(2,1)S(1)}, bf16[8,4096]{1,0:T(8,128)(2,1)S(1)}, u32[]{:S(2)}, u32[]{:S(2)}) collective-permute-start(bf16[8,4096]{1,0:T(8,128)(2,1)S(1)} %get-tuple-element.74), channel_id=1, source_target_pairs={{1,0},{2,1},{3,2},{4,3},{5,4},{6,5},{7,6},{8,7},{9,8},{10,9},{11,1... | collective-permute-start | bytes 196616 | tf_op jit(solution)/shard_map/ppermute | solution.py:53
  70.7 15.1 %copy-start.14 = (bf16[8,4096]{1,0:T(8,128)(2,1)}, bf16[8,4096]{1,0:T(8,128)(2,1)S(1)}, u32[]{:S(2)}) copy-start(bf16[8,4096]{1,0:T(8,128)(2,1)S(1)} %collective-permute-done.5.after_ref) | copy-start | bytes 196612
  71.4 18.7 %all-to-all-start.1 = ((bf16[8,1,136,128]{3,2,1,0:T(8,128)(2,1)}), bf16[8,1,136,128]{3,2,1,0:T(8,128)(2,1)S(1)}, u32[]{:S(2)}, u32[]{:S(2)}) async-start(bf16[8,1,136,128]{3,2,1,0:T(8,128)(2,1)} %broadcast_in_dim.33), calls=%async_computation.1 | async-start | bytes 557056 | tf_op jit(solution)/shard_map/all_to_all | solution.py:378
  91.1 13.2 %all-to-all-start.2 = ((bf16[16,1,136,128]{3,2,1,0:T(8,128)(2,1)}), bf16[16,1,136,128]{3,2,1,0:T(8,128)(2,1)S(1)}, u32[]{:S(2)}, u32[]{:S(2)}) async-start(bf16[16,1,136,128]{3,2,1,0:T(8,128)(2,1)} %broadcast_in_dim.37), calls=%async_computation.2 | async-start | bytes 1114112 | tf_op jit(solution)/shard_map/all_to_all | solution.py:378
  104.3 6.0 %collective-permute-start.6 = (bf16[16,136,128]{2,1,0:T(8,128)(2,1)S(1)}, bf16[16,136,128]{2,1,0:T(8,128)(2,1)S(1)}, u32[]{:S(2)}, u32[]{:S(2)}) collective-permute-start(bf16[16,136,128]{2,1,0:T(8,128)(2,1)S(1)} %bitcast.30), channel_id=1, source_target_pairs={{0,32},{32,0},{1,33},{33,1},{2,34},{34,2},{3,35},{35,3},{4,36},{36... | collective-permute-start | bytes 1671176 | tf_op jit(solution)/shard_map/ppermute | solution.py:390
